TPU v7x, 32 devices: a whole 2x2x4 slice. The times are simulated.
32 devices in a mesh: group: 4 (over y, x), shard: 8 (over z, core).
Axes of the slice: x: 2, y: 2, z: 4, core: 2. Of those that a mesh axis runs over, the one named last changes fastest.
Arguments:
- tokens: bfloat16 [2048, 2048], P(('group', 'shard')), may hold values from -7 to 7
- w_qk: bfloat16 [2048, 1024], P('shard'), may hold values from -0.09375 to 0.09375
- w_in: bfloat16 [128, 2048], replicated, may hold values from -0.5 to 0.5
- w_out: bfloat16 [2048, 128], replicated, may hold values from -0.125 to 0.125
- particles: bfloat16 [131072, 128], P(('group', 'shard')), may hold values from -6 to 6
- cotangent: bfloat16 [131072, 128], P(('group', 'shard')), may hold values from -6 to 6
- clusters: int32 [131072], P(('group', 'shard')), may hold values from 0 to 63
- owners: int32 [1024], P(('group', 'shard')), may hold values from 0 to 7, as said below
Outputs:
- particle_out: bfloat16 [131072, 128], P(('group', 'shard'))
- qk_grad: float32 [2048, 1024], P('shard')
Inputs may be any that keep to these rules, and one draw needn't show every extreme that they name: `owners`: each device's blocks name one owner at most 8 times; in every group some owner is named exactly 8 times by the blocks of every device of the group.
All inputs are finite; a program needn't handle non-finite values.
Results may differ from a plain program's by a relative error of at most 0.028.
Values may be sent and summed in bfloat16 or wider, within the bound.
No kernel may reach another device: no remote copies, remote signals or barrier semaphores. Data moves between devices by JAX's collectives and lax.ppermute only.
A program may use at most 64 MiB of HBM per device.

v0:
```python
import math

import jax
import jax.numpy as jnp
from jax import lax
from jax.sharding import PartitionSpec as P

HEADS = 8


def token_pass(tokens, pooled, w_qk, w_in, w_out, pooled_grad):
    hidden_sum = tokens.astype(jnp.float32) + jnp.dot(
        pooled, w_in, preferred_element_type=jnp.float32
    )
    hidden = hidden_sum.astype(jnp.bfloat16)
    queries = jnp.dot(hidden, w_qk, preferred_element_type=jnp.float32).astype(jnp.bfloat16)
    num_rows = hidden.shape[0]
    head_cols = queries.shape[1]
    q_heads = queries.reshape(num_rows, HEADS, -1).astype(jnp.float32)
    score_scale = 1.0 / math.sqrt(q_heads.shape[2])
    scores = jnp.einsum("ihd,jhd->hij", q_heads, q_heads) * score_scale
    self_mask = jnp.eye(num_rows, dtype=bool)
    scores = jnp.where(self_mask[None], -1000000000.0, scores)
    row_max = jnp.max(scores, axis=2, keepdims=True)
    weights_exp = jnp.exp(scores - row_max)
    attn_prob = weights_exp / jnp.sum(weights_exp, axis=2, keepdims=True)
    prob_low = lax.optimization_barrier(attn_prob.astype(jnp.bfloat16)).astype(jnp.float32)
    hidden_wide = hidden.astype(jnp.float32)
    values = hidden_wide[:, :head_cols].reshape(num_rows, HEADS, -1)
    attended = jnp.einsum("hij,jhv->ihv", prob_low, values).reshape(num_rows, head_cols)
    output = jnp.concatenate(
        [hidden_wide[:, :head_cols] + attended, hidden_wide[:, head_cols:]], axis=1
    ).astype(jnp.bfloat16)
    unpooled = jnp.dot(output, w_out, preferred_element_type=jnp.float32).astype(jnp.bfloat16)
    out_grad = jnp.dot(pooled_grad, w_out.T, preferred_element_type=jnp.float32).astype(
        jnp.bfloat16
    )
    grad_heads = out_grad[:, :head_cols].reshape(num_rows, HEADS, -1).astype(jnp.float32)
    prob_grad = jnp.einsum("ihv,jhv->hij", grad_heads, values)
    score_grad = (
        attn_prob
        * (prob_grad - jnp.sum(prob_grad * attn_prob, axis=2, keepdims=True))
        * score_scale
    )
    score_low = lax.optimization_barrier(score_grad.astype(jnp.bfloat16)).astype(jnp.float32)
    q_grad = jnp.einsum("hij,jhd->ihd", score_low, q_heads) + jnp.einsum(
        "hji,jhd->ihd", score_low, q_heads
    )
    q_grad = q_grad.reshape(num_rows, -1).astype(jnp.bfloat16)
    return (unpooled, hidden, q_grad)


def local(tokens, w_qk, w_in, w_out, particles, cotangent, clusters, owners):
    n_shard = lax.axis_size("shard")
    num_blocks = owners.shape[0]
    block_rows = particles.shape[0] // num_blocks
    channels = particles.shape[1]
    capacity = 2 * num_blocks // n_shard
    slot_count = n_shard * capacity
    t_rows = tokens.shape[0]
    owner_hot = (owners[:, None] == jnp.arange(n_shard, dtype=jnp.int32)[None, :]).astype(jnp.int32)
    earlier = jnp.cumsum(owner_hot, axis=0) - owner_hot
    slot_rank = jnp.sum(earlier * owner_hot, axis=1)
    target = owners * capacity + slot_rank
    placing = (target[None, :] == jnp.arange(slot_count, dtype=jnp.int32)[:, None]).astype(
        jnp.bfloat16
    )
    feat_rows = particles.reshape(num_blocks, block_rows * channels)
    grad_rows = cotangent.reshape(num_blocks, block_rows * channels)
    send_feat = jnp.dot(placing, feat_rows, preferred_element_type=jnp.float32).astype(jnp.bfloat16)
    send_grad = jnp.dot(placing, grad_rows, preferred_element_type=jnp.float32).astype(jnp.bfloat16)
    label_rows = (clusters.reshape(num_blocks, block_rows) + 1).astype(jnp.float32)
    send_label = (
        jnp.dot(placing.astype(jnp.float32), label_rows, precision=lax.Precision.HIGHEST) - 1.0
    )
    send_feat = send_feat.reshape(n_shard, capacity, block_rows, channels)
    send_grad = send_grad.reshape(n_shard, capacity, block_rows, channels)
    send_label = send_label.astype(jnp.bfloat16).reshape(n_shard, capacity, block_rows)
    got_feat, got_grad, got_label = (
        lax.all_to_all(send_feat, "shard", split_axis=0, concat_axis=0, tiled=True),
        lax.all_to_all(send_grad, "shard", split_axis=0, concat_axis=0, tiled=True),
        lax.all_to_all(send_label, "shard", split_axis=0, concat_axis=0, tiled=True),
    )
    received = slot_count * block_rows
    labels = got_label.reshape(received).astype(jnp.float32)
    member = (labels[None, :] == jnp.arange(t_rows, dtype=jnp.float32)[:, None]).astype(
        jnp.bfloat16
    )
    counts = jnp.sum(member, axis=1, dtype=jnp.float32)
    pooled_sum = jnp.dot(
        member, got_feat.reshape(received, channels), preferred_element_type=jnp.float32
    )
    pooled = (pooled_sum / jnp.maximum(counts, 1.0)[:, None]).astype(jnp.bfloat16)
    pooled_grad = jnp.dot(
        member, got_grad.reshape(received, channels), preferred_element_type=jnp.float32
    ).astype(jnp.bfloat16)
    full_qk = lax.all_gather(w_qk, "shard", axis=0, tiled=True)
    unpooled, hidden, q_grad = token_pass(tokens, pooled, full_qk, w_in, w_out, pooled_grad)
    all_tokens = lax.all_gather(unpooled, "shard", axis=0, tiled=True)
    lookup = jnp.repeat(owners, block_rows) * t_rows + clusters
    returned_rows = jnp.take(all_tokens, lookup, axis=0).astype(jnp.float32)
    particle_out = (particles.astype(jnp.float32) + returned_rows).astype(jnp.bfloat16)
    shard_sum = lax.psum_scatter(
        jnp.einsum("td,tk->dk", hidden, q_grad, preferred_element_type=jnp.float32).astype(
            jnp.bfloat16
        ),
        "shard",
        scatter_dimension=0,
        tiled=True,
    )
    qk_grad = lax.psum(shard_sum, "group").astype(jnp.float32)
    return (particle_out, qk_grad)


def solution(mesh):
    placed = (
        P(("group", "shard"), None),
        P("shard", None),
        P(),
        P(),
        P(("group", "shard"), None),
        P(("group", "shard"), None),
        P(("group", "shard")),
        P(("group", "shard")),
    )
    return jax.shard_map(
        local,
        mesh=mesh,
        in_specs=placed,
        out_specs=(P(("group", "shard"), None), P("shard", None)),
        check_vma=False,
    )
```

profile of v0, /device:TPU:0, one launch (start us, length us, event | category | flops | bytes accessed | tf_op | source)
XLA Modules:
  0.0 276.6 jit_solution(7949322319219188592)
XLA Ops:
  7.2 0.0 copy-start
  7.2 0.8 fusion.57
  8.0 0.1 reduce_window_sum.11
  8.0 0.8 select_reduce_fusion
  8.9 0.7 broadcast_multiply_fusion
  9.5 1.5 fusion.22
  11.0 6.3 %all-to-all-start = ((bf16[8,8,128]{2,1,0:T(8,128)(2,1)}), bf16[8,8,128]{2,1,0:T(8,128)(2,1)S(1)}, u32[]{:S(2)}, u32[]{:S(2)}) async-start(bf16[8,8,128]{2,1,0:T(8,128)(2,1)} %fusion.22), calls=%async_computation | async-start | bytes 32768 | tf_op jit(solution)/shard_map/all_to_all | solution.py:82
  17.3 1.5 reshape.75
  18.8 0.7 fusion.6
  19.5 1.9 copy.33
  21.4 1.5 all-to-all-done
  23.0 3.6 %all-to-all-start.1 = ((bf16[8,8,128,128]{3,2,1,0:T(8,128)(2,1)}), bf16[8,8,128,128]{3,2,1,0:T(8,128)(2,1)S(1)}, u32[]{:S(2)}, u32[]{:S(2)}) async-start(bf16[8,8,128,128]{3,2,1,0:T(8,128)(2,1)} %copy.33), calls=%async_computation.1 | async-start | bytes 4194304 | tf_op jit(solution)/shard_map/all_to_all | solution.py:80
  26.6 0.0 all-gather.2.cloned.1.call-start
  26.6 0.7 all-gather.2.cloned.1.call-update
  27.3 2.3 reshape.81
  29.6 1.9 fusion.7
  31.5 1.9 copy.39
  33.5 75.4 %all-to-all-done.1 = bf16[8,8,128,128]{3,2,1,0:T(8,128)(2,1)S(1)} async-done(((bf16[8,8,128,128]{3,2,1,0:T(8,128)(2,1)}), bf16[8,8,128,128]{3,2,1,0:T(8,128)(2,1)S(1)}, u32[]{:S(2)}, u32[]{:S(2)}) %all-to-all-start.1) | async-done | bytes 2097184 | tf_op jit(solution)/shard_map/all_to_all | solution.py:80
  108.9 4.3 %all-to-all-start.2 = ((bf16[8,8,128,128]{3,2,1,0:T(8,128)(2,1)}), bf16[8,8,128,128]{3,2,1,0:T(8,128)(2,1)}, u32[]{:S(2)}, u32[]{:S(2)}) async-start(bf16[8,8,128,128]{3,2,1,0:T(8,128)(2,1)} %copy.39), calls=%async_computation.2 | async-start | bytes 4194304 | tf_op jit(solution)/shard_map/all_to_all | solution.py:81
  113.2 0.0 reduce-scatter.2.cloned.1.call-start
  113.3 0.3 convert_reduce_fusion
  113.6 0.0 copy-done.2
  113.6 1.6 fusion.2
  115.3 47.0 %all-to-all-done.2 = bf16[8,8,128,128]{3,2,1,0:T(8,128)(2,1)} async-done(((bf16[8,8,128,128]{3,2,1,0:T(8,128)(2,1)}), bf16[8,8,128,128]{3,2,1,0:T(8,128)(2,1)}, u32[]{:S(2)}, u32[]{:S(2)}) %all-to-all-start.2) | async-done | bytes 2097184 | tf_op jit(solution)/shard_map/all_to_all | solution.py:81
  162.3 0.0 copy-done
  162.3 2.3 fusion.23
  164.6 0.2 fusion.36
  164.8 0.0 all-gather.2.cloned.1.call-done
  164.8 3.0 %fusion.16 = bf16[8,8,8,128]{3,2,1,0:T(8,128)(2,1)S(1)} fusion(bf16[64,2048]{1,0:T(8,128)(2,1)S(1)} %fusion.2, bf16[2048,1024]{1,0:T(8,128)(2,1)} %all-gather.2.cloned.1.call-done), kind=kOutput, calls=%fused_computation.28 | convolution fusion | flops 268500992 | bytes 4587520 | tf_op jit(solution)/shard_map/dot_general | solution.py:16
  167.9 0.3 fusion.70
  168.1 0.1 fusion.15
  168.2 0.2 fusion.40
  168.4 0.2 fusion.17
  168.6 3.2 %convolution_convert_fusion.2 = bf16[2048,1024]{1,0:T(8,128)(2,1)} fusion(bf16[64,2048]{1,0:T(8,128)(2,1)S(1)} %fusion.2, bf16[8,8,8,128]{3,2,1,0:T(8,128)(2,1)S(1)} %fusion.17), kind=kOutput, calls=%fused_computation.5 | convolution fusion | flops 270532608 | bytes 4587520 | tf_op jit(solution)/shard_map/td,tk->dk/dot_general | solution.py:104
  171.8 0.0 reduce-scatter.2.cloned.1.call-update
  171.9 0.0 all-reduce.2.cloned.1.call-start
  171.9 0.6 copy-done.3
  172.5 0.1 compare_and_fusion
  172.6 0.1 fusion.60
  172.7 0.2 convolution_bitcast_fusion
  173.0 0.2 convolution_convert_fusion.4
  173.2 14.3 %all_gather.7 = bf16[512,128]{1,0:T(8,128)(2,1)S(1)} all-gather(bf16[64,128]{1,0:T(8,128)(2,1)S(1)} %convolution_convert_fusion.4), channel_id=1, replica_groups=mesh['group'=4,'shard'=8] {'shard'}, dimensions={0}, use_global_device_ids=true | all-gather | bytes 147456 | tf_op jit(solution)/shard_map/all_gather | solution.py:99
  187.6 12.1 %gather_fusion = bf16[4096,128]{1,0:T(8,128)(2,1)S(1)} fusion(bf16[512,128]{1,0:T(8,128)(2,1)S(1)} %all_gather.7, s32[4096]{0:T(1024)S(1)} %fusion.60), kind=kCustom, calls=%fused_computation | custom fusion | bytes 2113536 | tf_op jit(solution)/shard_map/jit(_take)/gather | solution.py:101
  199.7 21.8 %reduce-scatter.2.cloned.1.call-done = bf16[256,1024]{1,0:T(8,128)(2,1)} async-done(((bf16[2048,1024]{1,0:T(8,128)(2,1)}), bf16[256,1024]{1,0:T(8,128)(2,1)}) %reduce-scatter.2.cloned.1.call-update) | async-done | bytes 524304 | tf_op jit(solution)/shard_map/reduce_scatter | solution.py:103
  221.5 0.0 all-reduce.2.cloned.1.call-update
  221.5 2.9 %add_convert_fusion = bf16[4096,128]{1,0:T(8,128)(2,1)} fusion(bf16[4096,128]{1,0:T(8,128)(2,1)S(1)} %copy-done.1, bf16[4096,128]{1,0:T(8,128)(2,1)S(1)} %gather_fusion, pred[4096]{0:T(1024)(128)(4,1)S(1)} %compare_and_fusion), kind=kLoop, calls=%fused_computation.8 | loop fusion | flops 2621440 | bytes 3149824 | tf_op jit(solution)/shard_map/convert_element_type | solution.py:102
  224.4 43.6 %all-reduce.2.cloned.1.call-done = bf16[256,1024]{1,0:T(8,128)(2,1)} async-done(((bf16[256,1024]{1,0:T(8,128)(2,1)}), bf16[256,1024]{1,0:T(8,128)(2,1)}) %all-reduce.2.cloned.1.call-update) | async-done | bytes 524304 | tf_op jit(solution)/shard_map/psum | solution.py:111
  268.0 2.1 convert_element_type.119
  (10 shorter events, 0.1 us)
Async XLA Ops:
  7.2 155.1 %copy-start = (bf16[2048,128]{1,0:T(8,128)(2,1)S(1)}, bf16[2048,128]{1,0:T(8,128)(2,1)}, u32[]{:S(2)}) copy-start(bf16[2048,128]{1,0:T(8,128)(2,1)} %param.11) | copy-start | bytes 1572868
  11.0 12.0 %all-to-all-start = ((bf16[8,8,128]{2,1,0:T(8,128)(2,1)}), bf16[8,8,128]{2,1,0:T(8,128)(2,1)S(1)}, u32[]{:S(2)}, u32[]{:S(2)}) async-start(bf16[8,8,128]{2,1,0:T(8,128)(2,1)} %fusion.22), calls=%async_computation | async-start | bytes 32768 | tf_op jit(solution)/shard_map/all_to_all | solution.py:82
  23.0 85.9 %all-to-all-start.1 = ((bf16[8,8,128,128]{3,2,1,0:T(8,128)(2,1)}), bf16[8,8,128,128]{3,2,1,0:T(8,128)(2,1)S(1)}, u32[]{:S(2)}, u32[]{:S(2)}) async-start(bf16[8,8,128,128]{3,2,1,0:T(8,128)(2,1)} %copy.33), calls=%async_computation.1 | async-start | bytes 4194304 | tf_op jit(solution)/shard_map/all_to_all | solution.py:80
  26.6 138.2 %all-gather.2.cloned.1.call-start = ((), (), s32[]{:S(2)}) async-start(), calls=%async_computation.4 | async-start | bytes 4718592 | tf_op jit(solution)/shard_map/all_gather | solution.py:97
  33.5 80.2 %copy-start.2 = (bf16[128,2048]{1,0:T(8,128)(2,1)S(1)}, bf16[128,2048]{1,0:T(8,128)(2,1)}, u32[]{:S(2)}) copy-start(bf16[128,2048]{1,0:T(8,128)(2,1)} %param.10) | copy-start | bytes 1572868
  108.9 53.4 %all-to-all-start.2 = ((bf16[8,8,128,128]{3,2,1,0:T(8,128)(2,1)}), bf16[8,8,128,128]{3,2,1,0:T(8,128)(2,1)}, u32[]{:S(2)}, u32[]{:S(2)}) async-start(bf16[8,8,128,128]{3,2,1,0:T(8,128)(2,1)} %copy.39), calls=%async_computation.2 | async-start | bytes 4194304 | tf_op jit(solution)/shard_map/all_to_all | solution.py:81
  113.2 108.3 %reduce-scatter.2.cloned.1.call-start = ((), (), s32[]{:S(2)}) async-start(), calls=%async_computation.5 | async-start | bytes 4718592 | tf_op jit(solution)/shard_map/reduce_scatter | solution.py:103
  171.8 0.7 copy-start.3
  171.9 96.1 %all-reduce.2.cloned.1.call-start = ((), (), s32[]{:S(2)}) async-start(), calls=%async_computation.6 | async-start | bytes 1048576 | tf_op jit(solution)/shard_map/psum | solution.py:111
  187.6 33.9 %copy-start.1 = (bf16[4096,128]{1,0:T(8,128)(2,1)S(1)}, bf16[4096,128]{1,0:T(8,128)(2,1)}, u32[]{:S(2)}) copy-start(bf16[4096,128]{1,0:T(8,128)(2,1)} %param.12) | copy-start | bytes 3145732
Sparse Core Ops, SparseCore 0:
  29.0 81.8 all-gather.1
  172.0 49.4 reduce-scatter.1
  224.5 43.4 all-reduce.1
where the time goes:
time: 277 us
  waiting for transfers between devices  190 us (69%)
  local copies, waits for them, and re-layouts  20.5 us (7%)
  matrix products  15.5 us (6%)
  starting transfers between devices  14.4 us (5%)
  blocking collectives  14.3 us (5%)
  between operations  13.9 us (5%)
  other arithmetic  8 us (3%)
    all_to_all x1, waiting for transfers between devices, local(): lax.all_to_all(send_feat, 'shard', split_axis=0, concat_axis=0, tiled=True)  75.4 us
    all_to_all x1, waiting for transfers between devices, local(): lax.all_to_all(send_grad, 'shard', split_axis=0, concat_axis=0, tiled=True)  47 us
    psum x1, waiting for transfers between devices, local(): qk_grad = lax.psum(shard_sum, 'group').astype(jnp.float32)  43.6 us
    reduce_scatter x1, waiting for transfers between devices, local(): lax.psum_scatter(jnp.einsum('td,tk->dk', hidden, q_grad, preferred_elemen...  21.8 us
    all_gather x1, blocking collectives, local(): all_tokens = lax.all_gather(unpooled, 'shard', axis=0, tiled=True)  14.3 us
    gather x1, local copies, waits for them, and re-layouts, local(): returned_rows = jnp.take(all_tokens, lookup, axis=0).astype(jnp.float32)  12.1 us
    all_to_all x1, starting transfers between devices, local(): lax.all_to_all(send_label, 'shard', split_axis=0, concat_axis=0, tiled=True)  6.33 us
  transfers between devices with their start and end apart: 6, of which 5 were waited for; matrix products, arithmetic and copies ran while one was open for 11% of the time, Pallas kernels for 0%

commit v1 on v0

v1 whole, which is shorter than its diff:
```python
import functools
import math

import jax
import jax.numpy as jnp
from jax import lax
from jax.experimental import pallas as pl
from jax.experimental.pallas import tpu as pltpu
from jax.sharding import PartitionSpec as P

HEADS = 8
F32 = jnp.float32
BF16 = jnp.bfloat16
VMEM = pl.BlockSpec(memory_space=pltpu.VMEM)


def params(mib):
    return pltpu.CompilerParams(vmem_limit_bytes=mib << 20)


def contract(a, b, da, db):
    return lax.dot_general(a, b, (((da,), (db,)), ((), ())), preferred_element_type=F32)


def pool_kernel(t_rows, owners_ref, clusters_ref, feat_ref, grad_ref, keep_ref, give_ref, acc_ref):
    step = pl.program_id(0)
    blocks, rows = clusters_ref.shape
    width = feat_ref.shape[1]

    @pl.when(step == 0)
    def _():
        acc_ref[...] = jnp.zeros_like(acc_ref)

    token = lax.broadcasted_iota(jnp.int32, (t_rows, rows), 0)
    for b in range(blocks):
        member = (clusters_ref[b : b + 1, :] == token).astype(F32)
        span = pl.ds(b * rows, rows)
        both = jnp.concatenate([feat_ref[span, :], grad_ref[span, :]], axis=1)
        sums = jnp.dot(member.astype(BF16), both, preferred_element_type=F32)
        place = pl.ds(pl.multiple_of(owners_ref[step * blocks + b] * t_rows, t_rows), t_rows)
        acc_ref[place, : 2 * width] += sums
        acc_ref[place, 2 * width :] += member

    @pl.when(step == pl.num_programs(0) - 1)
    def _():
        me = lax.axis_index("shard")
        for k in range(keep_ref.shape[0]):
            mine = me ^ (2 * k)
            keep_ref[k] = acc_ref[pl.ds(pl.multiple_of(mine * t_rows, t_rows), t_rows), :]
            other = mine ^ 1
            give_ref[k] = acc_ref[
                pl.ds(pl.multiple_of(other * t_rows, t_rows), t_rows), :
            ].astype(BF16)


def pool(particles, cotangent, clusters, owners, t_rows, n_shard):
    num_blocks = owners.shape[0]
    count, width = particles.shape
    rows = count // num_blocks
    steps = 4
    shape = (n_shard // 2, t_rows, 2 * width + rows)
    whole = pl.BlockSpec(shape, lambda i, own: (0, 0, 0))
    return pl.pallas_call(
        functools.partial(pool_kernel, t_rows),
        grid_spec=pltpu.PrefetchScalarGridSpec(
            num_scalar_prefetch=1,
            grid=(steps,),
            in_specs=[
                pl.BlockSpec((num_blocks // steps, rows), lambda i, own: (i, 0)),
                pl.BlockSpec((count // steps, width), lambda i, own: (i, 0)),
                pl.BlockSpec((count // steps, width), lambda i, own: (i, 0)),
            ],
            out_specs=[whole, whole],
            scratch_shapes=[pltpu.VMEM((n_shard * t_rows, shape[2]), F32)],
        ),
        out_shape=[jax.ShapeDtypeStruct(shape, F32), jax.ShapeDtypeStruct(shape, BF16)],
        compiler_params=params(24),
        name="pool",
    )(owners, clusters.reshape(num_blocks, rows), particles, cotangent)


def attend_kernel(parts, *refs):
    tok = refs[:parts]
    pooled_refs = refs[parts : 2 * parts]
    near, far, w_in, w_out, up_ref, keep_ref, give_ref, weight, hid, term = refs[2 * parts :]
    pairs, rows, cols = near.shape
    t_rows, width = tok[0].shape
    head_cols = cols * parts
    channels = w_in.shape[0]
    group, me = lax.axis_index("group"), lax.axis_index("shard")
    part = lax.rem(group, parts)
    core = lax.rem(me, 2)
    pair = lax.div(me, 2)
    for k in range(pairs):
        base = (pair ^ k) * (2 * rows)
        weight[pl.ds(pl.multiple_of(base + core * rows, rows), rows), :] = near[k]
        weight[pl.ds(pl.multiple_of(base + (1 - core) * rows, rows), rows), :] = far[k]
    pooled = jnp.concatenate([r[:, :channels] for r in pooled_refs], axis=0)
    pooled_grad = jnp.concatenate([r[:, channels:] for r in pooled_refs], axis=0)
    step = 512
    for n in range(0, width, step):
        wide = jnp.dot(pooled, w_in[:, n : n + step], preferred_element_type=F32)
        for k in range(parts):
            span = slice(k * t_rows, (k + 1) * t_rows)
            hid[span, n : n + step] = (
                tok[k][:, n : n + step].astype(F32) + wide[span]
            ).astype(BF16)
    queries = jnp.dot(hid[...], weight[...], preferred_element_type=F32).astype(BF16)
    first = pl.ds(pl.multiple_of(part * cols, cols), cols)
    values = hid[:, first]
    out_w = w_out[first, :]
    out_grad = contract(pooled_grad, out_w, 1, 1).astype(BF16)
    dim = head_cols // HEADS
    scale = 1.0 / math.sqrt(dim)
    total = parts * t_rows
    row = lax.broadcasted_iota(jnp.int32, (total, total), 0)
    col = lax.broadcasted_iota(jnp.int32, (total, total), 1)
    same = lax.div(row, t_rows) == lax.div(col, t_rows)
    outs, grads = [], []
    for h in range(cols // dim):
        lanes = slice(h * dim, (h + 1) * dim)
        q, v, g = queries[:, lanes], values[:, lanes], out_grad[:, lanes]
        scores = contract(q, q, 1, 1) * scale
        scores = jnp.where(row == col, -1000000000.0, scores)
        scores = jnp.where(same, scores, -3.0e38)
        e = jnp.exp(scores - jnp.max(scores, axis=1, keepdims=True))
        prob = e / jnp.sum(e, axis=1, keepdims=True)
        attended = jnp.dot(prob.astype(BF16), v, preferred_element_type=F32)
        outs.append((v.astype(F32) + attended).astype(BF16))
        prob_grad = contract(g, v, 1, 1)
        inner = jnp.sum(prob_grad * prob, axis=1, keepdims=True)
        score_grad = (prob * (prob_grad - inner) * scale).astype(BF16)
        grads.append(
            jnp.dot(score_grad, q, preferred_element_type=F32) + contract(score_grad, q, 0, 0)
        )
    output = jnp.concatenate(outs, axis=1)
    q_grad = jnp.concatenate(grads, axis=1).astype(BF16)
    rest = (width - head_cols) // parts
    second = pl.ds(pl.multiple_of(head_cols + part * rest, rest), rest)
    up = jnp.dot(output, out_w, preferred_element_type=F32) + jnp.dot(
        hid[:, second], w_out[second, :], preferred_element_type=F32
    )
    for k in range(parts):
        up_ref[k] = up[k * t_rows : (k + 1) * t_rows].astype(BF16)
    for k in range(pairs):
        chunk = pl.ds(pl.multiple_of((pair ^ k) * (2 * rows), 2 * rows), 2 * rows)
        term[...] = contract(hid[:, chunk], q_grad, 0, 0)
        keep_ref[k] = term[pl.ds(pl.multiple_of(core * rows, rows), rows), :].astype(BF16)
        give_ref[k] = term[pl.ds(pl.multiple_of((1 - core) * rows, rows), rows), :].astype(BF16)


def attend(tok, pooled, near, far, w_in, w_out):
    parts = len(tok)
    t_rows, width = tok[0].shape
    pairs, rows, cols = near.shape
    channels = w_in.shape[0]
    shape = jax.ShapeDtypeStruct((pairs, rows, cols), BF16)
    return pl.pallas_call(
        functools.partial(attend_kernel, parts),
        in_specs=[VMEM] * (2 * parts + 4),
        out_specs=[VMEM] * 3,
        out_shape=[jax.ShapeDtypeStruct((parts, t_rows, channels), BF16), shape, shape],
        scratch_shapes=[
            pltpu.VMEM((width, cols), BF16),
            pltpu.VMEM((parts * t_rows, width), BF16),
            pltpu.VMEM((2 * rows, cols), F32),
        ],
        compiler_params=params(24),
        name="attend",
    )(*tok, *pooled, near, far, w_in, w_out)


def unpool_kernel(owners_ref, clusters_ref, feat_ref, near, far, out_ref, rows_ref):
    step = pl.program_id(0)
    blocks, rows = clusters_ref.shape
    pairs, t_rows, _ = near.shape

    @pl.when(step == 0)
    def _():
        me = lax.axis_index("shard")
        for k in range(pairs):
            mine = me ^ (2 * k)
            rows_ref[pl.ds(pl.multiple_of(mine * t_rows, t_rows), t_rows), :] = near[k]
            rows_ref[pl.ds(pl.multiple_of((mine ^ 1) * t_rows, t_rows), t_rows), :] = far[k]

    token = lax.broadcasted_iota(jnp.int32, (t_rows, rows), 0)
    for b in range(blocks):
        member = (clusters_ref[b : b + 1, :] == token).astype(F32).astype(BF16)
        place = pl.ds(pl.multiple_of(owners_ref[step * blocks + b] * t_rows, t_rows), t_rows)
        span = pl.ds(b * rows, rows)
        picked = contract(member, rows_ref[place, :], 0, 0)
        out_ref[span, :] = (feat_ref[span, :].astype(F32) + picked).astype(BF16)


def unpool(particles, clusters, owners, near, far):
    num_blocks = owners.shape[0]
    count, width = particles.shape
    rows = count // num_blocks
    steps = 4
    pairs, t_rows, _ = near.shape
    whole = pl.BlockSpec(near.shape, lambda i, own: (0, 0, 0))
    return pl.pallas_call(
        unpool_kernel,
        grid_spec=pltpu.PrefetchScalarGridSpec(
            num_scalar_prefetch=1,
            grid=(steps,),
            in_specs=[
                pl.BlockSpec((num_blocks // steps, rows), lambda i, own: (i, 0)),
                pl.BlockSpec((count // steps, width), lambda i, own: (i, 0)),
                whole,
                whole,
            ],
            out_specs=pl.BlockSpec((count // steps, width), lambda i, own: (i, 0)),
            scratch_shapes=[pltpu.VMEM((2 * pairs * t_rows, width), BF16)],
        ),
        out_shape=jax.ShapeDtypeStruct(particles.shape, BF16),
        compiler_params=params(16),
        name="unpool",
    )(owners, clusters.reshape(num_blocks, rows), particles, near, far)


def spread_kernel(*refs):
    pieces, out_ref = refs[:-1], refs[-1]
    part = lax.rem(lax.axis_index("group"), len(pieces))
    cols = pieces[0].shape[1]
    for k, piece in enumerate(pieces):
        out_ref[:, pl.ds(pl.multiple_of((part ^ k) * cols, cols), cols)] = piece[...].astype(F32)


def spread(pieces):
    rows, cols = pieces[0].shape
    return pl.pallas_call(
        spread_kernel,
        in_specs=[VMEM] * len(pieces),
        out_specs=VMEM,
        out_shape=jax.ShapeDtypeStruct((rows, cols * len(pieces)), F32),
        compiler_params=params(16),
        name="spread",
    )(*pieces)


def swap(x, axis, k):
    n = lax.axis_size(axis)
    return lax.ppermute(x, axis, [(i, i ^ k) for i in range(n)])


def local(tokens, w_qk, w_in, w_out, particles, cotangent, clusters, owners):
    n_group, n_shard = lax.axis_size("group"), lax.axis_size("shard")
    parts = math.gcd(n_group, 4)
    pairs = n_shard // 2
    t_rows = tokens.shape[0]
    cols = w_qk.shape[1] // parts
    part = lax.rem(lax.axis_index("group"), parts)

    w_own = lax.dynamic_slice_in_dim(w_qk, part * cols, cols, axis=1)
    near = [w_own] + [swap(w_own, "shard", 2 * k) for k in range(1, pairs)]
    tok = [tokens] + [swap(tokens, "group", k) for k in range(1, parts)]
    near = jnp.stack(near)
    far = swap(near, "shard", 1)

    keep, give = pool(particles, cotangent, clusters, owners, t_rows, n_shard)
    joined = keep + swap(give, "shard", 1).astype(F32)
    sums = joined[0]
    for k in range(1, pairs):
        sums = sums + swap(joined[k].astype(BF16), "shard", 2 * k).astype(F32)
    channels = particles.shape[1]
    counts = jnp.sum(sums[:, 2 * channels :], axis=1, keepdims=True)
    pooled = jnp.concatenate(
        [sums[:, :channels] / jnp.maximum(counts, 1.0), sums[:, channels : 2 * channels]], axis=1
    ).astype(BF16)
    pooled = [pooled] + [swap(pooled, "group", k) for k in range(1, parts)]

    up, keep, give = attend(tok, pooled, near, far, w_in, w_out)

    joined = keep.astype(F32) + swap(give, "shard", 1).astype(F32)
    unpooled = up[0].astype(F32)
    for k in range(1, parts):
        unpooled = unpooled + swap(up[k], "group", k).astype(F32)
    unpooled = unpooled.astype(BF16)
    near = jnp.stack([unpooled] + [swap(unpooled, "shard", 2 * k) for k in range(1, pairs)])
    far = swap(near, "shard", 1)
    particle_out = unpool(particles, clusters, owners, near, far)

    grad = joined[0]
    for k in range(1, pairs):
        grad = grad + swap(joined[k].astype(BF16), "shard", 2 * k).astype(F32)
    if n_group > parts:
        part_sum = grad.astype(BF16)
        for k in range(1, n_group // parts):
            grad = grad + swap(part_sum, "group", k * parts).astype(F32)
    grad = grad.astype(BF16)
    qk_grad = spread([grad] + [swap(grad, "group", k) for k in range(1, parts)])
    return (particle_out, qk_grad)


def solution(mesh):
    placed = (
        P(("group", "shard"), None),
        P("shard", None),
        P(),
        P(),
        P(("group", "shard"), None),
        P(("group", "shard"), None),
        P(("group", "shard")),
        P(("group", "shard")),
    )
    return jax.shard_map(
        local,
        mesh=mesh,
        in_specs=placed,
        out_specs=(P(("group", "shard"), None), P("shard", None)),
        check_vma=False,
    )
```

time: 277 us -> 69.7 us (0.25)
  waiting for transfers between devices: 190 us -> 15.7 us
  starting transfers between devices: 14.4 us -> 39.4 us
  local copies, waits for them, and re-layouts: 20.5 us -> 4 us
  matrix products: 15.5 us -> 0 us
  blocking collectives: 14.3 us -> 0 us
  between operations: 13.9 us -> 0.86 us
  Pallas kernels: 0 us -> 8.85 us
  other arithmetic: 8 us -> 0.57 us
    all_to_all x3 -> x0, waiting for transfers between devices: 124 us -> none  [the longest x1 75.4 us: local(): lax.all_to_all(send_feat, 'shard', split_axis=0, concat_axis=0, tiled=True)]
    psum x1 -> x0, waiting for transfers between devices: 43.6 us -> none  [local(): qk_grad = lax.psum(shard_sum, 'group').astype(jnp.float32)]
    ppermute x0 -> x28, starting transfers between devices: none -> 39.4 us  [swap(): return lax.ppermute(x, axis, [(i, i ^ k) for i in range(n)])]
    reduce_scatter x1 -> x0, waiting for transfers between devices: 21.8 us -> none  [local(): lax.psum_scatter(jnp.einsum('td,tk->dk', hidden, q_grad, preferred_elemen...]
    ppermute x0 -> x28, waiting for transfers between devices: none -> 15.7 us  [swap(): return lax.ppermute(x, axis, [(i, i ^ k) for i in range(n)])]
    dot_general x12 -> x0, matrix products: 15.3 us -> none  [the longest x1 3.21 us: local(): jnp.einsum('td,tk->dk', hidden, q_grad, preferred_element_type=jnp.float32)]
    all_gather x1 -> x0, blocking collectives: 14.3 us -> none  [local(): all_tokens = lax.all_gather(unpooled, 'shard', axis=0, tiled=True)]
    all_to_all x3 -> x0, starting transfers between devices: 14.3 us -> none  [the longest x1 6.33 us: local(): lax.all_to_all(send_label, 'shard', split_axis=0, concat_axis=0, tiled=True)]
  transfers between devices with their start and end apart: 6 -> 28, of which waited for: 5 -> 10; matrix products, arithmetic and copies ran while one was open for 11% -> 1% of each run, Pallas kernels for 0% -> 4%
where the time goes in v1:
time: 69.7 us; the launch traced here: 69.4 us
  starting transfers between devices  39.4 us (57%)
  waiting for transfers between devices  15.7 us (23%)
  Pallas kernels  8.85 us (13%)
  local copies, waits for them, and re-layouts  4 us (6%)
  between operations  0.86 us (1%)
    ppermute x28, starting transfers between devices, swap(): return lax.ppermute(x, axis, [(i, i ^ k) for i in range(n)])  39.4 us
    ppermute x28, waiting for transfers between devices, swap(): return lax.ppermute(x, axis, [(i, i ^ k) for i in range(n)])  15.7 us
    unnamed x20, local copies, waits for them, and re-layouts  3.91 us
    pallas_call x1, Pallas kernels, attend(): pl.pallas_call(functools.partial(attend_kernel, parts), in_specs=[VMEM] *...  3.32 us
    pallas_call x1, Pallas kernels, unpool(): pl.pallas_call(unpool_kernel, grid_spec=pltpu.PrefetchScalarGridSpec(num_...  2.82 us
    pallas_call x1, Pallas kernels, pool(): pl.pallas_call(functools.partial(pool_kernel, t_rows), grid_spec=pltpu.Pr...  1.64 us
  transfers between devices with their start and end apart: 28, of which 10 were waited for; matrix products, arithmetic and copies ran while one was open for 1% of the time, Pallas kernels for 4%

profile of v1, /device:TPU:0, one launch (start us, length us, event | category | flops | bytes accessed | tf_op | source)
XLA Modules:
  0.0 69.4 jit_solution(3710233310720407046)
XLA Ops:
  0.7 0.7 %copy-done.9 = s32[32]{0:T(128)S(1)} copy-done((s32[32]{0:T(128)S(1)}, s32[32]{0:T(128)}, u32[]{:S(2)}) %copy-start.9) | copy-done | bytes 152
  1.4 1.2 %copy-done.1 = bf16[4096,128]{1,0:T(8,128)(2,1)S(1)} copy-done((bf16[4096,128]{1,0:T(8,128)(2,1)S(1)}, bf16[4096,128]{1,0:T(8,128)(2,1)}, u32[]{:S(2)}) %copy-start.1) | copy-done | bytes 1048600
  2.6 1.2 %copy-done.3 = bf16[4096,128]{1,0:T(8,128)(2,1)S(1)} copy-done((bf16[4096,128]{1,0:T(8,128)(2,1)S(1)}, bf16[4096,128]{1,0:T(8,128)(2,1)}, u32[]{:S(2)}) %copy-start.3) | copy-done | bytes 1048600
  3.8 0.7 %copy-done.7 = s32[4096]{0:T(1024)S(1)} copy-done((s32[4096]{0:T(1024)S(1)}, s32[4096]{0:T(1024)}, u32[]{:S(2)}) %copy-start.7) | copy-done | bytes 16408
  4.5 1.6 %pool.1 = (f32[4,64,384]{2,1,0:T(8,128)S(1)}, bf16[4,64,384]{2,1,0:T(8,128)(2,1)S(1)}) custom-call(s32[32]{0:T(128)S(1)} %copy-done.9, s32[32,128]{1,0:T(8,128)S(1)} %bitcast.49, bf16[4096,128]{1,0:T(8,128)(2,1)S(1)} %copy-done.1, bf16[4096,128]{1,0:T(8,128)(2,1)S(1)} %copy-done.3), custom_call_target="tpu_custom_call" | custom-call | tf_op jit(solution)/shard_map/pool/pallas_call | solution.py:63
  6.2 0.5 collective-permute-start.3
  6.7 3.7 %collective-permute-start.11 = (bf16[256,256]{1,0:T(8,128)(2,1)S(1)}, bf16[256,256]{1,0:T(8,128)(2,1)S(1)}, u32[]{:S(2)}, u32[]{:S(2)}) collective-permute-start(bf16[256,256]{1,0:T(8,128)(2,1)S(1)} %constant_dynamic-slice_fusion), channel_id=1, source_target_pairs={{0,4},{1,5},{2,6},{3,7},{4,0},{5,1},{6,2},{7,3},{8,12},{9,13},{10,... | collective-permute-start | bytes 393224 | tf_op jit(solution)/shard_map/ppermute | solution.py:244
  10.4 1.6 %collective-permute-start.10 = (bf16[256,256]{1,0:T(8,128)(2,1)S(1)}, bf16[256,256]{1,0:T(8,128)(2,1)S(1)}, u32[]{:S(2)}, u32[]{:S(2)}) collective-permute-start(bf16[256,256]{1,0:T(8,128)(2,1)S(1)} %constant_dynamic-slice_fusion), channel_id=1, source_target_pairs={{0,2},{1,3},{2,0},{3,1},{4,6},{5,7},{6,4},{7,5},{8,10},{9,11},{10,... | collective-permute-start | bytes 393224 | tf_op jit(solution)/shard_map/ppermute | solution.py:244
  12.0 1.7 %collective-permute-start.1 = (bf16[64,2048]{1,0:T(8,128)(2,1)S(1)}, bf16[64,2048]{1,0:T(8,128)(2,1)S(1)}, u32[]{:S(2)}, u32[]{:S(2)}) collective-permute-start(bf16[64,2048]{1,0:T(8,128)(2,1)S(1)} %copy-done.6), channel_id=1, source_target_pairs={{0,16},{8,24},{16,0},{24,8},{1,17},{9,25},{17,1},{25,9},{2,18},{10... | collective-permute-start | bytes 786440 | tf_op jit(solution)/shard_map/ppermute | solution.py:244
  13.8 1.6 %collective-permute-start = (bf16[64,2048]{1,0:T(8,128)(2,1)S(1)}, bf16[64,2048]{1,0:T(8,128)(2,1)S(1)}, u32[]{:S(2)}, u32[]{:S(2)}) collective-permute-start(bf16[64,2048]{1,0:T(8,128)(2,1)S(1)} %copy-done.6), channel_id=1, source_target_pairs={{0,8},{8,0},{16,24},{24,16},{1,9},{9,1},{17,25},{25,17},{2,10},{10... | collective-permute-start | bytes 786440 | tf_op jit(solution)/shard_map/ppermute | solution.py:244
  15.4 2.2 %collective-permute-done.11 = bf16[256,256]{1,0:T(8,128)(2,1)S(1)} collective-permute-done((bf16[256,256]{1,0:T(8,128)(2,1)S(1)}, bf16[256,256]{1,0:T(8,128)(2,1)S(1)}, u32[]{:S(2)}, u32[]{:S(2)}) %collective-permute-start.11) | collective-permute-done | bytes 131104 | tf_op jit(solution)/shard_map/ppermute | solution.py:244
  17.6 0.7 %collective-permute-start.4 = (bf16[64,384]{1,0:T(8,128)(2,1)S(1)}, bf16[64,384]{1,0:T(8,128)(2,1)S(1)}, u32[]{:S(2)}, u32[]{:S(2)}) collective-permute-start(bf16[64,384]{1,0:T(8,128)(2,1)S(1)} %get-tuple-element.19), channel_id=1, source_target_pairs={{0,2},{1,3},{2,0},{3,1},{4,6},{5,7},{6,4},{7,5},{8,10},{9,11},{10,... | collective-permute-start | bytes 147464 | tf_op jit(solution)/shard_map/ppermute | solution.py:244
  18.3 3.1 %collective-permute-start.6 = (bf16[64,384]{1,0:T(8,128)(2,1)S(1)}, bf16[64,384]{1,0:T(8,128)(2,1)S(1)}, u32[]{:S(2)}, u32[]{:S(2)}) collective-permute-start(bf16[64,384]{1,0:T(8,128)(2,1)S(1)} %get-tuple-element.20), channel_id=1, source_target_pairs={{0,6},{1,7},{2,4},{3,5},{4,2},{5,3},{6,0},{7,1},{8,14},{9,15},{10,... | collective-permute-start | bytes 147464 | tf_op jit(solution)/shard_map/ppermute | solution.py:244
  21.4 5.3 %collective-permute-start.5 = (bf16[64,384]{1,0:T(8,128)(2,1)S(1)}, bf16[64,384]{1,0:T(8,128)(2,1)S(1)}, u32[]{:S(2)}, u32[]{:S(2)}) collective-permute-start(bf16[64,384]{1,0:T(8,128)(2,1)S(1)} %get-tuple-element.21), channel_id=1, source_target_pairs={{0,4},{1,5},{2,6},{3,7},{4,0},{5,1},{6,2},{7,3},{8,12},{9,13},{10,... | collective-permute-start | bytes 147464 | tf_op jit(solution)/shard_map/ppermute | solution.py:244
  26.7 0.1 pad_maximum_fusion.refs_8_
  26.8 2.5 %collective-permute-start.2 = (bf16[64,2048]{1,0:T(8,128)(2,1)S(1)}, bf16[64,2048]{1,0:T(8,128)(2,1)S(1)}, u32[]{:S(2)}, u32[]{:S(2)}) collective-permute-start(bf16[64,2048]{1,0:T(8,128)(2,1)S(1)} %copy-done.6), channel_id=1, source_target_pairs={{0,24},{8,16},{16,8},{24,0},{1,25},{9,17},{17,9},{25,1},{2,26},{10... | collective-permute-start | bytes 786440 | tf_op jit(solution)/shard_map/ppermute | solution.py:244
  29.4 0.1 slice_reduce_fusion
  29.5 0.1 fusion.7
  29.6 2.0 %collective-permute-start.9 = (bf16[64,256]{1,0:T(8,128)(2,1)S(1)}, bf16[64,256]{1,0:T(8,128)(2,1)S(1)}, u32[]{:S(2)}, u32[]{:S(2)}) collective-permute-start(bf16[64,256]{1,0:T(8,128)(2,1)S(1)} %pad_maximum_fusion.2.refs_4_), channel_id=1, source_target_pairs={{0,24},{8,16},{16,8},{24,0},{1,25},{9,17},{17,9},{25,1},{2,26},{10... | collective-permute-start | bytes 98312 | tf_op jit(solution)/shard_map/ppermute | solution.py:244
  31.6 0.5 collective-permute-start.8
  32.1 1.1 %collective-permute-start.7 = (bf16[64,256]{1,0:T(8,128)(2,1)S(1)}, bf16[64,256]{1,0:T(8,128)(2,1)S(1)}, u32[]{:S(2)}, u32[]{:S(2)}) collective-permute-start(bf16[64,256]{1,0:T(8,128)(2,1)S(1)} %pad_maximum_fusion.2.refs_4_), channel_id=1, source_target_pairs={{0,8},{8,0},{16,24},{24,16},{1,9},{9,1},{17,25},{25,17},{2,10},{10... | collective-permute-start | bytes 98312 | tf_op jit(solution)/shard_map/ppermute | solution.py:244
  33.2 3.4 %collective-permute-done.2.refs_3_ = bf16[64,2048]{1,0:T(8,128)(2,1)S(1)} collective-permute-done((bf16[64,2048]{1,0:T(8,128)(2,1)S(1)}, bf16[64,2048]{1,0:T(8,128)(2,1)S(1)}, u32[]{:S(2)}, u32[]{:S(2)}) %collective-permute-start.2) | collective-permute-done | bytes 262176 | tf_op jit(solution)/shard_map/ppermute | solution.py:244
  36.5 0.4 collective-permute-done.9.refs_7_
  36.9 0.3 collective-permute-done.8.refs_6_
  37.1 0.1 collective-permute-done.7.refs_5_
  37.2 3.3 %attend.1 = (bf16[4,64,128]{2,1,0:T(8,128)(2,1)S(1)}, bf16[4,256,256]{2,1,0:T(8,128)(2,1)S(1)}, bf16[4,256,256]{2,1,0:T(8,128)(2,1)S(1)}) custom-call(bf16[64,2048]{1,0:T(8,128)(2,1)S(1)} %copy-done.6, bf16[64,2048]{1,0:T(8,128)(2,1)S(1)} %collective-permute-done.refs_1_, bf16[64,2048]{1,0:T(8,128)(2,1)S(1)} %collective-permute-done.1.refs_2_, ...), custom_call_target="tpu_custom_call" | custom-call | tf_op jit(solution)/shard_map/attend/pallas_call | solution.py:158
  40.6 0.1 collective-permute-start.21
  40.7 1.6 %collective-permute-start.14 = (bf16[64,128]{1,0:T(8,128)(2,1)S(1)}, bf16[64,128]{1,0:T(8,128)(2,1)S(1)}, u32[]{:S(2)}, u32[]{:S(2)}) collective-permute-start(bf16[64,128]{1,0:T(8,128)(2,1)S(1)} %get-tuple-element.22), channel_id=1, source_target_pairs={{0,8},{8,0},{16,24},{24,16},{1,9},{9,1},{17,25},{25,17},{2,10},{10... | collective-permute-start | bytes 49160 | tf_op jit(solution)/shard_map/ppermute | solution.py:244
  42.2 1.4 %collective-permute-start.16 = (bf16[64,128]{1,0:T(8,128)(2,1)S(1)}, bf16[64,128]{1,0:T(8,128)(2,1)S(1)}, u32[]{:S(2)}, u32[]{:S(2)}) collective-permute-start(bf16[64,128]{1,0:T(8,128)(2,1)S(1)} %get-tuple-element.23), channel_id=1, source_target_pairs={{0,24},{8,16},{16,8},{24,0},{1,25},{9,17},{17,9},{25,1},{2,26},{10... | collective-permute-start | bytes 49160 | tf_op jit(solution)/shard_map/ppermute | solution.py:244
  43.6 0.6 collective-permute-start.15
  44.2 0.1 fusion.11
  44.4 0.1 collective-permute-start.22
  44.5 3.1 %collective-permute-start.24 = (bf16[256,256]{1,0:T(8,128)(2,1)S(1)}, bf16[256,256]{1,0:T(8,128)(2,1)S(1)}, u32[]{:S(2)}, u32[]{:S(2)}) collective-permute-start(bf16[256,256]{1,0:T(8,128)(2,1)S(1)} %get-tuple-element.17), channel_id=1, source_target_pairs={{0,6},{1,7},{2,4},{3,5},{4,2},{5,3},{6,0},{7,1},{8,14},{9,15},{10,... | collective-permute-start | bytes 393224 | tf_op jit(solution)/shard_map/ppermute | solution.py:244
  47.6 0.3 collective-permute-start.23
  48.0 1.3 %collective-permute-start.19 = (bf16[64,128]{1,0:T(8,128)(2,1)S(1)}, bf16[64,128]{1,0:T(8,128)(2,1)S(1)}, u32[]{:S(2)}, u32[]{:S(2)}) collective-permute-start(bf16[64,128]{1,0:T(8,128)(2,1)S(1)} %fusion.10), channel_id=1, source_target_pairs={{0,6},{1,7},{2,4},{3,5},{4,2},{5,3},{6,0},{7,1},{8,14},{9,15},{10,... | collective-permute-start | bytes 49160 | tf_op jit(solution)/shard_map/ppermute | solution.py:244
  49.2 1.5 %collective-permute-start.18 = (bf16[64,128]{1,0:T(8,128)(2,1)S(1)}, bf16[64,128]{1,0:T(8,128)(2,1)S(1)}, u32[]{:S(2)}, u32[]{:S(2)}) collective-permute-start(bf16[64,128]{1,0:T(8,128)(2,1)S(1)} %fusion.10), channel_id=1, source_target_pairs={{0,4},{1,5},{2,6},{3,7},{4,0},{5,1},{6,2},{7,3},{8,12},{9,13},{10,... | collective-permute-start | bytes 49160 | tf_op jit(solution)/shard_map/ppermute | solution.py:244
  50.7 1.7 %collective-permute-start.17 = (bf16[64,128]{1,0:T(8,128)(2,1)S(1)}, bf16[64,128]{1,0:T(8,128)(2,1)S(1)}, u32[]{:S(2)}, u32[]{:S(2)}) collective-permute-start(bf16[64,128]{1,0:T(8,128)(2,1)S(1)} %fusion.10), channel_id=1, source_target_pairs={{0,2},{1,3},{2,0},{3,1},{4,6},{5,7},{6,4},{7,5},{8,10},{9,11},{10,... | collective-permute-start | bytes 49160 | tf_op jit(solution)/shard_map/ppermute | solution.py:244
  52.4 2.4 %collective-permute-done.24 = bf16[256,256]{1,0:T(8,128)(2,1)S(1)} collective-permute-done((bf16[256,256]{1,0:T(8,128)(2,1)S(1)}, bf16[256,256]{1,0:T(8,128)(2,1)S(1)}, u32[]{:S(2)}, u32[]{:S(2)}) %collective-permute-start.24) | collective-permute-done | bytes 131104 | tf_op jit(solution)/shard_map/ppermute | solution.py:244
  54.8 5.4 %collective-permute-done.23 = bf16[256,256]{1,0:T(8,128)(2,1)S(1)} collective-permute-done((bf16[256,256]{1,0:T(8,128)(2,1)S(1)}, bf16[256,256]{1,0:T(8,128)(2,1)S(1)}, u32[]{:S(2)}, u32[]{:S(2)}) %collective-permute-start.23) | collective-permute-done | bytes 131104 | tf_op jit(solution)/shard_map/ppermute | solution.py:244
  60.2 0.1 fusion.3.refs_0_
  60.3 2.4 %collective-permute-start.27 = (bf16[256,256]{1,0:T(8,128)(2,1)S(1)}, bf16[256,256]{1,0:T(8,128)(2,1)S(1)}, u32[]{:S(2)}, u32[]{:S(2)}) collective-permute-start(bf16[256,256]{1,0:T(8,128)(2,1)S(1)} %fusion.3.refs_0_), channel_id=1, source_target_pairs={{0,24},{8,16},{16,8},{24,0},{1,25},{9,17},{17,9},{25,1},{2,26},{10... | collective-permute-start | bytes 393224 | tf_op jit(solution)/shard_map/ppermute | solution.py:244
  62.7 0.6 collective-permute-start.26
  63.2 0.6 collective-permute-start.25
  63.9 0.1 collective-permute-start.20
  64.0 1.2 %collective-permute-done.20.far = bf16[4,64,128]{2,1,0:T(8,128)(2,1)S(1)} collective-permute-done((bf16[4,64,128]{2,1,0:T(8,128)(2,1)S(1)}, bf16[4,64,128]{2,1,0:T(8,128)(2,1)S(1)}, u32[]{:S(2)}, u32[]{:S(2)}) %collective-permute-start.20) | collective-permute-done | bytes 65568 | tf_op jit(solution)/shard_map/ppermute | solution.py:244
  65.2 2.8 %unpool.1 = bf16[4096,128]{1,0:T(8,128)(2,1)} custom-call(s32[32]{0:T(128)S(1)} %copy-done.9, s32[32,128]{1,0:T(8,128)S(1)} %bitcast.50, bf16[4096,128]{1,0:T(8,128)(2,1)S(1)} %copy-done.2, bf16[4,64,128]{2,1,0:T(8,128)(2,1)S(1)} %pad_maximum_fusion.1.near, bf16[4,64,128]{2,1,0:T(8,128)(2,1)S(1)} %collective-permute-done.20.far), custom_call_target="tpu_custom_call" | custom-call | tf_op jit(solution)/shard_map/unpool/pallas_call | solution.py:202
  68.0 0.3 collective-permute-done.26.refs_2_
  68.3 1.1 %spread.1 = f32[256,1024]{1,0:T(8,128)} custom-call(bf16[256,256]{1,0:T(8,128)(2,1)S(1)} %fusion.3.refs_0_, bf16[256,256]{1,0:T(8,128)(2,1)S(1)} %collective-permute-done.25.refs_1_, bf16[256,256]{1,0:T(8,128)(2,1)S(1)} %collective-permute-done.26.refs_2_, bf16[256,256]{1,0:T(8,128)(2,1)S(1)} %collective-permute-done.27.refs_3_), custom_call_target="tpu_custom_call" | custom-call | tf_op jit(solution)/shard_map/spread/pallas_call | solution.py:232
  (49 shorter events, 0.4 us)
Async XLA Ops:
  0.6 6.1 %copy-start = (bf16[256,1024]{1,0:T(8,128)(2,1)S(1)}, bf16[256,1024]{1,0:T(8,128)(2,1)}, u32[]{:S(2)}) copy-start(bf16[256,1024]{1,0:T(8,128)(2,1)} %param.9) | copy-start | bytes 1572868
  0.6 0.7 %copy-start.9 = (s32[32]{0:T(128)S(1)}, s32[32]{0:T(128)}, u32[]{:S(2)}) copy-start(s32[32]{0:T(128)} %owners_ref.3) | copy-start | bytes 388
  1.4 1.2 %copy-start.1 = (bf16[4096,128]{1,0:T(8,128)(2,1)S(1)}, bf16[4096,128]{1,0:T(8,128)(2,1)}, u32[]{:S(2)}) copy-start(bf16[4096,128]{1,0:T(8,128)(2,1)} %feat_ref.3) | copy-start | bytes 3145732
  2.6 1.2 %copy-start.3 = (bf16[4096,128]{1,0:T(8,128)(2,1)S(1)}, bf16[4096,128]{1,0:T(8,128)(2,1)}, u32[]{:S(2)}) copy-start(bf16[4096,128]{1,0:T(8,128)(2,1)} %grad_ref.1) | copy-start | bytes 3145732
  3.8 0.7 %copy-start.7 = (s32[4096]{0:T(1024)S(1)}, s32[4096]{0:T(1024)}, u32[]{:S(2)}) copy-start(s32[4096]{0:T(1024)} %param.14) | copy-start | bytes 49156
  6.2 5.8 %copy-start.6 = (bf16[64,2048]{1,0:T(8,128)(2,1)S(1)}, bf16[64,2048]{1,0:T(8,128)(2,1)}, u32[]{:S(2)}) copy-start(bf16[64,2048]{1,0:T(8,128)(2,1)} %refs_0_.1) | copy-start | bytes 786436
  6.2 7.6 %collective-permute-start.3 = (bf16[4,64,384]{2,1,0:T(8,128)(2,1)S(1)}, bf16[4,64,384]{2,1,0:T(8,128)(2,1)S(1)}, u32[]{:S(2)}, u32[]{:S(2)}) collective-permute-start(bf16[4,64,384]{2,1,0:T(8,128)(2,1)S(1)} %get-tuple-element.8), channel_id=1, source_target_pairs={{0,1},{1,0},{2,3},{3,2},{4,5},{5,4},{6,7},{7,6},{8,9},{9,8},{10,11... | collective-permute-start | bytes 589832 | tf_op jit(solution)/shard_map/ppermute | solution.py:244
  6.7 10.9 %collective-permute-start.11 = (bf16[256,256]{1,0:T(8,128)(2,1)S(1)}, bf16[256,256]{1,0:T(8,128)(2,1)S(1)}, u32[]{:S(2)}, u32[]{:S(2)}) collective-permute-start(bf16[256,256]{1,0:T(8,128)(2,1)S(1)} %constant_dynamic-slice_fusion), channel_id=1, source_target_pairs={{0,4},{1,5},{2,6},{3,7},{4,0},{5,1},{6,2},{7,3},{8,12},{9,13},{10,... | collective-permute-start | bytes 393224 | tf_op jit(solution)/shard_map/ppermute | solution.py:244
  10.4 7.9 %collective-permute-start.10 = (bf16[256,256]{1,0:T(8,128)(2,1)S(1)}, bf16[256,256]{1,0:T(8,128)(2,1)S(1)}, u32[]{:S(2)}, u32[]{:S(2)}) collective-permute-start(bf16[256,256]{1,0:T(8,128)(2,1)S(1)} %constant_dynamic-slice_fusion), channel_id=1, source_target_pairs={{0,2},{1,3},{2,0},{3,1},{4,6},{5,7},{6,4},{7,5},{8,10},{9,11},{10,... | collective-permute-start | bytes 393224 | tf_op jit(solution)/shard_map/ppermute | solution.py:244
  12.0 9.4 %collective-permute-start.12 = (bf16[256,256]{1,0:T(8,128)(2,1)S(1)}, bf16[256,256]{1,0:T(8,128)(2,1)S(1)}, u32[]{:S(2)}, u32[]{:S(2)}) collective-permute-start(bf16[256,256]{1,0:T(8,128)(2,1)S(1)} %constant_dynamic-slice_fusion), channel_id=1, source_target_pairs={{0,6},{1,7},{2,4},{3,5},{4,2},{5,3},{6,0},{7,1},{8,14},{9,15},{10,... | collective-permute-start | bytes 393224 | tf_op jit(solution)/shard_map/ppermute | solution.py:244
  12.0 19.6 %collective-permute-start.1 = (bf16[64,2048]{1,0:T(8,128)(2,1)S(1)}, bf16[64,2048]{1,0:T(8,128)(2,1)S(1)}, u32[]{:S(2)}, u32[]{:S(2)}) collective-permute-start(bf16[64,2048]{1,0:T(8,128)(2,1)S(1)} %copy-done.6), channel_id=1, source_target_pairs={{0,16},{8,24},{16,0},{24,8},{1,17},{9,25},{17,1},{25,9},{2,18},{10... | collective-permute-start | bytes 786440 | tf_op jit(solution)/shard_map/ppermute | solution.py:244
  13.8 18.3 %collective-permute-start = (bf16[64,2048]{1,0:T(8,128)(2,1)S(1)}, bf16[64,2048]{1,0:T(8,128)(2,1)S(1)}, u32[]{:S(2)}, u32[]{:S(2)}) collective-permute-start(bf16[64,2048]{1,0:T(8,128)(2,1)S(1)} %copy-done.6), channel_id=1, source_target_pairs={{0,8},{8,0},{16,24},{24,16},{1,9},{9,1},{17,25},{25,17},{2,10},{10... | collective-permute-start | bytes 786440 | tf_op jit(solution)/shard_map/ppermute | solution.py:244
  17.6 9.2 %collective-permute-start.4 = (bf16[64,384]{1,0:T(8,128)(2,1)S(1)}, bf16[64,384]{1,0:T(8,128)(2,1)S(1)}, u32[]{:S(2)}, u32[]{:S(2)}) collective-permute-start(bf16[64,384]{1,0:T(8,128)(2,1)S(1)} %get-tuple-element.19), channel_id=1, source_target_pairs={{0,2},{1,3},{2,0},{3,1},{4,6},{5,7},{6,4},{7,5},{8,10},{9,11},{10,... | collective-permute-start | bytes 147464 | tf_op jit(solution)/shard_map/ppermute | solution.py:244
  18.3 11.0 %collective-permute-start.6 = (bf16[64,384]{1,0:T(8,128)(2,1)S(1)}, bf16[64,384]{1,0:T(8,128)(2,1)S(1)}, u32[]{:S(2)}, u32[]{:S(2)}) collective-permute-start(bf16[64,384]{1,0:T(8,128)(2,1)S(1)} %get-tuple-element.20), channel_id=1, source_target_pairs={{0,6},{1,7},{2,4},{3,5},{4,2},{5,3},{6,0},{7,1},{8,14},{9,15},{10,... | collective-permute-start | bytes 147464 | tf_op jit(solution)/shard_map/ppermute | solution.py:244
  21.4 7.9 %collective-permute-start.5 = (bf16[64,384]{1,0:T(8,128)(2,1)S(1)}, bf16[64,384]{1,0:T(8,128)(2,1)S(1)}, u32[]{:S(2)}, u32[]{:S(2)}) collective-permute-start(bf16[64,384]{1,0:T(8,128)(2,1)S(1)} %get-tuple-element.21), channel_id=1, source_target_pairs={{0,4},{1,5},{2,6},{3,7},{4,0},{5,1},{6,2},{7,3},{8,12},{9,13},{10,... | collective-permute-start | bytes 147464 | tf_op jit(solution)/shard_map/ppermute | solution.py:244
  26.7 10.5 %copy-start.5 = (bf16[2048,128]{1,0:T(8,128)(2,1)S(1)}, bf16[2048,128]{1,0:T(8,128)(2,1)}, u32[]{:S(2)}) copy-start(bf16[2048,128]{1,0:T(8,128)(2,1)} %refs_11_.1) | copy-start | bytes 1572868
  26.8 10.5 %copy-start.4 = (bf16[128,2048]{1,0:T(8,128)(2,1)S(1)}, bf16[128,2048]{1,0:T(8,128)(2,1)}, u32[]{:S(2)}) copy-start(bf16[128,2048]{1,0:T(8,128)(2,1)} %refs_10_.1) | copy-start | bytes 1572868
  26.8 9.7 %collective-permute-start.2 = (bf16[64,2048]{1,0:T(8,128)(2,1)S(1)}, bf16[64,2048]{1,0:T(8,128)(2,1)S(1)}, u32[]{:S(2)}, u32[]{:S(2)}) collective-permute-start(bf16[64,2048]{1,0:T(8,128)(2,1)S(1)} %copy-done.6), channel_id=1, source_target_pairs={{0,24},{8,16},{16,8},{24,0},{1,25},{9,17},{17,9},{25,1},{2,26},{10... | collective-permute-start | bytes 786440 | tf_op jit(solution)/shard_map/ppermute | solution.py:244
  29.3 7.9 %collective-permute-start.13 = (bf16[4,256,256]{2,1,0:T(8,128)(2,1)S(1)}, bf16[4,256,256]{2,1,0:T(8,128)(2,1)S(1)}, u32[]{:S(2)}, u32[]{:S(2)}) collective-permute-start(bf16[4,256,256]{2,1,0:T(8,128)(2,1)S(1)} %pad_maximum_fusion.refs_8_), channel_id=1, source_target_pairs={{0,1},{1,0},{2,3},{3,2},{4,5},{5,4},{6,7},{7,6},{8,9},{9,8},{10,11... | collective-permute-start | bytes 1572872 | tf_op jit(solution)/shard_map/ppermute | solution.py:244
  29.6 7.3 %collective-permute-start.9 = (bf16[64,256]{1,0:T(8,128)(2,1)S(1)}, bf16[64,256]{1,0:T(8,128)(2,1)S(1)}, u32[]{:S(2)}, u32[]{:S(2)}) collective-permute-start(bf16[64,256]{1,0:T(8,128)(2,1)S(1)} %pad_maximum_fusion.2.refs_4_), channel_id=1, source_target_pairs={{0,24},{8,16},{16,8},{24,0},{1,25},{9,17},{17,9},{25,1},{2,26},{10... | collective-permute-start | bytes 98312 | tf_op jit(solution)/shard_map/ppermute | solution.py:244
  31.6 5.6 %collective-permute-start.8 = (bf16[64,256]{1,0:T(8,128)(2,1)S(1)}, bf16[64,256]{1,0:T(8,128)(2,1)S(1)}, u32[]{:S(2)}, u32[]{:S(2)}) collective-permute-start(bf16[64,256]{1,0:T(8,128)(2,1)S(1)} %pad_maximum_fusion.2.refs_4_), channel_id=1, source_target_pairs={{0,16},{8,24},{16,0},{24,8},{1,17},{9,25},{17,1},{25,9},{2,18},{10... | collective-permute-start | bytes 98312 | tf_op jit(solution)/shard_map/ppermute | solution.py:244
  32.1 5.2 %collective-permute-start.7 = (bf16[64,256]{1,0:T(8,128)(2,1)S(1)}, bf16[64,256]{1,0:T(8,128)(2,1)S(1)}, u32[]{:S(2)}, u32[]{:S(2)}) collective-permute-start(bf16[64,256]{1,0:T(8,128)(2,1)S(1)} %pad_maximum_fusion.2.refs_4_), channel_id=1, source_target_pairs={{0,8},{8,0},{16,24},{24,16},{1,9},{9,1},{17,25},{25,17},{2,10},{10... | collective-permute-start | bytes 98312 | tf_op jit(solution)/shard_map/ppermute | solution.py:244
  40.6 3.6 %collective-permute-start.21 = (bf16[4,256,256]{2,1,0:T(8,128)(2,1)S(1)}, bf16[4,256,256]{2,1,0:T(8,128)(2,1)S(1)}, u32[]{:S(2)}, u32[]{:S(2)}) collective-permute-start(bf16[4,256,256]{2,1,0:T(8,128)(2,1)S(1)} %get-tuple-element.11), channel_id=1, source_target_pairs={{0,1},{1,0},{2,3},{3,2},{4,5},{5,4},{6,7},{7,6},{8,9},{9,8},{10,11... | collective-permute-start | bytes 1572872 | tf_op jit(solution)/shard_map/ppermute | solution.py:244
  40.7 7.0 %collective-permute-start.14 = (bf16[64,128]{1,0:T(8,128)(2,1)S(1)}, bf16[64,128]{1,0:T(8,128)(2,1)S(1)}, u32[]{:S(2)}, u32[]{:S(2)}) collective-permute-start(bf16[64,128]{1,0:T(8,128)(2,1)S(1)} %get-tuple-element.22), channel_id=1, source_target_pairs={{0,8},{8,0},{16,24},{24,16},{1,9},{9,1},{17,25},{25,17},{2,10},{10... | collective-permute-start | bytes 49160 | tf_op jit(solution)/shard_map/ppermute | solution.py:244
  42.2 5.7 %collective-permute-start.16 = (bf16[64,128]{1,0:T(8,128)(2,1)S(1)}, bf16[64,128]{1,0:T(8,128)(2,1)S(1)}, u32[]{:S(2)}, u32[]{:S(2)}) collective-permute-start(bf16[64,128]{1,0:T(8,128)(2,1)S(1)} %get-tuple-element.23), channel_id=1, source_target_pairs={{0,24},{8,16},{16,8},{24,0},{1,25},{9,17},{17,9},{25,1},{2,26},{10... | collective-permute-start | bytes 49160 | tf_op jit(solution)/shard_map/ppermute | solution.py:244
  43.6 4.3 %collective-permute-start.15 = (bf16[64,128]{1,0:T(8,128)(2,1)S(1)}, bf16[64,128]{1,0:T(8,128)(2,1)S(1)}, u32[]{:S(2)}, u32[]{:S(2)}) collective-permute-start(bf16[64,128]{1,0:T(8,128)(2,1)S(1)} %get-tuple-element.24), channel_id=1, source_target_pairs={{0,16},{8,24},{16,0},{24,8},{1,17},{9,25},{17,1},{25,9},{2,18},{10... | collective-permute-start | bytes 49160 | tf_op jit(solution)/shard_map/ppermute | solution.py:244
  44.4 20.8 %copy-start.2 = (bf16[4096,128]{1,0:T(8,128)(2,1)S(1)}, bf16[4096,128]{1,0:T(8,128)(2,1)}, u32[]{:S(2)}) copy-start(bf16[4096,128]{1,0:T(8,128)(2,1)} %feat_ref.3) | copy-start | bytes 3145732
  44.4 6.3 %collective-permute-start.22 = (bf16[256,256]{1,0:T(8,128)(2,1)S(1)}, bf16[256,256]{1,0:T(8,128)(2,1)S(1)}, u32[]{:S(2)}, u32[]{:S(2)}) collective-permute-start(bf16[256,256]{1,0:T(8,128)(2,1)S(1)} %get-tuple-element.16), channel_id=1, source_target_pairs={{0,2},{1,3},{2,0},{3,1},{4,6},{5,7},{6,4},{7,5},{8,10},{9,11},{10,... | collective-permute-start | bytes 393224 | tf_op jit(solution)/shard_map/ppermute | solution.py:244
  44.5 10.3 %collective-permute-start.24 = (bf16[256,256]{1,0:T(8,128)(2,1)S(1)}, bf16[256,256]{1,0:T(8,128)(2,1)S(1)}, u32[]{:S(2)}, u32[]{:S(2)}) collective-permute-start(bf16[256,256]{1,0:T(8,128)(2,1)S(1)} %get-tuple-element.17), channel_id=1, source_target_pairs={{0,6},{1,7},{2,4},{3,5},{4,2},{5,3},{6,0},{7,1},{8,14},{9,15},{10,... | collective-permute-start | bytes 393224 | tf_op jit(solution)/shard_map/ppermute | solution.py:244
  47.6 12.6 %collective-permute-start.23 = (bf16[256,256]{1,0:T(8,128)(2,1)S(1)}, bf16[256,256]{1,0:T(8,128)(2,1)S(1)}, u32[]{:S(2)}, u32[]{:S(2)}) collective-permute-start(bf16[256,256]{1,0:T(8,128)(2,1)S(1)} %get-tuple-element.18), channel_id=1, source_target_pairs={{0,4},{1,5},{2,6},{3,7},{4,0},{5,1},{6,2},{7,3},{8,12},{9,13},{10,... | collective-permute-start | bytes 393224 | tf_op jit(solution)/shard_map/ppermute | solution.py:244
  48.0 15.2 %collective-permute-start.19 = (bf16[64,128]{1,0:T(8,128)(2,1)S(1)}, bf16[64,128]{1,0:T(8,128)(2,1)S(1)}, u32[]{:S(2)}, u32[]{:S(2)}) collective-permute-start(bf16[64,128]{1,0:T(8,128)(2,1)S(1)} %fusion.10), channel_id=1, source_target_pairs={{0,6},{1,7},{2,4},{3,5},{4,2},{5,3},{6,0},{7,1},{8,14},{9,15},{10,... | collective-permute-start | bytes 49160 | tf_op jit(solution)/shard_map/ppermute | solution.py:244
  49.2 14.6 %collective-permute-start.18 = (bf16[64,128]{1,0:T(8,128)(2,1)S(1)}, bf16[64,128]{1,0:T(8,128)(2,1)S(1)}, u32[]{:S(2)}, u32[]{:S(2)}) collective-permute-start(bf16[64,128]{1,0:T(8,128)(2,1)S(1)} %fusion.10), channel_id=1, source_target_pairs={{0,4},{1,5},{2,6},{3,7},{4,0},{5,1},{6,2},{7,3},{8,12},{9,13},{10,... | collective-permute-start | bytes 49160 | tf_op jit(solution)/shard_map/ppermute | solution.py:244
  50.7 13.1 %collective-permute-start.17 = (bf16[64,128]{1,0:T(8,128)(2,1)S(1)}, bf16[64,128]{1,0:T(8,128)(2,1)S(1)}, u32[]{:S(2)}, u32[]{:S(2)}) collective-permute-start(bf16[64,128]{1,0:T(8,128)(2,1)S(1)} %fusion.10), channel_id=1, source_target_pairs={{0,2},{1,3},{2,0},{3,1},{4,6},{5,7},{6,4},{7,5},{8,10},{9,11},{10,... | collective-permute-start | bytes 49160 | tf_op jit(solution)/shard_map/ppermute | solution.py:244
  60.3 7.7 %collective-permute-start.27 = (bf16[256,256]{1,0:T(8,128)(2,1)S(1)}, bf16[256,256]{1,0:T(8,128)(2,1)S(1)}, u32[]{:S(2)}, u32[]{:S(2)}) collective-permute-start(bf16[256,256]{1,0:T(8,128)(2,1)S(1)} %fusion.3.refs_0_), channel_id=1, source_target_pairs={{0,24},{8,16},{16,8},{24,0},{1,25},{9,17},{17,9},{25,1},{2,26},{10... | collective-permute-start | bytes 393224 | tf_op jit(solution)/shard_map/ppermute | solution.py:244
  62.7 5.7 %collective-permute-start.26 = (bf16[256,256]{1,0:T(8,128)(2,1)S(1)}, bf16[256,256]{1,0:T(8,128)(2,1)S(1)}, u32[]{:S(2)}, u32[]{:S(2)}) collective-permute-start(bf16[256,256]{1,0:T(8,128)(2,1)S(1)} %fusion.3.refs_0_), channel_id=1, source_target_pairs={{0,16},{8,24},{16,0},{24,8},{1,17},{9,25},{17,1},{25,9},{2,18},{10... | collective-permute-start | bytes 393224 | tf_op jit(solution)/shard_map/ppermute | solution.py:244
  63.2 5.1 %collective-permute-start.25 = (bf16[256,256]{1,0:T(8,128)(2,1)S(1)}, bf16[256,256]{1,0:T(8,128)(2,1)S(1)}, u32[]{:S(2)}, u32[]{:S(2)}) collective-permute-start(bf16[256,256]{1,0:T(8,128)(2,1)S(1)} %fusion.3.refs_0_), channel_id=1, source_target_pairs={{0,8},{8,0},{16,24},{24,16},{1,9},{9,1},{17,25},{25,17},{2,10},{10... | collective-permute-start | bytes 393224 | tf_op jit(solution)/shard_map/ppermute | solution.py:244
  63.8 1.4 %copy-start.8 = (s32[4096]{0:T(1024)S(1)}, s32[4096]{0:T(1024)}, u32[]{:S(2)}) copy-start(s32[4096]{0:T(1024)} %param.14) | copy-start | bytes 49156
  63.9 1.3 %collective-permute-start.20 = (bf16[4,64,128]{2,1,0:T(8,128)(2,1)S(1)}, bf16[4,64,128]{2,1,0:T(8,128)(2,1)S(1)}, u32[]{:S(2)}, u32[]{:S(2)}) collective-permute-start(bf16[4,64,128]{2,1,0:T(8,128)(2,1)S(1)} %pad_maximum_fusion.1.near), channel_id=1, source_target_pairs={{0,1},{1,0},{2,3},{3,2},{4,5},{5,4},{6,7},{7,6},{8,9},{9,8},{10,11... | collective-permute-start | bytes 196616 | tf_op jit(solution)/shard_map/ppermute | solution.py:244

commit v2 on v1

--- a/solution.py
+++ b/solution.py
@@ -45,7 +45,7 @@
     def _():
         me = lax.axis_index("shard")
         for k in range(keep_ref.shape[0]):
-            mine = me ^ (2 * k)
+            mine = me ^ other_chip(k)
             keep_ref[k] = acc_ref[pl.ds(pl.multiple_of(mine * t_rows, t_rows), t_rows), :]
             other = mine ^ 1
             give_ref[k] = acc_ref[
@@ -92,9 +92,9 @@
     core = lax.rem(me, 2)
     pair = lax.div(me, 2)
     for k in range(pairs):
-        base = (pair ^ k) * (2 * rows)
-        weight[pl.ds(pl.multiple_of(base + core * rows, rows), rows), :] = near[k]
-        weight[pl.ds(pl.multiple_of(base + (1 - core) * rows, rows), rows), :] = far[k]
+        mine = me ^ other_chip(k)
+        weight[pl.ds(pl.multiple_of(mine * rows, rows), rows), :] = near[k]
+        weight[pl.ds(pl.multiple_of((mine ^ 1) * rows, rows), rows), :] = far[k]
     pooled = jnp.concatenate([r[:, :channels] for r in pooled_refs], axis=0)
     pooled_grad = jnp.concatenate([r[:, channels:] for r in pooled_refs], axis=0)
     step = 512
@@ -145,8 +145,9 @@
     for k in range(pairs):
         chunk = pl.ds(pl.multiple_of((pair ^ k) * (2 * rows), 2 * rows), 2 * rows)
         term[...] = contract(hid[:, chunk], q_grad, 0, 0)
-        keep_ref[k] = term[pl.ds(pl.multiple_of(core * rows, rows), rows), :].astype(BF16)
-        give_ref[k] = term[pl.ds(pl.multiple_of((1 - core) * rows, rows), rows), :].astype(BF16)
+        mine = core ^ 1 if k else core
+        keep_ref[k] = term[pl.ds(pl.multiple_of(mine * rows, rows), rows), :].astype(BF16)
+        give_ref[k] = term[pl.ds(pl.multiple_of((1 - mine) * rows, rows), rows), :].astype(BF16)
 
 
 def attend(tok, pooled, near, far, w_in, w_out):
@@ -179,7 +180,7 @@
     def _():
         me = lax.axis_index("shard")
         for k in range(pairs):
-            mine = me ^ (2 * k)
+            mine = me ^ other_chip(k)
             rows_ref[pl.ds(pl.multiple_of(mine * t_rows, t_rows), t_rows), :] = near[k]
             rows_ref[pl.ds(pl.multiple_of((mine ^ 1) * t_rows, t_rows), t_rows), :] = far[k]
 
@@ -239,9 +240,15 @@
     )(*pieces)
 
 
-def swap(x, axis, k):
-    n = lax.axis_size(axis)
-    return lax.ppermute(x, axis, [(i, i ^ k) for i in range(n)])
+def swap(x, group, shard):
+    n = lax.axis_size("shard")
+    flip = group * n + shard
+    pairs = [(i, i ^ flip) for i in range(lax.axis_size("group") * n)]
+    return lax.ppermute(x, ("group", "shard"), pairs)
+
+
+def other_chip(k):
+    return 2 * k + 1 if k else 0
 
 
 def local(tokens, w_qk, w_in, w_out, particles, cotangent, clusters, owners):
@@ -253,43 +260,45 @@
     part = lax.rem(lax.axis_index("group"), parts)
 
     w_own = lax.dynamic_slice_in_dim(w_qk, part * cols, cols, axis=1)
-    near = [w_own] + [swap(w_own, "shard", 2 * k) for k in range(1, pairs)]
-    tok = [tokens] + [swap(tokens, "group", k) for k in range(1, parts)]
+    near = [w_own] + [swap(w_own, 0, other_chip(k)) for k in range(1, pairs)]
+    tok = [tokens] + [swap(tokens, k, 1) for k in range(1, parts)]
+    owners, near[1] = lax.optimization_barrier((owners, near[1]))
     near = jnp.stack(near)
-    far = swap(near, "shard", 1)
+    far = swap(near, 0, 1)
 
     keep, give = pool(particles, cotangent, clusters, owners, t_rows, n_shard)
-    joined = keep + swap(give, "shard", 1).astype(F32)
+    joined = keep + swap(give, 0, 1).astype(F32)
     sums = joined[0]
     for k in range(1, pairs):
-        sums = sums + swap(joined[k].astype(BF16), "shard", 2 * k).astype(F32)
+        sums = sums + swap(joined[k].astype(BF16), 0, other_chip(k)).astype(F32)
     channels = particles.shape[1]
     counts = jnp.sum(sums[:, 2 * channels :], axis=1, keepdims=True)
     pooled = jnp.concatenate(
         [sums[:, :channels] / jnp.maximum(counts, 1.0), sums[:, channels : 2 * channels]], axis=1
     ).astype(BF16)
-    pooled = [pooled] + [swap(pooled, "group", k) for k in range(1, parts)]
+    pooled = [pooled] + [swap(pooled, k, 1) for k in range(1, parts)]
 
     up, keep, give = attend(tok, pooled, near, far, w_in, w_out)
 
-    joined = keep.astype(F32) + swap(give, "shard", 1).astype(F32)
+    joined = keep.astype(F32) + swap(give, 0, 1).astype(F32)
+    up, joined = lax.optimization_barrier((up, joined))
     unpooled = up[0].astype(F32)
     for k in range(1, parts):
-        unpooled = unpooled + swap(up[k], "group", k).astype(F32)
+        unpooled = unpooled + swap(up[k], k, 1).astype(F32)
     unpooled = unpooled.astype(BF16)
-    near = jnp.stack([unpooled] + [swap(unpooled, "shard", 2 * k) for k in range(1, pairs)])
-    far = swap(near, "shard", 1)
+    near = jnp.stack([unpooled] + [swap(unpooled, 0, other_chip(k)) for k in range(1, pairs)])
+    far = swap(near, 0, 1)
     particle_out = unpool(particles, clusters, owners, near, far)
 
     grad = joined[0]
     for k in range(1, pairs):
-        grad = grad + swap(joined[k].astype(BF16), "shard", 2 * k).astype(F32)
+        grad = grad + swap(joined[k].astype(BF16), 0, other_chip(k)).astype(F32)
     if n_group > parts:
         part_sum = grad.astype(BF16)
         for k in range(1, n_group // parts):
-            grad = grad + swap(part_sum, "group", k * parts).astype(F32)
+            grad = grad + swap(part_sum, k * parts, 0).astype(F32)
     grad = grad.astype(BF16)
-    qk_grad = spread([grad] + [swap(grad, "group", k) for k in range(1, parts)])
+    qk_grad = spread([grad] + [swap(grad, k, 0) for k in range(1, parts)])
     return (particle_out, qk_grad)
 
 

time: 69.7 us -> 77.8 us (1.12)
  waiting for transfers between devices: 15.7 us -> 28.3 us
  starting transfers between devices: 39.4 us -> 35.4 us
    ppermute x28, waiting for transfers between devices: 15.7 us -> 28.3 us  [swap(): return lax.ppermute(x, ('group', 'shard'), pairs)]
    ppermute x28, starting transfers between devices: 39.4 us -> 35.4 us  [swap(): return lax.ppermute(x, ('group', 'shard'), pairs)]
    unnamed x20 -> x18, local copies, waits for them, and re-layouts: 3.91 us -> 3.51 us
  transfers between devices with their start and end apart: 28 -> 28, of which waited for: 10 -> 12; matrix products, arithmetic and copies ran while one was open for 1% -> 1% of each run, Pallas kernels for 4% -> 4%
where the time goes in v2:
time: 77.8 us; the launch traced here: 77.6 us
  starting transfers between devices  35.4 us (46%)
  waiting for transfers between devices  28.3 us (36%)
  Pallas kernels  8.76 us (11%)
  local copies, waits for them, and re-layouts  3.6 us (5%)
  between operations  0.87 us (1%)
    ppermute x28, starting transfers between devices, swap(): return lax.ppermute(x, ('group', 'shard'), pairs)  35.4 us
    ppermute x28, waiting for transfers between devices, swap(): return lax.ppermute(x, ('group', 'shard'), pairs)  28.3 us
    unnamed x18, local copies, waits for them, and re-layouts  3.51 us
    pallas_call x1, Pallas kernels, attend(): pl.pallas_call(functools.partial(attend_kernel, parts), in_specs=[VMEM] *...  3.24 us
    pallas_call x1, Pallas kernels, unpool(): pl.pallas_call(unpool_kernel, grid_spec=pltpu.PrefetchScalarGridSpec(num_...  2.82 us
    pallas_call x1, Pallas kernels, pool(): pl.pallas_call(functools.partial(pool_kernel, t_rows), grid_spec=pltpu.Pr...  1.64 us
  transfers between devices with their start and end apart: 28, of which 12 were waited for; matrix products, arithmetic and copies ran while one was open for 1% of the time, Pallas kernels for 4%

profile of v2, /device:TPU:0, one launch (start us, length us, event | category | flops | bytes accessed | tf_op | source)
XLA Modules:
  0.0 77.6 jit_solution(937416292710140202)
XLA Ops:
  0.7 1.0 %copy-done = bf16[256,1024]{1,0:T(8,128)(2,1)S(1)} copy-done((bf16[256,1024]{1,0:T(8,128)(2,1)S(1)}, bf16[256,1024]{1,0:T(8,128)(2,1)}, u32[]{:S(2)}) %copy-start) | copy-done | bytes 524312
  1.7 2.5 %collective-permute-start = (bf16[256,256]{1,0:T(8,128)(2,1)S(1)}, bf16[256,256]{1,0:T(8,128)(2,1)S(1)}, u32[]{:S(2)}, u32[]{:S(2)}) collective-permute-start(bf16[256,256]{1,0:T(8,128)(2,1)S(1)} %constant_dynamic-slice_fusion), channel_id=1, source_target_pairs={{0,3},{1,2},{2,1},{3,0},{4,7},{5,6},{6,5},{7,4},{8,11},{9,10},{10,... | collective-permute-start | bytes 393224 | tf_op jit(solution)/shard_map/ppermute | solution.py:247
  4.2 3.9 %collective-permute-done = bf16[256,256]{1,0:T(8,128)(2,1)S(1)} collective-permute-done((bf16[256,256]{1,0:T(8,128)(2,1)S(1)}, bf16[256,256]{1,0:T(8,128)(2,1)S(1)}, u32[]{:S(2)}, u32[]{:S(2)}) %collective-permute-start) | collective-permute-done | bytes 131104 | tf_op jit(solution)/shard_map/ppermute | solution.py:247
  8.1 1.2 %copy-done.1 = bf16[4096,128]{1,0:T(8,128)(2,1)S(1)} copy-done((bf16[4096,128]{1,0:T(8,128)(2,1)S(1)}, bf16[4096,128]{1,0:T(8,128)(2,1)}, u32[]{:S(2)}) %copy-start.1) | copy-done | bytes 1048600
  9.4 1.2 %copy-done.3 = bf16[4096,128]{1,0:T(8,128)(2,1)S(1)} copy-done((bf16[4096,128]{1,0:T(8,128)(2,1)S(1)}, bf16[4096,128]{1,0:T(8,128)(2,1)}, u32[]{:S(2)}) %copy-start.3) | copy-done | bytes 1048600
  10.6 1.6 %pool.1 = (f32[4,64,384]{2,1,0:T(8,128)S(1)}, bf16[4,64,384]{2,1,0:T(8,128)(2,1)S(1)}) custom-call(s32[32]{0:T(128)S(1)} %copy-done.8, s32[32,128]{1,0:T(8,128)S(1)} %bitcast.47, bf16[4096,128]{1,0:T(8,128)(2,1)S(1)} %copy-done.1, bf16[4096,128]{1,0:T(8,128)(2,1)S(1)} %copy-done.3), custom_call_target="tpu_custom_call" | custom-call | tf_op jit(solution)/shard_map/pool/pallas_call | solution.py:63
  12.2 0.2 collective-permute-start.4
  12.4 3.4 %collective-permute-start.11 = (bf16[256,256]{1,0:T(8,128)(2,1)S(1)}, bf16[256,256]{1,0:T(8,128)(2,1)S(1)}, u32[]{:S(2)}, u32[]{:S(2)}) collective-permute-start(bf16[256,256]{1,0:T(8,128)(2,1)S(1)} %constant_dynamic-slice_fusion), channel_id=1, source_target_pairs={{0,5},{1,4},{2,7},{3,6},{4,1},{5,0},{6,3},{7,2},{8,13},{9,12},{10,... | collective-permute-start | bytes 393224 | tf_op jit(solution)/shard_map/ppermute | solution.py:247
  15.8 1.2 %collective-permute-start.12 = (bf16[256,256]{1,0:T(8,128)(2,1)S(1)}, bf16[256,256]{1,0:T(8,128)(2,1)S(1)}, u32[]{:S(2)}, u32[]{:S(2)}) collective-permute-start(bf16[256,256]{1,0:T(8,128)(2,1)S(1)} %constant_dynamic-slice_fusion), channel_id=1, source_target_pairs={{0,7},{1,6},{2,5},{3,4},{4,3},{5,2},{6,1},{7,0},{8,15},{9,14},{10,... | collective-permute-start | bytes 393224 | tf_op jit(solution)/shard_map/ppermute | solution.py:247
  17.0 1.5 %collective-permute-start.2 = (bf16[64,2048]{1,0:T(8,128)(2,1)S(1)}, bf16[64,2048]{1,0:T(8,128)(2,1)S(1)}, u32[]{:S(2)}, u32[]{:S(2)}) collective-permute-start(bf16[64,2048]{1,0:T(8,128)(2,1)S(1)} %copy-done.6), channel_id=1, source_target_pairs={{0,17},{1,16},{2,19},{3,18},{4,21},{5,20},{6,23},{7,22},{8,25},{9,... | collective-permute-start | bytes 786440 | tf_op jit(solution)/shard_map/ppermute | solution.py:247
  18.5 1.3 %collective-permute-start.1 = (bf16[64,2048]{1,0:T(8,128)(2,1)S(1)}, bf16[64,2048]{1,0:T(8,128)(2,1)S(1)}, u32[]{:S(2)}, u32[]{:S(2)}) collective-permute-start(bf16[64,2048]{1,0:T(8,128)(2,1)S(1)} %copy-done.6), channel_id=1, source_target_pairs={{0,9},{1,8},{2,11},{3,10},{4,13},{5,12},{6,15},{7,14},{8,1},{9,0},... | collective-permute-start | bytes 786440 | tf_op jit(solution)/shard_map/ppermute | solution.py:247
  19.9 0.3 collective-permute-start.5
  20.2 5.1 %collective-permute-done.11 = bf16[256,256]{1,0:T(8,128)(2,1)S(1)} collective-permute-done((bf16[256,256]{1,0:T(8,128)(2,1)S(1)}, bf16[256,256]{1,0:T(8,128)(2,1)S(1)}, u32[]{:S(2)}, u32[]{:S(2)}) %collective-permute-start.11) | collective-permute-done | bytes 131104 | tf_op jit(solution)/shard_map/ppermute | solution.py:247
  25.2 3.5 %collective-permute-start.7 = (bf16[64,384]{1,0:T(8,128)(2,1)S(1)}, bf16[64,384]{1,0:T(8,128)(2,1)S(1)}, u32[]{:S(2)}, u32[]{:S(2)}) collective-permute-start(bf16[64,384]{1,0:T(8,128)(2,1)S(1)} %get-tuple-element.26), channel_id=1, source_target_pairs={{0,7},{1,6},{2,5},{3,4},{4,3},{5,2},{6,1},{7,0},{8,15},{9,14},{10,... | collective-permute-start | bytes 147464 | tf_op jit(solution)/shard_map/ppermute | solution.py:247
  28.7 2.0 %collective-permute-start.6 = (bf16[64,384]{1,0:T(8,128)(2,1)S(1)}, bf16[64,384]{1,0:T(8,128)(2,1)S(1)}, u32[]{:S(2)}, u32[]{:S(2)}) collective-permute-start(bf16[64,384]{1,0:T(8,128)(2,1)S(1)} %get-tuple-element.27), channel_id=1, source_target_pairs={{0,5},{1,4},{2,7},{3,6},{4,1},{5,0},{6,3},{7,2},{8,13},{9,12},{10,... | collective-permute-start | bytes 147464 | tf_op jit(solution)/shard_map/ppermute | solution.py:247
  30.8 2.4 %collective-permute-start.3 = (bf16[64,2048]{1,0:T(8,128)(2,1)S(1)}, bf16[64,2048]{1,0:T(8,128)(2,1)S(1)}, u32[]{:S(2)}, u32[]{:S(2)}) collective-permute-start(bf16[64,2048]{1,0:T(8,128)(2,1)S(1)} %copy-done.6), channel_id=1, source_target_pairs={{0,25},{1,24},{2,27},{3,26},{4,29},{5,28},{6,31},{7,30},{8,17},{9,... | collective-permute-start | bytes 786440 | tf_op jit(solution)/shard_map/ppermute | solution.py:247
  33.2 0.2 collective-permute-start.13
  33.4 1.0 %collective-permute-done.6 = bf16[64,384]{1,0:T(8,128)(2,1)S(1)} collective-permute-done((bf16[64,384]{1,0:T(8,128)(2,1)S(1)}, bf16[64,384]{1,0:T(8,128)(2,1)S(1)}, u32[]{:S(2)}, u32[]{:S(2)}) %collective-permute-start.6) | collective-permute-done | bytes 49184 | tf_op jit(solution)/shard_map/ppermute | solution.py:247
  34.5 0.1 slice_reduce_fusion
  34.6 0.1 fusion.6
  34.7 2.2 %collective-permute-start.10 = (bf16[64,256]{1,0:T(8,128)(2,1)S(1)}, bf16[64,256]{1,0:T(8,128)(2,1)S(1)}, u32[]{:S(2)}, u32[]{:S(2)}) collective-permute-start(bf16[64,256]{1,0:T(8,128)(2,1)S(1)} %pad_maximum_fusion.2.refs_4_), channel_id=1, source_target_pairs={{0,25},{1,24},{2,27},{3,26},{4,29},{5,28},{6,31},{7,30},{8,17},{9,... | collective-permute-start | bytes 98312 | tf_op jit(solution)/shard_map/ppermute | solution.py:247
  36.9 0.5 collective-permute-start.9
  37.5 0.3 collective-permute-start.8
  37.7 2.3 %collective-permute-done.3.refs_3_ = bf16[64,2048]{1,0:T(8,128)(2,1)S(1)} collective-permute-done((bf16[64,2048]{1,0:T(8,128)(2,1)S(1)}, bf16[64,2048]{1,0:T(8,128)(2,1)S(1)}, u32[]{:S(2)}, u32[]{:S(2)}) %collective-permute-start.3) | collective-permute-done | bytes 262176 | tf_op jit(solution)/shard_map/ppermute | solution.py:247
  40.0 0.8 %collective-permute-done.10.refs_7_ = bf16[64,256]{1,0:T(8,128)(2,1)S(1)} collective-permute-done((bf16[64,256]{1,0:T(8,128)(2,1)S(1)}, bf16[64,256]{1,0:T(8,128)(2,1)S(1)}, u32[]{:S(2)}, u32[]{:S(2)}) %collective-permute-start.10) | collective-permute-done | bytes 32800 | tf_op jit(solution)/shard_map/ppermute | solution.py:247
  40.8 1.0 %collective-permute-done.9.refs_6_ = bf16[64,256]{1,0:T(8,128)(2,1)S(1)} collective-permute-done((bf16[64,256]{1,0:T(8,128)(2,1)S(1)}, bf16[64,256]{1,0:T(8,128)(2,1)S(1)}, u32[]{:S(2)}, u32[]{:S(2)}) %collective-permute-start.9) | collective-permute-done | bytes 32800 | tf_op jit(solution)/shard_map/ppermute | solution.py:247
  41.8 3.2 %attend.1 = (bf16[4,64,128]{2,1,0:T(8,128)(2,1)S(1)}, bf16[4,256,256]{2,1,0:T(8,128)(2,1)S(1)}, bf16[4,256,256]{2,1,0:T(8,128)(2,1)S(1)}) custom-call(bf16[64,2048]{1,0:T(8,128)(2,1)S(1)} %copy-done.6, bf16[64,2048]{1,0:T(8,128)(2,1)S(1)} %collective-permute-done.1.refs_1_, bf16[64,2048]{1,0:T(8,128)(2,1)S(1)} %collective-permute-done.2.refs_2_, ...), custom_call_target="tpu_custom_call" | custom-call | tf_op jit(solution)/shard_map/attend/pallas_call | solution.py:159
  45.0 0.2 collective-permute-start.14
  45.2 1.8 %collective-permute-done.14 = bf16[4,256,256]{2,1,0:T(8,128)(2,1)S(1)} collective-permute-done((bf16[4,256,256]{2,1,0:T(8,128)(2,1)S(1)}, bf16[4,256,256]{2,1,0:T(8,128)(2,1)S(1)}, u32[]{:S(2)}, u32[]{:S(2)}) %collective-permute-start.14) | collective-permute-done | bytes 524320 | tf_op jit(solution)/shard_map/ppermute | solution.py:247
  47.0 0.1 convert_add_fusion
  47.1 1.3 %collective-permute-start.15 = (bf16[64,128]{1,0:T(8,128)(2,1)S(1)}, bf16[64,128]{1,0:T(8,128)(2,1)S(1)}, u32[]{:S(2)}, u32[]{:S(2)}) collective-permute-start(bf16[64,128]{1,0:T(8,128)(2,1)S(1)} %get-tuple-element.28), channel_id=1, source_target_pairs={{0,9},{1,8},{2,11},{3,10},{4,13},{5,12},{6,15},{7,14},{8,1},{9,0},... | collective-permute-start | bytes 49160 | tf_op jit(solution)/shard_map/ppermute | solution.py:247
  48.4 1.5 %collective-permute-start.17 = (bf16[64,128]{1,0:T(8,128)(2,1)S(1)}, bf16[64,128]{1,0:T(8,128)(2,1)S(1)}, u32[]{:S(2)}, u32[]{:S(2)}) collective-permute-start(bf16[64,128]{1,0:T(8,128)(2,1)S(1)} %get-tuple-element.29), channel_id=1, source_target_pairs={{0,25},{1,24},{2,27},{3,26},{4,29},{5,28},{6,31},{7,30},{8,17},{9,... | collective-permute-start | bytes 49160 | tf_op jit(solution)/shard_map/ppermute | solution.py:247
  49.9 0.3 collective-permute-start.16
  50.3 2.2 %collective-permute-start.24 = (bf16[256,256]{1,0:T(8,128)(2,1)S(1)}, bf16[256,256]{1,0:T(8,128)(2,1)S(1)}, u32[]{:S(2)}, u32[]{:S(2)}) collective-permute-start(bf16[256,256]{1,0:T(8,128)(2,1)S(1)} %get-tuple-element.23), channel_id=1, source_target_pairs={{0,7},{1,6},{2,5},{3,4},{4,3},{5,2},{6,1},{7,0},{8,15},{9,14},{10,... | collective-permute-start | bytes 393224 | tf_op jit(solution)/shard_map/ppermute | solution.py:247
  52.5 1.0 %collective-permute-start.23 = (bf16[256,256]{1,0:T(8,128)(2,1)S(1)}, bf16[256,256]{1,0:T(8,128)(2,1)S(1)}, u32[]{:S(2)}, u32[]{:S(2)}) collective-permute-start(bf16[256,256]{1,0:T(8,128)(2,1)S(1)} %get-tuple-element.24), channel_id=1, source_target_pairs={{0,5},{1,4},{2,7},{3,6},{4,1},{5,0},{6,3},{7,2},{8,13},{9,12},{10,... | collective-permute-start | bytes 393224 | tf_op jit(solution)/shard_map/ppermute | solution.py:247
  53.5 1.0 %collective-permute-start.20 = (bf16[64,128]{1,0:T(8,128)(2,1)S(1)}, bf16[64,128]{1,0:T(8,128)(2,1)S(1)}, u32[]{:S(2)}, u32[]{:S(2)}) collective-permute-start(bf16[64,128]{1,0:T(8,128)(2,1)S(1)} %fusion.9), channel_id=1, source_target_pairs={{0,7},{1,6},{2,5},{3,4},{4,3},{5,2},{6,1},{7,0},{8,15},{9,14},{10,... | collective-permute-start | bytes 49160 | tf_op jit(solution)/shard_map/ppermute | solution.py:247
  54.5 1.3 %collective-permute-start.19 = (bf16[64,128]{1,0:T(8,128)(2,1)S(1)}, bf16[64,128]{1,0:T(8,128)(2,1)S(1)}, u32[]{:S(2)}, u32[]{:S(2)}) collective-permute-start(bf16[64,128]{1,0:T(8,128)(2,1)S(1)} %fusion.9), channel_id=1, source_target_pairs={{0,5},{1,4},{2,7},{3,6},{4,1},{5,0},{6,3},{7,2},{8,13},{9,12},{10,... | collective-permute-start | bytes 49160 | tf_op jit(solution)/shard_map/ppermute | solution.py:247
  55.8 1.7 %collective-permute-start.18 = (bf16[64,128]{1,0:T(8,128)(2,1)S(1)}, bf16[64,128]{1,0:T(8,128)(2,1)S(1)}, u32[]{:S(2)}, u32[]{:S(2)}) collective-permute-start(bf16[64,128]{1,0:T(8,128)(2,1)S(1)} %fusion.9), channel_id=1, source_target_pairs={{0,3},{1,2},{2,1},{3,0},{4,7},{5,6},{6,5},{7,4},{8,11},{9,10},{10,... | collective-permute-start | bytes 49160 | tf_op jit(solution)/shard_map/ppermute | solution.py:247
  57.5 1.6 %collective-permute-done.24 = bf16[256,256]{1,0:T(8,128)(2,1)S(1)} collective-permute-done((bf16[256,256]{1,0:T(8,128)(2,1)S(1)}, bf16[256,256]{1,0:T(8,128)(2,1)S(1)}, u32[]{:S(2)}, u32[]{:S(2)}) %collective-permute-start.24) | collective-permute-done | bytes 131104 | tf_op jit(solution)/shard_map/ppermute | solution.py:247
  59.1 7.3 %collective-permute-done.23 = bf16[256,256]{1,0:T(8,128)(2,1)S(1)} collective-permute-done((bf16[256,256]{1,0:T(8,128)(2,1)S(1)}, bf16[256,256]{1,0:T(8,128)(2,1)S(1)}, u32[]{:S(2)}, u32[]{:S(2)}) %collective-permute-start.23) | collective-permute-done | bytes 131104 | tf_op jit(solution)/shard_map/ppermute | solution.py:247
  66.4 2.5 %collective-permute-start.27 = (bf16[256,256]{1,0:T(8,128)(2,1)S(1)}, bf16[256,256]{1,0:T(8,128)(2,1)S(1)}, u32[]{:S(2)}, u32[]{:S(2)}) collective-permute-start(bf16[256,256]{1,0:T(8,128)(2,1)S(1)} %fusion.2.refs_0_), channel_id=1, source_target_pairs={{0,24},{1,25},{2,26},{3,27},{4,28},{5,29},{6,30},{7,31},{8,16},{9,... | collective-permute-start | bytes 393224 | tf_op jit(solution)/shard_map/ppermute | solution.py:247
  68.9 0.5 collective-permute-start.26
  69.4 0.6 collective-permute-start.25
  70.1 1.2 %collective-permute-done.21.far = bf16[4,64,128]{2,1,0:T(8,128)(2,1)S(1)} collective-permute-done((bf16[4,64,128]{2,1,0:T(8,128)(2,1)S(1)}, bf16[4,64,128]{2,1,0:T(8,128)(2,1)S(1)}, u32[]{:S(2)}, u32[]{:S(2)}) %collective-permute-start.21) | collective-permute-done | bytes 65568 | tf_op jit(solution)/shard_map/ppermute | solution.py:247
  71.3 2.8 %unpool.1 = bf16[4096,128]{1,0:T(8,128)(2,1)} custom-call(s32[32]{0:T(128)S(1)} %copy-done.8, s32[32,128]{1,0:T(8,128)S(1)} %bitcast.48, bf16[4096,128]{1,0:T(8,128)(2,1)S(1)} %copy-done.2, bf16[4,64,128]{2,1,0:T(8,128)(2,1)S(1)} %pad_maximum_fusion.1.near, bf16[4,64,128]{2,1,0:T(8,128)(2,1)S(1)} %collective-permute-done.21.far), custom_call_target="tpu_custom_call" | custom-call | tf_op jit(solution)/shard_map/unpool/pallas_call | solution.py:203
  74.1 2.2 %collective-permute-done.26.refs_2_ = bf16[256,256]{1,0:T(8,128)(2,1)S(1)} collective-permute-done((bf16[256,256]{1,0:T(8,128)(2,1)S(1)}, bf16[256,256]{1,0:T(8,128)(2,1)S(1)}, u32[]{:S(2)}, u32[]{:S(2)}) %collective-permute-start.26) | collective-permute-done | bytes 131104 | tf_op jit(solution)/shard_map/ppermute | solution.py:247
  76.4 0.1 collective-permute-done.25.refs_1_
  76.5 1.1 %spread.1 = f32[256,1024]{1,0:T(8,128)} custom-call(bf16[256,256]{1,0:T(8,128)(2,1)S(1)} %fusion.2.refs_0_, bf16[256,256]{1,0:T(8,128)(2,1)S(1)} %collective-permute-done.25.refs_1_, bf16[256,256]{1,0:T(8,128)(2,1)S(1)} %collective-permute-done.26.refs_2_, bf16[256,256]{1,0:T(8,128)(2,1)S(1)} %collective-permute-done.27.refs_3_), custom_call_target="tpu_custom_call" | custom-call | tf_op jit(solution)/shard_map/spread/pallas_call | solution.py:233
  (48 shorter events, 0.6 us)
Async XLA Ops:
  0.6 1.0 %copy-start = (bf16[256,1024]{1,0:T(8,128)(2,1)S(1)}, bf16[256,1024]{1,0:T(8,128)(2,1)}, u32[]{:S(2)}) copy-start(bf16[256,1024]{1,0:T(8,128)(2,1)} %param.9) | copy-start | bytes 1572868
  1.7 6.5 %copy-start.7 = (s32[4096]{0:T(1024)S(1)}, s32[4096]{0:T(1024)}, u32[]{:S(2)}) copy-start(s32[4096]{0:T(1024)} %param.14) | copy-start | bytes 49156
  1.7 6.4 %copy-start.8 = (s32[32]{0:T(128)S(1)}, s32[32]{0:T(128)}, u32[]{:S(2)}) copy-start(s32[32]{0:T(128)} %owners_ref.1) | copy-start | bytes 388
  1.7 6.4 %collective-permute-start = (bf16[256,256]{1,0:T(8,128)(2,1)S(1)}, bf16[256,256]{1,0:T(8,128)(2,1)S(1)}, u32[]{:S(2)}, u32[]{:S(2)}) collective-permute-start(bf16[256,256]{1,0:T(8,128)(2,1)S(1)} %constant_dynamic-slice_fusion), channel_id=1, source_target_pairs={{0,3},{1,2},{2,1},{3,0},{4,7},{5,6},{6,5},{7,4},{8,11},{9,10},{10,... | collective-permute-start | bytes 393224 | tf_op jit(solution)/shard_map/ppermute | solution.py:247
  8.1 1.2 %copy-start.1 = (bf16[4096,128]{1,0:T(8,128)(2,1)S(1)}, bf16[4096,128]{1,0:T(8,128)(2,1)}, u32[]{:S(2)}) copy-start(bf16[4096,128]{1,0:T(8,128)(2,1)} %feat_ref.3) | copy-start | bytes 3145732
  9.4 1.2 %copy-start.3 = (bf16[4096,128]{1,0:T(8,128)(2,1)S(1)}, bf16[4096,128]{1,0:T(8,128)(2,1)}, u32[]{:S(2)}) copy-start(bf16[4096,128]{1,0:T(8,128)(2,1)} %grad_ref.1) | copy-start | bytes 3145732
  10.6 6.4 %copy-start.6 = (bf16[64,2048]{1,0:T(8,128)(2,1)S(1)}, bf16[64,2048]{1,0:T(8,128)(2,1)}, u32[]{:S(2)}) copy-start(bf16[64,2048]{1,0:T(8,128)(2,1)} %refs_0_.1) | copy-start | bytes 786436
  12.2 7.5 %collective-permute-start.4 = (bf16[4,64,384]{2,1,0:T(8,128)(2,1)S(1)}, bf16[4,64,384]{2,1,0:T(8,128)(2,1)S(1)}, u32[]{:S(2)}, u32[]{:S(2)}) collective-permute-start(bf16[4,64,384]{2,1,0:T(8,128)(2,1)S(1)} %get-tuple-element.13), channel_id=1, source_target_pairs={{0,1},{1,0},{2,3},{3,2},{4,5},{5,4},{6,7},{7,6},{8,9},{9,8},{10,11... | collective-permute-start | bytes 589832 | tf_op jit(solution)/shard_map/ppermute | solution.py:247
  12.4 12.8 %collective-permute-start.11 = (bf16[256,256]{1,0:T(8,128)(2,1)S(1)}, bf16[256,256]{1,0:T(8,128)(2,1)S(1)}, u32[]{:S(2)}, u32[]{:S(2)}) collective-permute-start(bf16[256,256]{1,0:T(8,128)(2,1)S(1)} %constant_dynamic-slice_fusion), channel_id=1, source_target_pairs={{0,5},{1,4},{2,7},{3,6},{4,1},{5,0},{6,3},{7,2},{8,13},{9,12},{10,... | collective-permute-start | bytes 393224 | tf_op jit(solution)/shard_map/ppermute | solution.py:247
  15.8 13.0 %collective-permute-start.12 = (bf16[256,256]{1,0:T(8,128)(2,1)S(1)}, bf16[256,256]{1,0:T(8,128)(2,1)S(1)}, u32[]{:S(2)}, u32[]{:S(2)}) collective-permute-start(bf16[256,256]{1,0:T(8,128)(2,1)S(1)} %constant_dynamic-slice_fusion), channel_id=1, source_target_pairs={{0,7},{1,6},{2,5},{3,4},{4,3},{5,2},{6,1},{7,0},{8,15},{9,14},{10,... | collective-permute-start | bytes 393224 | tf_op jit(solution)/shard_map/ppermute | solution.py:247
  17.0 20.0 %collective-permute-start.2 = (bf16[64,2048]{1,0:T(8,128)(2,1)S(1)}, bf16[64,2048]{1,0:T(8,128)(2,1)S(1)}, u32[]{:S(2)}, u32[]{:S(2)}) collective-permute-start(bf16[64,2048]{1,0:T(8,128)(2,1)S(1)} %copy-done.6), channel_id=1, source_target_pairs={{0,17},{1,16},{2,19},{3,18},{4,21},{5,20},{6,23},{7,22},{8,25},{9,... | collective-permute-start | bytes 786440 | tf_op jit(solution)/shard_map/ppermute | solution.py:247
  18.5 19.0 %collective-permute-start.1 = (bf16[64,2048]{1,0:T(8,128)(2,1)S(1)}, bf16[64,2048]{1,0:T(8,128)(2,1)S(1)}, u32[]{:S(2)}, u32[]{:S(2)}) collective-permute-start(bf16[64,2048]{1,0:T(8,128)(2,1)S(1)} %copy-done.6), channel_id=1, source_target_pairs={{0,9},{1,8},{2,11},{3,10},{4,13},{5,12},{6,15},{7,14},{8,1},{9,0},... | collective-permute-start | bytes 786440 | tf_op jit(solution)/shard_map/ppermute | solution.py:247
  19.9 11.0 %collective-permute-start.5 = (bf16[64,384]{1,0:T(8,128)(2,1)S(1)}, bf16[64,384]{1,0:T(8,128)(2,1)S(1)}, u32[]{:S(2)}, u32[]{:S(2)}) collective-permute-start(bf16[64,384]{1,0:T(8,128)(2,1)S(1)} %get-tuple-element.25), channel_id=1, source_target_pairs={{0,3},{1,2},{2,1},{3,0},{4,7},{5,6},{6,5},{7,4},{8,11},{9,10},{10,... | collective-permute-start | bytes 147464 | tf_op jit(solution)/shard_map/ppermute | solution.py:247
  25.2 8.0 %collective-permute-start.7 = (bf16[64,384]{1,0:T(8,128)(2,1)S(1)}, bf16[64,384]{1,0:T(8,128)(2,1)S(1)}, u32[]{:S(2)}, u32[]{:S(2)}) collective-permute-start(bf16[64,384]{1,0:T(8,128)(2,1)S(1)} %get-tuple-element.26), channel_id=1, source_target_pairs={{0,7},{1,6},{2,5},{3,4},{4,3},{5,2},{6,1},{7,0},{8,15},{9,14},{10,... | collective-permute-start | bytes 147464 | tf_op jit(solution)/shard_map/ppermute | solution.py:247
  28.7 5.7 %collective-permute-start.6 = (bf16[64,384]{1,0:T(8,128)(2,1)S(1)}, bf16[64,384]{1,0:T(8,128)(2,1)S(1)}, u32[]{:S(2)}, u32[]{:S(2)}) collective-permute-start(bf16[64,384]{1,0:T(8,128)(2,1)S(1)} %get-tuple-element.27), channel_id=1, source_target_pairs={{0,5},{1,4},{2,7},{3,6},{4,1},{5,0},{6,3},{7,2},{8,13},{9,12},{10,... | collective-permute-start | bytes 147464 | tf_op jit(solution)/shard_map/ppermute | solution.py:247
  30.7 11.0 %copy-start.5 = (bf16[2048,128]{1,0:T(8,128)(2,1)S(1)}, bf16[2048,128]{1,0:T(8,128)(2,1)}, u32[]{:S(2)}) copy-start(bf16[2048,128]{1,0:T(8,128)(2,1)} %refs_11_.1) | copy-start | bytes 1572868
  30.8 11.0 %copy-start.4 = (bf16[128,2048]{1,0:T(8,128)(2,1)S(1)}, bf16[128,2048]{1,0:T(8,128)(2,1)}, u32[]{:S(2)}) copy-start(bf16[128,2048]{1,0:T(8,128)(2,1)} %refs_10_.1) | copy-start | bytes 1572868
  30.8 9.2 %collective-permute-start.3 = (bf16[64,2048]{1,0:T(8,128)(2,1)S(1)}, bf16[64,2048]{1,0:T(8,128)(2,1)S(1)}, u32[]{:S(2)}, u32[]{:S(2)}) collective-permute-start(bf16[64,2048]{1,0:T(8,128)(2,1)S(1)} %copy-done.6), channel_id=1, source_target_pairs={{0,25},{1,24},{2,27},{3,26},{4,29},{5,28},{6,31},{7,30},{8,17},{9,... | collective-permute-start | bytes 786440 | tf_op jit(solution)/shard_map/ppermute | solution.py:247
  33.2 8.5 %collective-permute-start.13 = (bf16[4,256,256]{2,1,0:T(8,128)(2,1)S(1)}, bf16[4,256,256]{2,1,0:T(8,128)(2,1)S(1)}, u32[]{:S(2)}, u32[]{:S(2)}) collective-permute-start(bf16[4,256,256]{2,1,0:T(8,128)(2,1)S(1)} %pad_maximum_fusion.refs_8_), channel_id=1, source_target_pairs={{0,1},{1,0},{2,3},{3,2},{4,5},{5,4},{6,7},{7,6},{8,9},{9,8},{10,11... | collective-permute-start | bytes 1572872 | tf_op jit(solution)/shard_map/ppermute | solution.py:247
  34.7 6.1 %collective-permute-start.10 = (bf16[64,256]{1,0:T(8,128)(2,1)S(1)}, bf16[64,256]{1,0:T(8,128)(2,1)S(1)}, u32[]{:S(2)}, u32[]{:S(2)}) collective-permute-start(bf16[64,256]{1,0:T(8,128)(2,1)S(1)} %pad_maximum_fusion.2.refs_4_), channel_id=1, source_target_pairs={{0,25},{1,24},{2,27},{3,26},{4,29},{5,28},{6,31},{7,30},{8,17},{9,... | collective-permute-start | bytes 98312 | tf_op jit(solution)/shard_map/ppermute | solution.py:247
  36.9 4.8 %collective-permute-start.9 = (bf16[64,256]{1,0:T(8,128)(2,1)S(1)}, bf16[64,256]{1,0:T(8,128)(2,1)S(1)}, u32[]{:S(2)}, u32[]{:S(2)}) collective-permute-start(bf16[64,256]{1,0:T(8,128)(2,1)S(1)} %pad_maximum_fusion.2.refs_4_), channel_id=1, source_target_pairs={{0,17},{1,16},{2,19},{3,18},{4,21},{5,20},{6,23},{7,22},{8,25},{9,... | collective-permute-start | bytes 98312 | tf_op jit(solution)/shard_map/ppermute | solution.py:247
  37.5 4.3 %collective-permute-start.8 = (bf16[64,256]{1,0:T(8,128)(2,1)S(1)}, bf16[64,256]{1,0:T(8,128)(2,1)S(1)}, u32[]{:S(2)}, u32[]{:S(2)}) collective-permute-start(bf16[64,256]{1,0:T(8,128)(2,1)S(1)} %pad_maximum_fusion.2.refs_4_), channel_id=1, source_target_pairs={{0,9},{1,8},{2,11},{3,10},{4,13},{5,12},{6,15},{7,14},{8,1},{9,0},... | collective-permute-start | bytes 98312 | tf_op jit(solution)/shard_map/ppermute | solution.py:247
  45.0 2.0 %collective-permute-start.14 = (bf16[4,256,256]{2,1,0:T(8,128)(2,1)S(1)}, bf16[4,256,256]{2,1,0:T(8,128)(2,1)S(1)}, u32[]{:S(2)}, u32[]{:S(2)}) collective-permute-start(bf16[4,256,256]{2,1,0:T(8,128)(2,1)S(1)} %get-tuple-element.17), channel_id=1, source_target_pairs={{0,1},{1,0},{2,3},{3,2},{4,5},{5,4},{6,7},{7,6},{8,9},{9,8},{10,11... | collective-permute-start | bytes 1572872 | tf_op jit(solution)/shard_map/ppermute | solution.py:247
  47.1 5.4 %collective-permute-start.15 = (bf16[64,128]{1,0:T(8,128)(2,1)S(1)}, bf16[64,128]{1,0:T(8,128)(2,1)S(1)}, u32[]{:S(2)}, u32[]{:S(2)}) collective-permute-start(bf16[64,128]{1,0:T(8,128)(2,1)S(1)} %get-tuple-element.28), channel_id=1, source_target_pairs={{0,9},{1,8},{2,11},{3,10},{4,13},{5,12},{6,15},{7,14},{8,1},{9,0},... | collective-permute-start | bytes 49160 | tf_op jit(solution)/shard_map/ppermute | solution.py:247
  48.4 5.1 %collective-permute-start.17 = (bf16[64,128]{1,0:T(8,128)(2,1)S(1)}, bf16[64,128]{1,0:T(8,128)(2,1)S(1)}, u32[]{:S(2)}, u32[]{:S(2)}) collective-permute-start(bf16[64,128]{1,0:T(8,128)(2,1)S(1)} %get-tuple-element.29), channel_id=1, source_target_pairs={{0,25},{1,24},{2,27},{3,26},{4,29},{5,28},{6,31},{7,30},{8,17},{9,... | collective-permute-start | bytes 49160 | tf_op jit(solution)/shard_map/ppermute | solution.py:247
  49.9 3.6 %collective-permute-start.16 = (bf16[64,128]{1,0:T(8,128)(2,1)S(1)}, bf16[64,128]{1,0:T(8,128)(2,1)S(1)}, u32[]{:S(2)}, u32[]{:S(2)}) collective-permute-start(bf16[64,128]{1,0:T(8,128)(2,1)S(1)} %get-tuple-element.30), channel_id=1, source_target_pairs={{0,17},{1,16},{2,19},{3,18},{4,21},{5,20},{6,23},{7,22},{8,25},{9,... | collective-permute-start | bytes 49160 | tf_op jit(solution)/shard_map/ppermute | solution.py:247
  50.2 21.1 %copy-start.2 = (bf16[4096,128]{1,0:T(8,128)(2,1)S(1)}, bf16[4096,128]{1,0:T(8,128)(2,1)}, u32[]{:S(2)}) copy-start(bf16[4096,128]{1,0:T(8,128)(2,1)} %feat_ref.3) | copy-start | bytes 3145732
  50.3 5.5 %collective-permute-start.22 = (bf16[256,256]{1,0:T(8,128)(2,1)S(1)}, bf16[256,256]{1,0:T(8,128)(2,1)S(1)}, u32[]{:S(2)}, u32[]{:S(2)}) collective-permute-start(bf16[256,256]{1,0:T(8,128)(2,1)S(1)} %get-tuple-element.22), channel_id=1, source_target_pairs={{0,3},{1,2},{2,1},{3,0},{4,7},{5,6},{6,5},{7,4},{8,11},{9,10},{10,... | collective-permute-start | bytes 393224 | tf_op jit(solution)/shard_map/ppermute | solution.py:247
  50.3 8.7 %collective-permute-start.24 = (bf16[256,256]{1,0:T(8,128)(2,1)S(1)}, bf16[256,256]{1,0:T(8,128)(2,1)S(1)}, u32[]{:S(2)}, u32[]{:S(2)}) collective-permute-start(bf16[256,256]{1,0:T(8,128)(2,1)S(1)} %get-tuple-element.23), channel_id=1, source_target_pairs={{0,7},{1,6},{2,5},{3,4},{4,3},{5,2},{6,1},{7,0},{8,15},{9,14},{10,... | collective-permute-start | bytes 393224 | tf_op jit(solution)/shard_map/ppermute | solution.py:247
  52.5 13.8 %collective-permute-start.23 = (bf16[256,256]{1,0:T(8,128)(2,1)S(1)}, bf16[256,256]{1,0:T(8,128)(2,1)S(1)}, u32[]{:S(2)}, u32[]{:S(2)}) collective-permute-start(bf16[256,256]{1,0:T(8,128)(2,1)S(1)} %get-tuple-element.24), channel_id=1, source_target_pairs={{0,5},{1,4},{2,7},{3,6},{4,1},{5,0},{6,3},{7,2},{8,13},{9,12},{10,... | collective-permute-start | bytes 393224 | tf_op jit(solution)/shard_map/ppermute | solution.py:247
  53.5 15.9 %collective-permute-start.20 = (bf16[64,128]{1,0:T(8,128)(2,1)S(1)}, bf16[64,128]{1,0:T(8,128)(2,1)S(1)}, u32[]{:S(2)}, u32[]{:S(2)}) collective-permute-start(bf16[64,128]{1,0:T(8,128)(2,1)S(1)} %fusion.9), channel_id=1, source_target_pairs={{0,7},{1,6},{2,5},{3,4},{4,3},{5,2},{6,1},{7,0},{8,15},{9,14},{10,... | collective-permute-start | bytes 49160 | tf_op jit(solution)/shard_map/ppermute | solution.py:247
  54.5 15.5 %collective-permute-start.19 = (bf16[64,128]{1,0:T(8,128)(2,1)S(1)}, bf16[64,128]{1,0:T(8,128)(2,1)S(1)}, u32[]{:S(2)}, u32[]{:S(2)}) collective-permute-start(bf16[64,128]{1,0:T(8,128)(2,1)S(1)} %fusion.9), channel_id=1, source_target_pairs={{0,5},{1,4},{2,7},{3,6},{4,1},{5,0},{6,3},{7,2},{8,13},{9,12},{10,... | collective-permute-start | bytes 49160 | tf_op jit(solution)/shard_map/ppermute | solution.py:247
  55.8 14.2 %collective-permute-start.18 = (bf16[64,128]{1,0:T(8,128)(2,1)S(1)}, bf16[64,128]{1,0:T(8,128)(2,1)S(1)}, u32[]{:S(2)}, u32[]{:S(2)}) collective-permute-start(bf16[64,128]{1,0:T(8,128)(2,1)S(1)} %fusion.9), channel_id=1, source_target_pairs={{0,3},{1,2},{2,1},{3,0},{4,7},{5,6},{6,5},{7,4},{8,11},{9,10},{10,... | collective-permute-start | bytes 49160 | tf_op jit(solution)/shard_map/ppermute | solution.py:247
  66.4 7.7 %collective-permute-start.27 = (bf16[256,256]{1,0:T(8,128)(2,1)S(1)}, bf16[256,256]{1,0:T(8,128)(2,1)S(1)}, u32[]{:S(2)}, u32[]{:S(2)}) collective-permute-start(bf16[256,256]{1,0:T(8,128)(2,1)S(1)} %fusion.2.refs_0_), channel_id=1, source_target_pairs={{0,24},{1,25},{2,26},{3,27},{4,28},{5,29},{6,30},{7,31},{8,16},{9,... | collective-permute-start | bytes 393224 | tf_op jit(solution)/shard_map/ppermute | solution.py:247
  68.9 7.5 %collective-permute-start.26 = (bf16[256,256]{1,0:T(8,128)(2,1)S(1)}, bf16[256,256]{1,0:T(8,128)(2,1)S(1)}, u32[]{:S(2)}, u32[]{:S(2)}) collective-permute-start(bf16[256,256]{1,0:T(8,128)(2,1)S(1)} %fusion.2.refs_0_), channel_id=1, source_target_pairs={{0,16},{1,17},{2,18},{3,19},{4,20},{5,21},{6,22},{7,23},{8,24},{9,... | collective-permute-start | bytes 393224 | tf_op jit(solution)/shard_map/ppermute | solution.py:247
  69.4 7.1 %collective-permute-start.25 = (bf16[256,256]{1,0:T(8,128)(2,1)S(1)}, bf16[256,256]{1,0:T(8,128)(2,1)S(1)}, u32[]{:S(2)}, u32[]{:S(2)}) collective-permute-start(bf16[256,256]{1,0:T(8,128)(2,1)S(1)} %fusion.2.refs_0_), channel_id=1, source_target_pairs={{0,8},{1,9},{2,10},{3,11},{4,12},{5,13},{6,14},{7,15},{8,0},{9,1},... | collective-permute-start | bytes 393224 | tf_op jit(solution)/shard_map/ppermute | solution.py:247
  70.0 1.3 %collective-permute-start.21 = (bf16[4,64,128]{2,1,0:T(8,128)(2,1)S(1)}, bf16[4,64,128]{2,1,0:T(8,128)(2,1)S(1)}, u32[]{:S(2)}, u32[]{:S(2)}) collective-permute-start(bf16[4,64,128]{2,1,0:T(8,128)(2,1)S(1)} %pad_maximum_fusion.1.near), channel_id=1, source_target_pairs={{0,1},{1,0},{2,3},{3,2},{4,5},{5,4},{6,7},{7,6},{8,9},{9,8},{10,11... | collective-permute-start | bytes 196616 | tf_op jit(solution)/shard_map/ppermute | solution.py:247

commit v3 on v2

--- a/solution.py
+++ b/solution.py
@@ -22,66 +22,65 @@
     return lax.dot_general(a, b, (((da,), (db,)), ((), ())), preferred_element_type=F32)
 
 
-def pool_kernel(t_rows, owners_ref, clusters_ref, feat_ref, grad_ref, keep_ref, give_ref, acc_ref):
-    step = pl.program_id(0)
+def pool_kernel(
+    owners_hbm, clusters_hbm, feat_hbm, grad_hbm, keep_ref, give_ref, acc_ref, rows_ref, sems, owners_ref, clusters_ref
+):
     blocks, rows = clusters_ref.shape
-    width = feat_ref.shape[1]
-
-    @pl.when(step == 0)
-    def _():
-        acc_ref[...] = jnp.zeros_like(acc_ref)
-
+    pairs, t_rows, _ = keep_ref.shape
+    width = feat_hbm.shape[1]
+    copies = [
+        pltpu.make_async_copy(owners_hbm, owners_ref, sems.at[0]),
+        pltpu.make_async_copy(clusters_hbm, clusters_ref, sems.at[1]),
+        pltpu.make_async_copy(feat_hbm, rows_ref.at[0], sems.at[2]),
+        pltpu.make_async_copy(grad_hbm, rows_ref.at[1], sems.at[3]),
+    ]
+    for copy in copies:
+        copy.start()
+    acc_ref[...] = jnp.zeros_like(acc_ref)
+    for copy in copies:
+        copy.wait()
     token = lax.broadcasted_iota(jnp.int32, (t_rows, rows), 0)
     for b in range(blocks):
         member = (clusters_ref[b : b + 1, :] == token).astype(F32)
         span = pl.ds(b * rows, rows)
-        both = jnp.concatenate([feat_ref[span, :], grad_ref[span, :]], axis=1)
+        both = jnp.concatenate([rows_ref[0, span, :], rows_ref[1, span, :]], axis=1)
         sums = jnp.dot(member.astype(BF16), both, preferred_element_type=F32)
-        place = pl.ds(pl.multiple_of(owners_ref[step * blocks + b] * t_rows, t_rows), t_rows)
+        place = pl.ds(pl.multiple_of(owners_ref[b] * t_rows, t_rows), t_rows)
         acc_ref[place, : 2 * width] += sums
         acc_ref[place, 2 * width :] += member
-
-    @pl.when(step == pl.num_programs(0) - 1)
-    def _():
-        me = lax.axis_index("shard")
-        for k in range(keep_ref.shape[0]):
-            mine = me ^ other_chip(k)
-            keep_ref[k] = acc_ref[pl.ds(pl.multiple_of(mine * t_rows, t_rows), t_rows), :]
-            other = mine ^ 1
-            give_ref[k] = acc_ref[
-                pl.ds(pl.multiple_of(other * t_rows, t_rows), t_rows), :
-            ].astype(BF16)
+    me = lax.axis_index("shard")
+    for k in range(pairs):
+        mine = me ^ chip(k)
+        keep_ref[k] = acc_ref[pl.ds(pl.multiple_of(mine * t_rows, t_rows), t_rows), :]
+        other = mine ^ 1
+        give_ref[k] = acc_ref[pl.ds(pl.multiple_of(other * t_rows, t_rows), t_rows), :].astype(BF16)
 
 
 def pool(particles, cotangent, clusters, owners, t_rows, n_shard):
     num_blocks = owners.shape[0]
     count, width = particles.shape
     rows = count // num_blocks
-    steps = 4
     shape = (n_shard // 2, t_rows, 2 * width + rows)
-    whole = pl.BlockSpec(shape, lambda i, own: (0, 0, 0))
+    whole = pl.BlockSpec(memory_space=pl.ANY)
     return pl.pallas_call(
-        functools.partial(pool_kernel, t_rows),
-        grid_spec=pltpu.PrefetchScalarGridSpec(
-            num_scalar_prefetch=1,
-            grid=(steps,),
-            in_specs=[
-                pl.BlockSpec((num_blocks // steps, rows), lambda i, own: (i, 0)),
-                pl.BlockSpec((count // steps, width), lambda i, own: (i, 0)),
-                pl.BlockSpec((count // steps, width), lambda i, own: (i, 0)),
-            ],
-            out_specs=[whole, whole],
-            scratch_shapes=[pltpu.VMEM((n_shard * t_rows, shape[2]), F32)],
-        ),
+        pool_kernel,
+        in_specs=[whole] * 4,
+        out_specs=[VMEM, VMEM],
         out_shape=[jax.ShapeDtypeStruct(shape, F32), jax.ShapeDtypeStruct(shape, BF16)],
-        compiler_params=params(24),
+        scratch_shapes=[
+            pltpu.VMEM((n_shard * t_rows, shape[2]), F32),
+            pltpu.VMEM((2, count, width), BF16),
+            pltpu.SemaphoreType.DMA((4,)),
+            pltpu.SMEM(owners.shape, jnp.int32),
+            pltpu.VMEM((num_blocks, rows), jnp.int32),
+        ],
+        compiler_params=params(60),
         name="pool",
     )(owners, clusters.reshape(num_blocks, rows), particles, cotangent)
 
 
 def attend_kernel(parts, *refs):
-    tok = refs[:parts]
-    pooled_refs = refs[parts : 2 * parts]
+    tok, pooled_refs = refs[:parts], refs[parts : 2 * parts]
     near, far, w_in, w_out, up_ref, keep_ref, give_ref, weight, hid, term = refs[2 * parts :]
     pairs, rows, cols = near.shape
     t_rows, width = tok[0].shape
@@ -92,7 +91,7 @@
     core = lax.rem(me, 2)
     pair = lax.div(me, 2)
     for k in range(pairs):
-        mine = me ^ other_chip(k)
+        mine = me ^ chip(reverse(k, pairs))
         weight[pl.ds(pl.multiple_of(mine * rows, rows), rows), :] = near[k]
         weight[pl.ds(pl.multiple_of((mine ^ 1) * rows, rows), rows), :] = far[k]
     pooled = jnp.concatenate([r[:, :channels] for r in pooled_refs], axis=0)
@@ -145,7 +144,7 @@
     for k in range(pairs):
         chunk = pl.ds(pl.multiple_of((pair ^ k) * (2 * rows), 2 * rows), 2 * rows)
         term[...] = contract(hid[:, chunk], q_grad, 0, 0)
-        mine = core ^ 1 if k else core
+        mine = core ^ odd(k)
         keep_ref[k] = term[pl.ds(pl.multiple_of(mine * rows, rows), rows), :].astype(BF16)
         give_ref[k] = term[pl.ds(pl.multiple_of((1 - mine) * rows, rows), rows), :].astype(BF16)
 
@@ -180,7 +179,7 @@
     def _():
         me = lax.axis_index("shard")
         for k in range(pairs):
-            mine = me ^ other_chip(k)
+            mine = me ^ chip(k)
             rows_ref[pl.ds(pl.multiple_of(mine * t_rows, t_rows), t_rows), :] = near[k]
             rows_ref[pl.ds(pl.multiple_of((mine ^ 1) * t_rows, t_rows), t_rows), :] = far[k]
 
@@ -247,8 +246,17 @@
     return lax.ppermute(x, ("group", "shard"), pairs)
 
 
-def other_chip(k):
-    return 2 * k + 1 if k else 0
+def odd(k):
+    return bin(k).count("1") % 2
+
+
+def reverse(k, count):
+    bits = count.bit_length() - 1
+    return sum(((k >> i) & 1) << (bits - 1 - i) for i in range(bits))
+
+
+def chip(k):
+    return 2 * k + odd(k)
 
 
 def local(tokens, w_qk, w_in, w_out, particles, cotangent, clusters, owners):
@@ -260,39 +268,51 @@
     part = lax.rem(lax.axis_index("group"), parts)
 
     w_own = lax.dynamic_slice_in_dim(w_qk, part * cols, cols, axis=1)
-    near = [w_own] + [swap(w_own, 0, other_chip(k)) for k in range(1, pairs)]
-    tok = [tokens] + [swap(tokens, k, 1) for k in range(1, parts)]
-    owners, near[1] = lax.optimization_barrier((owners, near[1]))
-    near = jnp.stack(near)
-    far = swap(near, 0, 1)
+
+    bits = [pairs >> i for i in range(1, pairs.bit_length())]
+    first = [w_own[None]]
+    for k in bits[:-1]:
+        first.append(swap(jnp.concatenate(first), 0, chip(k)))
+    tok = tokens[None]
+    tok_x = swap(tok, 1, 1)
+    tok = jnp.concatenate([tok, tok_x])
+    for k in [1 << i for i in range(1, parts.bit_length() - 1)]:
+        tok = jnp.concatenate([tok, swap(tok, k, 1)])
 
     keep, give = pool(particles, cotangent, clusters, owners, t_rows, n_shard)
-    joined = keep + swap(give, 0, 1).astype(F32)
+    got = swap(give, 0, 1)
+    got, first[-1], tok_x = lax.optimization_barrier((got, first[-1], tok_x))
+    first = jnp.concatenate(first)
+    joined = keep + got.astype(F32)
     sums = joined[0]
     for k in range(1, pairs):
-        sums = sums + swap(joined[k].astype(BF16), 0, other_chip(k)).astype(F32)
+        sums = sums + swap(joined[k].astype(BF16), 0, chip(k)).astype(F32)
+    second = swap(first, 0, chip(1))
+    far_first = swap(first, 0, 1)
     channels = particles.shape[1]
     counts = jnp.sum(sums[:, 2 * channels :], axis=1, keepdims=True)
     pooled = jnp.concatenate(
         [sums[:, :channels] / jnp.maximum(counts, 1.0), sums[:, channels : 2 * channels]], axis=1
     ).astype(BF16)
-    pooled = [pooled] + [swap(pooled, k, 1) for k in range(1, parts)]
-
-    up, keep, give = attend(tok, pooled, near, far, w_in, w_out)
+    pooled = [pooled] + [swap(pooled, k, odd(k)) for k in range(1, parts)]
+    second, pooled[-1] = lax.optimization_barrier((second, pooled[-1]))
+    near = jnp.concatenate([first, second])
+    far = jnp.concatenate([far_first, swap(second, 0, 1)])
+
+    up, keep, give = attend([tok[0], tok_x[0]] + [tok[k] for k in range(2, parts)], pooled, near, far, w_in, w_out)
 
     joined = keep.astype(F32) + swap(give, 0, 1).astype(F32)
-    up, joined = lax.optimization_barrier((up, joined))
     unpooled = up[0].astype(F32)
     for k in range(1, parts):
-        unpooled = unpooled + swap(up[k], k, 1).astype(F32)
+        unpooled = unpooled + swap(up[k], k, odd(k)).astype(F32)
     unpooled = unpooled.astype(BF16)
-    near = jnp.stack([unpooled] + [swap(unpooled, 0, other_chip(k)) for k in range(1, pairs)])
+    near = jnp.stack([unpooled] + [swap(unpooled, 0, chip(k)) for k in range(1, pairs)])
     far = swap(near, 0, 1)
     particle_out = unpool(particles, clusters, owners, near, far)
 
     grad = joined[0]
     for k in range(1, pairs):
-        grad = grad + swap(joined[k].astype(BF16), 0, other_chip(k)).astype(F32)
+        grad = grad + swap(joined[k].astype(BF16), 0, chip(k)).astype(F32)
     if n_group > parts:
         part_sum = grad.astype(BF16)
         for k in range(1, n_group // parts):

time: 77.8 us -> 64.5 us (0.83)
  waiting for transfers between devices: 28.3 us -> 19.8 us
  local copies, waits for them, and re-layouts: 3.6 us -> 0.16 us
  starting transfers between devices: 35.4 us -> 32.7 us
  Pallas kernels: 8.76 us -> 10.2 us
    ppermute x28 -> x27, waiting for transfers between devices: 28.3 us -> 19.8 us  [swap(): return lax.ppermute(x, ('group', 'shard'), pairs)]
    unnamed x18 -> x16, local copies, waits for them, and re-layouts: 3.51 us -> 0.05 us
    ppermute x28 -> x27, starting transfers between devices: 35.4 us -> 32.7 us  [swap(): return lax.ppermute(x, ('group', 'shard'), pairs)]
    pallas_call x1, Pallas kernels: 1.64 us -> 3.09 us  [pool(): pl.pallas_call(pool_kernel, in_specs=[whole] * 4, out_specs=[VMEM, VMEM],...]
  transfers between devices with their start and end apart: 28 -> 27, of which waited for: 12 -> 13; matrix products, arithmetic and copies ran while one was open for 1% -> 1% of each run, Pallas kernels for 4% -> 9%
where the time goes in v3:
time: 64.5 us; the launch traced here: 64.4 us
  starting transfers between devices  32.7 us (51%)
  waiting for transfers between devices  19.8 us (31%)
  Pallas kernels  10.2 us (16%)
  between operations  0.87 us (1%)
  other arithmetic  0.66 us (1%)
    ppermute x27, starting transfers between devices, swap(): return lax.ppermute(x, ('group', 'shard'), pairs)  32.7 us
    ppermute x27, waiting for transfers between devices, swap(): return lax.ppermute(x, ('group', 'shard'), pairs)  19.8 us
    pallas_call x1, Pallas kernels, attend(): pl.pallas_call(functools.partial(attend_kernel, parts), in_specs=[VMEM] *...  3.23 us
    pallas_call x1, Pallas kernels, pool(): pl.pallas_call(pool_kernel, in_specs=[whole] * 4, out_specs=[VMEM, VMEM],...  3.09 us
    pallas_call x1, Pallas kernels, unpool(): pl.pallas_call(unpool_kernel, grid_spec=pltpu.PrefetchScalarGridSpec(num_...  2.82 us
  transfers between devices with their start and end apart: 27, of which 13 were waited for; matrix products, arithmetic and copies ran while one was open for 1% of the time, Pallas kernels for 9%

profile of v3, /device:TPU:0, one launch (start us, length us, event | category | flops | bytes accessed | tf_op | source)
XLA Modules:
  0.0 64.4 jit_solution(10480261811137673252)
XLA Ops:
  0.6 2.4 %collective-permute-start.2 = (bf16[1,64,2048]{2,1,0:T(8,128)(2,1)}, bf16[1,64,2048]{2,1,0:T(8,128)(2,1)S(1)}, u32[]{:S(2)}, u32[]{:S(2)}) collective-permute-start(bf16[1,64,2048]{2,1,0:T(8,128)(2,1)} %bitcast.52), channel_id=1, source_target_pairs={{0,9},{1,8},{2,11},{3,10},{4,13},{5,12},{6,15},{7,14},{8,1},{9,0},... | collective-permute-start | bytes 786440 | tf_op jit(solution)/shard_map/ppermute | solution.py:246
  3.1 2.9 %collective-permute-start.1 = (bf16[1,256,256]{2,1,0:T(8,128)(2,1)S(1)}, bf16[1,256,256]{2,1,0:T(8,128)(2,1)S(1)}, u32[]{:S(2)}, u32[]{:S(2)}) collective-permute-start(bf16[1,256,256]{2,1,0:T(8,128)(2,1)S(1)} %dynamic-slice_bitcast_fusion), channel_id=1, source_target_pairs={{0,5},{1,4},{2,7},{3,6},{4,1},{5,0},{6,3},{7,2},{8,13},{9,12},{10,... | collective-permute-start | bytes 393224 | tf_op jit(solution)/shard_map/ppermute | solution.py:246
  6.0 3.1 %pool.1 = (f32[4,64,384]{2,1,0:T(8,128)}, bf16[4,64,384]{2,1,0:T(8,128)(2,1)}) custom-call(s32[32]{0:T(128)} %owners_ref.1, s32[32,128]{1,0:T(8,128)} %bitcast.55, bf16[4096,128]{1,0:T(8,128)(2,1)} %feat_ref.1, bf16[4096,128]{1,0:T(8,128)(2,1)} %grad_hbm.1), custom_call_target="tpu_custom_call" | custom-call | tf_op jit(solution)/shard_map/pool/pallas_call | solution.py:65
  9.2 0.1 collective-permute-start
  9.2 0.9 %collective-permute-done.2 = bf16[1,64,2048]{2,1,0:T(8,128)(2,1)S(1)} collective-permute-done((bf16[1,64,2048]{2,1,0:T(8,128)(2,1)}, bf16[1,64,2048]{2,1,0:T(8,128)(2,1)S(1)}, u32[]{:S(2)}, u32[]{:S(2)}) %collective-permute-start.2) | collective-permute-done | bytes 262176 | tf_op jit(solution)/shard_map/ppermute | solution.py:246
  10.1 0.1 pad_maximum_fusion
  10.1 2.2 %collective-permute-start.3 = (bf16[2,64,2048]{2,1,0:T(8,128)(2,1)S(1)}, bf16[2,64,2048]{2,1,0:T(8,128)(2,1)S(1)}, u32[]{:S(2)}, u32[]{:S(2)}) collective-permute-start(bf16[2,64,2048]{2,1,0:T(8,128)(2,1)S(1)} %pad_maximum_fusion), channel_id=1, source_target_pairs={{0,17},{1,16},{2,19},{3,18},{4,21},{5,20},{6,23},{7,22},{8,25},{9,... | collective-permute-start | bytes 1572872 | tf_op jit(solution)/shard_map/ppermute | solution.py:246
  12.3 0.1 fusion.12
  12.4 1.6 %collective-permute-start.4 = (bf16[64,384]{1,0:T(8,128)(2,1)S(1)}, bf16[64,384]{1,0:T(8,128)(2,1)S(1)}, u32[]{:S(2)}, u32[]{:S(2)}) collective-permute-start(bf16[64,384]{1,0:T(8,128)(2,1)S(1)} %get-tuple-element.31), channel_id=1, source_target_pairs={{0,3},{1,2},{2,1},{3,0},{4,7},{5,6},{6,5},{7,4},{8,11},{9,10},{10,... | collective-permute-start | bytes 147464 | tf_op jit(solution)/shard_map/ppermute | solution.py:246
  14.1 2.5 %collective-permute-start.6 = (bf16[64,384]{1,0:T(8,128)(2,1)S(1)}, bf16[64,384]{1,0:T(8,128)(2,1)S(1)}, u32[]{:S(2)}, u32[]{:S(2)}) collective-permute-start(bf16[64,384]{1,0:T(8,128)(2,1)S(1)} %get-tuple-element.32), channel_id=1, source_target_pairs={{0,6},{1,7},{2,4},{3,5},{4,2},{5,3},{6,0},{7,1},{8,14},{9,15},{10,... | collective-permute-start | bytes 147464 | tf_op jit(solution)/shard_map/ppermute | solution.py:246
  16.6 1.7 %collective-permute-start.9 = (bf16[2,256,256]{2,1,0:T(8,128)(2,1)S(1)}, bf16[2,256,256]{2,1,0:T(8,128)(2,1)S(1)}, u32[]{:S(2)}, u32[]{:S(2)}) collective-permute-start(bf16[2,256,256]{2,1,0:T(8,128)(2,1)S(1)} %pad_maximum_fusion.3), channel_id=1, source_target_pairs={{0,3},{1,2},{2,1},{3,0},{4,7},{5,6},{6,5},{7,4},{8,11},{9,10},{10,... | collective-permute-start | bytes 786440 | tf_op jit(solution)/shard_map/ppermute | solution.py:246
  18.3 1.7 %collective-permute-done.6 = bf16[64,384]{1,0:T(8,128)(2,1)S(1)} collective-permute-done((bf16[64,384]{1,0:T(8,128)(2,1)S(1)}, bf16[64,384]{1,0:T(8,128)(2,1)S(1)}, u32[]{:S(2)}, u32[]{:S(2)}) %collective-permute-start.6) | collective-permute-done | bytes 49184 | tf_op jit(solution)/shard_map/ppermute | solution.py:246
  20.0 2.6 %collective-permute-done.5 = bf16[64,384]{1,0:T(8,128)(2,1)S(1)} collective-permute-done((bf16[64,384]{1,0:T(8,128)(2,1)S(1)}, bf16[64,384]{1,0:T(8,128)(2,1)S(1)}, u32[]{:S(2)}, u32[]{:S(2)}) %collective-permute-start.5) | collective-permute-done | bytes 49184 | tf_op jit(solution)/shard_map/ppermute | solution.py:246
  22.6 0.1 slice_reduce_fusion
  22.8 0.1 fusion.7
  22.9 2.4 %collective-permute-start.10 = (bf16[64,256]{1,0:T(8,128)(2,1)S(1)}, bf16[64,256]{1,0:T(8,128)(2,1)S(1)}, u32[]{:S(2)}, u32[]{:S(2)}) collective-permute-start(bf16[64,256]{1,0:T(8,128)(2,1)S(1)} %pad_maximum_fusion.5.refs_4_), channel_id=1, source_target_pairs={{0,24},{1,25},{2,26},{3,27},{4,28},{5,29},{6,30},{7,31},{8,16},{9,... | collective-permute-start | bytes 98312 | tf_op jit(solution)/shard_map/ppermute | solution.py:246
  25.3 0.7 %collective-permute-start.8 = (bf16[64,256]{1,0:T(8,128)(2,1)S(1)}, bf16[64,256]{1,0:T(8,128)(2,1)S(1)}, u32[]{:S(2)}, u32[]{:S(2)}) collective-permute-start(bf16[64,256]{1,0:T(8,128)(2,1)S(1)} %pad_maximum_fusion.5.refs_4_), channel_id=1, source_target_pairs={{0,17},{1,16},{2,19},{3,18},{4,21},{5,20},{6,23},{7,22},{8,25},{9,... | collective-permute-start | bytes 98312 | tf_op jit(solution)/shard_map/ppermute | solution.py:246
  26.0 1.7 %collective-permute-done.10.refs_7_ = bf16[64,256]{1,0:T(8,128)(2,1)S(1)} collective-permute-done((bf16[64,256]{1,0:T(8,128)(2,1)S(1)}, bf16[64,256]{1,0:T(8,128)(2,1)S(1)}, u32[]{:S(2)}, u32[]{:S(2)}) %collective-permute-start.10) | collective-permute-done | bytes 32800 | tf_op jit(solution)/shard_map/ppermute | solution.py:246
  27.8 1.7 %collective-permute-start.12 = (bf16[2,256,256]{2,1,0:T(8,128)(2,1)S(1)}, bf16[2,256,256]{2,1,0:T(8,128)(2,1)S(1)}, u32[]{:S(2)}, u32[]{:S(2)}) collective-permute-start(bf16[2,256,256]{2,1,0:T(8,128)(2,1)S(1)} %collective-permute-done.9), channel_id=1, source_target_pairs={{0,1},{1,0},{2,3},{3,2},{4,5},{5,4},{6,7},{7,6},{8,9},{9,8},{10,11... | collective-permute-start | bytes 786440 | tf_op jit(solution)/shard_map/ppermute | solution.py:246
  29.5 0.1 pad_maximum_fusion.1.refs_8_
  29.7 1.0 %collective-permute-done.12 = bf16[2,256,256]{2,1,0:T(8,128)(2,1)S(1)} collective-permute-done((bf16[2,256,256]{2,1,0:T(8,128)(2,1)S(1)}, bf16[2,256,256]{2,1,0:T(8,128)(2,1)S(1)}, u32[]{:S(2)}, u32[]{:S(2)}) %collective-permute-start.12) | collective-permute-done | bytes 262176 | tf_op jit(solution)/shard_map/ppermute | solution.py:246
  30.7 0.5 collective-permute-done.7.refs_5_
  31.3 3.2 %attend.1 = (bf16[4,64,128]{2,1,0:T(8,128)(2,1)S(1)}, bf16[4,256,256]{2,1,0:T(8,128)(2,1)S(1)}, bf16[4,256,256]{2,1,0:T(8,128)(2,1)S(1)}) custom-call(bf16[64,2048]{1,0:T(8,128)(2,1)S(1)} %copy-done.2, bf16[64,2048]{1,0:T(8,128)(2,1)S(1)} %bitcast.54, bf16[64,2048]{1,0:T(8,128)(2,1)S(1)} %get-tuple-element.30.refs_2_, ...), custom_call_target="tpu_custom_call" | custom-call | tf_op jit(solution)/shard_map/attend/pallas_call | solution.py:158
  34.5 0.2 collective-permute-start.20
  34.7 1.5 %collective-permute-start.13 = (bf16[64,128]{1,0:T(8,128)(2,1)S(1)}, bf16[64,128]{1,0:T(8,128)(2,1)S(1)}, u32[]{:S(2)}, u32[]{:S(2)}) collective-permute-start(bf16[64,128]{1,0:T(8,128)(2,1)S(1)} %get-tuple-element.34), channel_id=1, source_target_pairs={{0,9},{1,8},{2,11},{3,10},{4,13},{5,12},{6,15},{7,14},{8,1},{9,0},... | collective-permute-start | bytes 49160 | tf_op jit(solution)/shard_map/ppermute | solution.py:246
  36.2 1.3 %collective-permute-start.15 = (bf16[64,128]{1,0:T(8,128)(2,1)S(1)}, bf16[64,128]{1,0:T(8,128)(2,1)S(1)}, u32[]{:S(2)}, u32[]{:S(2)}) collective-permute-start(bf16[64,128]{1,0:T(8,128)(2,1)S(1)} %get-tuple-element.35), channel_id=1, source_target_pairs={{0,24},{1,25},{2,26},{3,27},{4,28},{5,29},{6,30},{7,31},{8,16},{9,... | collective-permute-start | bytes 49160 | tf_op jit(solution)/shard_map/ppermute | solution.py:246
  37.5 0.1 collective-permute-start.14
  37.7 0.1 fusion.11
  37.8 0.1 collective-permute-start.21
  37.9 2.5 %collective-permute-start.23 = (bf16[256,256]{1,0:T(8,128)(2,1)S(1)}, bf16[256,256]{1,0:T(8,128)(2,1)S(1)}, u32[]{:S(2)}, u32[]{:S(2)}) collective-permute-start(bf16[256,256]{1,0:T(8,128)(2,1)S(1)} %get-tuple-element.27), channel_id=1, source_target_pairs={{0,6},{1,7},{2,4},{3,5},{4,2},{5,3},{6,0},{7,1},{8,14},{9,15},{10,... | collective-permute-start | bytes 393224 | tf_op jit(solution)/shard_map/ppermute | solution.py:246
  40.4 0.4 collective-permute-start.22
  40.8 0.1 collective-permute-done.15
  40.9 0.1 collective-permute-done.14
  41.0 1.9 %collective-permute-start.18 = (bf16[64,128]{1,0:T(8,128)(2,1)S(1)}, bf16[64,128]{1,0:T(8,128)(2,1)S(1)}, u32[]{:S(2)}, u32[]{:S(2)}) collective-permute-start(bf16[64,128]{1,0:T(8,128)(2,1)S(1)} %fusion.10), channel_id=1, source_target_pairs={{0,6},{1,7},{2,4},{3,5},{4,2},{5,3},{6,0},{7,1},{8,14},{9,15},{10,... | collective-permute-start | bytes 49160 | tf_op jit(solution)/shard_map/ppermute | solution.py:246
  42.9 0.5 collective-permute-start.17
  43.4 1.8 %collective-permute-start.16 = (bf16[64,128]{1,0:T(8,128)(2,1)S(1)}, bf16[64,128]{1,0:T(8,128)(2,1)S(1)}, u32[]{:S(2)}, u32[]{:S(2)}) collective-permute-start(bf16[64,128]{1,0:T(8,128)(2,1)S(1)} %fusion.10), channel_id=1, source_target_pairs={{0,3},{1,2},{2,1},{3,0},{4,7},{5,6},{6,5},{7,4},{8,11},{9,10},{10,... | collective-permute-start | bytes 49160 | tf_op jit(solution)/shard_map/ppermute | solution.py:246
  45.2 2.4 %collective-permute-done.23 = bf16[256,256]{1,0:T(8,128)(2,1)S(1)} collective-permute-done((bf16[256,256]{1,0:T(8,128)(2,1)S(1)}, bf16[256,256]{1,0:T(8,128)(2,1)S(1)}, u32[]{:S(2)}, u32[]{:S(2)}) %collective-permute-start.23) | collective-permute-done | bytes 131104 | tf_op jit(solution)/shard_map/ppermute | solution.py:246
  47.6 5.3 %collective-permute-done.22 = bf16[256,256]{1,0:T(8,128)(2,1)S(1)} collective-permute-done((bf16[256,256]{1,0:T(8,128)(2,1)S(1)}, bf16[256,256]{1,0:T(8,128)(2,1)S(1)}, u32[]{:S(2)}, u32[]{:S(2)}) %collective-permute-start.22) | collective-permute-done | bytes 131104 | tf_op jit(solution)/shard_map/ppermute | solution.py:246
  52.9 0.1 fusion.3.refs_0_
  53.0 2.4 %collective-permute-start.26 = (bf16[256,256]{1,0:T(8,128)(2,1)S(1)}, bf16[256,256]{1,0:T(8,128)(2,1)S(1)}, u32[]{:S(2)}, u32[]{:S(2)}) collective-permute-start(bf16[256,256]{1,0:T(8,128)(2,1)S(1)} %fusion.3.refs_0_), channel_id=1, source_target_pairs={{0,24},{1,25},{2,26},{3,27},{4,28},{5,29},{6,30},{7,31},{8,16},{9,... | collective-permute-start | bytes 393224 | tf_op jit(solution)/shard_map/ppermute | solution.py:246
  55.4 0.5 collective-permute-start.25
  55.9 0.7 %collective-permute-start.24 = (bf16[256,256]{1,0:T(8,128)(2,1)S(1)}, bf16[256,256]{1,0:T(8,128)(2,1)S(1)}, u32[]{:S(2)}, u32[]{:S(2)}) collective-permute-start(bf16[256,256]{1,0:T(8,128)(2,1)S(1)} %fusion.3.refs_0_), channel_id=1, source_target_pairs={{0,8},{1,9},{2,10},{3,11},{4,12},{5,13},{6,14},{7,15},{8,0},{9,1},... | collective-permute-start | bytes 393224 | tf_op jit(solution)/shard_map/ppermute | solution.py:246
  56.6 0.5 collective-permute-start.19
  57.1 0.9 %collective-permute-done.19.far = bf16[4,64,128]{2,1,0:T(8,128)(2,1)S(1)} collective-permute-done((bf16[4,64,128]{2,1,0:T(8,128)(2,1)S(1)}, bf16[4,64,128]{2,1,0:T(8,128)(2,1)S(1)}, u32[]{:S(2)}, u32[]{:S(2)}) %collective-permute-start.19) | collective-permute-done | bytes 65568 | tf_op jit(solution)/shard_map/ppermute | solution.py:246
  58.0 2.8 %unpool.1 = bf16[4096,128]{1,0:T(8,128)(2,1)} custom-call(s32[32]{0:T(128)S(1)} %copy-done.6, s32[32,128]{1,0:T(8,128)S(1)} %bitcast.56, bf16[4096,128]{1,0:T(8,128)(2,1)S(1)} %copy-done.1, bf16[4,64,128]{2,1,0:T(8,128)(2,1)S(1)} %pad_maximum_fusion.4.near, bf16[4,64,128]{2,1,0:T(8,128)(2,1)S(1)} %collective-permute-done.19.far), custom_call_target="tpu_custom_call" | custom-call | tf_op jit(solution)/shard_map/unpool/pallas_call | solution.py:202
  60.8 2.3 %collective-permute-done.25.refs_2_ = bf16[256,256]{1,0:T(8,128)(2,1)S(1)} collective-permute-done((bf16[256,256]{1,0:T(8,128)(2,1)S(1)}, bf16[256,256]{1,0:T(8,128)(2,1)S(1)}, u32[]{:S(2)}, u32[]{:S(2)}) %collective-permute-start.25) | collective-permute-done | bytes 131104 | tf_op jit(solution)/shard_map/ppermute | solution.py:246
  63.1 0.2 collective-permute-done.24.refs_1_
  63.3 1.1 %spread.1 = f32[256,1024]{1,0:T(8,128)} custom-call(bf16[256,256]{1,0:T(8,128)(2,1)S(1)} %fusion.3.refs_0_, bf16[256,256]{1,0:T(8,128)(2,1)S(1)} %collective-permute-done.24.refs_1_, bf16[256,256]{1,0:T(8,128)(2,1)S(1)} %collective-permute-done.25.refs_2_, bf16[256,256]{1,0:T(8,128)(2,1)S(1)} %collective-permute-done.26.refs_3_), custom_call_target="tpu_custom_call" | custom-call | tf_op jit(solution)/shard_map/spread/pallas_call | solution.py:232
  (46 shorter events, 0.4 us)
Async XLA Ops:
  0.6 2.5 %copy-start = (bf16[256,1024]{1,0:T(8,128)(2,1)S(1)}, bf16[256,1024]{1,0:T(8,128)(2,1)}, u32[]{:S(2)}) copy-start(bf16[256,1024]{1,0:T(8,128)(2,1)} %param.9) | copy-start | bytes 1572868
  0.6 9.4 %collective-permute-start.2 = (bf16[1,64,2048]{2,1,0:T(8,128)(2,1)}, bf16[1,64,2048]{2,1,0:T(8,128)(2,1)S(1)}, u32[]{:S(2)}, u32[]{:S(2)}) collective-permute-start(bf16[1,64,2048]{2,1,0:T(8,128)(2,1)} %bitcast.52), channel_id=1, source_target_pairs={{0,9},{1,8},{2,11},{3,10},{4,13},{5,12},{6,15},{7,14},{8,1},{9,0},... | collective-permute-start | bytes 786440 | tf_op jit(solution)/shard_map/ppermute | solution.py:246
  3.1 9.2 %collective-permute-start.1 = (bf16[1,256,256]{2,1,0:T(8,128)(2,1)S(1)}, bf16[1,256,256]{2,1,0:T(8,128)(2,1)S(1)}, u32[]{:S(2)}, u32[]{:S(2)}) collective-permute-start(bf16[1,256,256]{2,1,0:T(8,128)(2,1)S(1)} %dynamic-slice_bitcast_fusion), channel_id=1, source_target_pairs={{0,5},{1,4},{2,7},{3,6},{4,1},{5,0},{6,3},{7,2},{8,13},{9,12},{10,... | collective-permute-start | bytes 393224 | tf_op jit(solution)/shard_map/ppermute | solution.py:246
  6.0 4.0 %copy-start.2 = (bf16[64,2048]{1,0:T(8,128)(2,1)S(1)}, bf16[64,2048]{1,0:T(8,128)(2,1)}, u32[]{:S(2)}) copy-start(bf16[64,2048]{1,0:T(8,128)(2,1)} %refs_0_.1) | copy-start | bytes 786436
  9.1 3.2 %copy-start.7 = (f32[4,64,384]{2,1,0:T(8,128)S(1)}, f32[4,64,384]{2,1,0:T(8,128)}, u32[]{:S(2)}) copy-start(f32[4,64,384]{2,1,0:T(8,128)} %get-tuple-element.14) | copy-start | bytes 1179652
  9.2 3.2 %collective-permute-start = (bf16[4,64,384]{2,1,0:T(8,128)(2,1)}, bf16[4,64,384]{2,1,0:T(8,128)(2,1)S(1)}, u32[]{:S(2)}, u32[]{:S(2)}) collective-permute-start(bf16[4,64,384]{2,1,0:T(8,128)(2,1)} %get-tuple-element.12), channel_id=1, source_target_pairs={{0,1},{1,0},{2,3},{3,2},{4,5},{5,4},{6,7},{7,6},{8,9},{9,8},{10,11... | collective-permute-start | bytes 589832 | tf_op jit(solution)/shard_map/ppermute | solution.py:246
  10.1 19.4 %collective-permute-start.3 = (bf16[2,64,2048]{2,1,0:T(8,128)(2,1)S(1)}, bf16[2,64,2048]{2,1,0:T(8,128)(2,1)S(1)}, u32[]{:S(2)}, u32[]{:S(2)}) collective-permute-start(bf16[2,64,2048]{2,1,0:T(8,128)(2,1)S(1)} %pad_maximum_fusion), channel_id=1, source_target_pairs={{0,17},{1,16},{2,19},{3,18},{4,21},{5,20},{6,23},{7,22},{8,25},{9,... | collective-permute-start | bytes 1572872 | tf_op jit(solution)/shard_map/ppermute | solution.py:246
  12.4 5.8 %collective-permute-start.4 = (bf16[64,384]{1,0:T(8,128)(2,1)S(1)}, bf16[64,384]{1,0:T(8,128)(2,1)S(1)}, u32[]{:S(2)}, u32[]{:S(2)}) collective-permute-start(bf16[64,384]{1,0:T(8,128)(2,1)S(1)} %get-tuple-element.31), channel_id=1, source_target_pairs={{0,3},{1,2},{2,1},{3,0},{4,7},{5,6},{6,5},{7,4},{8,11},{9,10},{10,... | collective-permute-start | bytes 147464 | tf_op jit(solution)/shard_map/ppermute | solution.py:246
  14.1 5.9 %collective-permute-start.6 = (bf16[64,384]{1,0:T(8,128)(2,1)S(1)}, bf16[64,384]{1,0:T(8,128)(2,1)S(1)}, u32[]{:S(2)}, u32[]{:S(2)}) collective-permute-start(bf16[64,384]{1,0:T(8,128)(2,1)S(1)} %get-tuple-element.32), channel_id=1, source_target_pairs={{0,6},{1,7},{2,4},{3,5},{4,2},{5,3},{6,0},{7,1},{8,14},{9,15},{10,... | collective-permute-start | bytes 147464 | tf_op jit(solution)/shard_map/ppermute | solution.py:246
  16.5 6.1 %collective-permute-start.5 = (bf16[64,384]{1,0:T(8,128)(2,1)S(1)}, bf16[64,384]{1,0:T(8,128)(2,1)S(1)}, u32[]{:S(2)}, u32[]{:S(2)}) collective-permute-start(bf16[64,384]{1,0:T(8,128)(2,1)S(1)} %get-tuple-element.33), channel_id=1, source_target_pairs={{0,5},{1,4},{2,7},{3,6},{4,1},{5,0},{6,3},{7,2},{8,13},{9,12},{10,... | collective-permute-start | bytes 147464 | tf_op jit(solution)/shard_map/ppermute | solution.py:246
  16.6 11.2 %collective-permute-start.9 = (bf16[2,256,256]{2,1,0:T(8,128)(2,1)S(1)}, bf16[2,256,256]{2,1,0:T(8,128)(2,1)S(1)}, u32[]{:S(2)}, u32[]{:S(2)}) collective-permute-start(bf16[2,256,256]{2,1,0:T(8,128)(2,1)S(1)} %pad_maximum_fusion.3), channel_id=1, source_target_pairs={{0,3},{1,2},{2,1},{3,0},{4,7},{5,6},{6,5},{7,4},{8,11},{9,10},{10,... | collective-permute-start | bytes 786440 | tf_op jit(solution)/shard_map/ppermute | solution.py:246
  22.9 4.9 %collective-permute-start.10 = (bf16[64,256]{1,0:T(8,128)(2,1)S(1)}, bf16[64,256]{1,0:T(8,128)(2,1)S(1)}, u32[]{:S(2)}, u32[]{:S(2)}) collective-permute-start(bf16[64,256]{1,0:T(8,128)(2,1)S(1)} %pad_maximum_fusion.5.refs_4_), channel_id=1, source_target_pairs={{0,24},{1,25},{2,26},{3,27},{4,28},{5,29},{6,30},{7,31},{8,16},{9,... | collective-permute-start | bytes 98312 | tf_op jit(solution)/shard_map/ppermute | solution.py:246
  25.3 4.3 %collective-permute-start.11 = (bf16[2,256,256]{2,1,0:T(8,128)(2,1)S(1)}, bf16[2,256,256]{2,1,0:T(8,128)(2,1)S(1)}, u32[]{:S(2)}, u32[]{:S(2)}) collective-permute-start(bf16[2,256,256]{2,1,0:T(8,128)(2,1)S(1)} %pad_maximum_fusion.3), channel_id=1, source_target_pairs={{0,1},{1,0},{2,3},{3,2},{4,5},{5,4},{6,7},{7,6},{8,9},{9,8},{10,11... | collective-permute-start | bytes 786440 | tf_op jit(solution)/shard_map/ppermute | solution.py:246
  25.3 5.4 %collective-permute-start.8 = (bf16[64,256]{1,0:T(8,128)(2,1)S(1)}, bf16[64,256]{1,0:T(8,128)(2,1)S(1)}, u32[]{:S(2)}, u32[]{:S(2)}) collective-permute-start(bf16[64,256]{1,0:T(8,128)(2,1)S(1)} %pad_maximum_fusion.5.refs_4_), channel_id=1, source_target_pairs={{0,17},{1,16},{2,19},{3,18},{4,21},{5,20},{6,23},{7,22},{8,25},{9,... | collective-permute-start | bytes 98312 | tf_op jit(solution)/shard_map/ppermute | solution.py:246
  27.8 3.5 %collective-permute-start.7 = (bf16[64,256]{1,0:T(8,128)(2,1)S(1)}, bf16[64,256]{1,0:T(8,128)(2,1)S(1)}, u32[]{:S(2)}, u32[]{:S(2)}) collective-permute-start(bf16[64,256]{1,0:T(8,128)(2,1)S(1)} %pad_maximum_fusion.5.refs_4_), channel_id=1, source_target_pairs={{0,9},{1,8},{2,11},{3,10},{4,13},{5,12},{6,15},{7,14},{8,1},{9,0},... | collective-permute-start | bytes 98312 | tf_op jit(solution)/shard_map/ppermute | solution.py:246
  27.8 2.9 %collective-permute-start.12 = (bf16[2,256,256]{2,1,0:T(8,128)(2,1)S(1)}, bf16[2,256,256]{2,1,0:T(8,128)(2,1)S(1)}, u32[]{:S(2)}, u32[]{:S(2)}) collective-permute-start(bf16[2,256,256]{2,1,0:T(8,128)(2,1)S(1)} %collective-permute-done.9), channel_id=1, source_target_pairs={{0,1},{1,0},{2,3},{3,2},{4,5},{5,4},{6,7},{7,6},{8,9},{9,8},{10,11... | collective-permute-start | bytes 786440 | tf_op jit(solution)/shard_map/ppermute | solution.py:246
  29.6 1.6 %copy-start.3 = (bf16[128,2048]{1,0:T(8,128)(2,1)S(1)}, bf16[128,2048]{1,0:T(8,128)(2,1)}, u32[]{:S(2)}) copy-start(bf16[128,2048]{1,0:T(8,128)(2,1)} %refs_10_.1) | copy-start | bytes 1572868
  29.6 1.6 %copy-start.4 = (bf16[2048,128]{1,0:T(8,128)(2,1)S(1)}, bf16[2048,128]{1,0:T(8,128)(2,1)}, u32[]{:S(2)}) copy-start(bf16[2048,128]{1,0:T(8,128)(2,1)} %refs_11_.1) | copy-start | bytes 1572868
  34.5 3.2 %collective-permute-start.20 = (bf16[4,256,256]{2,1,0:T(8,128)(2,1)S(1)}, bf16[4,256,256]{2,1,0:T(8,128)(2,1)S(1)}, u32[]{:S(2)}, u32[]{:S(2)}) collective-permute-start(bf16[4,256,256]{2,1,0:T(8,128)(2,1)S(1)} %get-tuple-element.21), channel_id=1, source_target_pairs={{0,1},{1,0},{2,3},{3,2},{4,5},{5,4},{6,7},{7,6},{8,9},{9,8},{10,11... | collective-permute-start | bytes 1572872 | tf_op jit(solution)/shard_map/ppermute | solution.py:246
  34.7 5.7 %collective-permute-start.13 = (bf16[64,128]{1,0:T(8,128)(2,1)S(1)}, bf16[64,128]{1,0:T(8,128)(2,1)S(1)}, u32[]{:S(2)}, u32[]{:S(2)}) collective-permute-start(bf16[64,128]{1,0:T(8,128)(2,1)S(1)} %get-tuple-element.34), channel_id=1, source_target_pairs={{0,9},{1,8},{2,11},{3,10},{4,13},{5,12},{6,15},{7,14},{8,1},{9,0},... | collective-permute-start | bytes 49160 | tf_op jit(solution)/shard_map/ppermute | solution.py:246
  36.2 4.7 %collective-permute-start.15 = (bf16[64,128]{1,0:T(8,128)(2,1)S(1)}, bf16[64,128]{1,0:T(8,128)(2,1)S(1)}, u32[]{:S(2)}, u32[]{:S(2)}) collective-permute-start(bf16[64,128]{1,0:T(8,128)(2,1)S(1)} %get-tuple-element.35), channel_id=1, source_target_pairs={{0,24},{1,25},{2,26},{3,27},{4,28},{5,29},{6,30},{7,31},{8,16},{9,... | collective-permute-start | bytes 49160 | tf_op jit(solution)/shard_map/ppermute | solution.py:246
  37.5 3.5 %collective-permute-start.14 = (bf16[64,128]{1,0:T(8,128)(2,1)S(1)}, bf16[64,128]{1,0:T(8,128)(2,1)S(1)}, u32[]{:S(2)}, u32[]{:S(2)}) collective-permute-start(bf16[64,128]{1,0:T(8,128)(2,1)S(1)} %get-tuple-element.36), channel_id=1, source_target_pairs={{0,17},{1,16},{2,19},{3,18},{4,21},{5,20},{6,23},{7,22},{8,25},{9,... | collective-permute-start | bytes 49160 | tf_op jit(solution)/shard_map/ppermute | solution.py:246
  37.8 20.2 %copy-start.1 = (bf16[4096,128]{1,0:T(8,128)(2,1)S(1)}, bf16[4096,128]{1,0:T(8,128)(2,1)}, u32[]{:S(2)}) copy-start(bf16[4096,128]{1,0:T(8,128)(2,1)} %feat_ref.1) | copy-start | bytes 3145732
  37.8 5.5 %collective-permute-start.21 = (bf16[256,256]{1,0:T(8,128)(2,1)S(1)}, bf16[256,256]{1,0:T(8,128)(2,1)S(1)}, u32[]{:S(2)}, u32[]{:S(2)}) collective-permute-start(bf16[256,256]{1,0:T(8,128)(2,1)S(1)} %get-tuple-element.26), channel_id=1, source_target_pairs={{0,3},{1,2},{2,1},{3,0},{4,7},{5,6},{6,5},{7,4},{8,11},{9,10},{10,... | collective-permute-start | bytes 393224 | tf_op jit(solution)/shard_map/ppermute | solution.py:246
  37.9 9.7 %collective-permute-start.23 = (bf16[256,256]{1,0:T(8,128)(2,1)S(1)}, bf16[256,256]{1,0:T(8,128)(2,1)S(1)}, u32[]{:S(2)}, u32[]{:S(2)}) collective-permute-start(bf16[256,256]{1,0:T(8,128)(2,1)S(1)} %get-tuple-element.27), channel_id=1, source_target_pairs={{0,6},{1,7},{2,4},{3,5},{4,2},{5,3},{6,0},{7,1},{8,14},{9,15},{10,... | collective-permute-start | bytes 393224 | tf_op jit(solution)/shard_map/ppermute | solution.py:246
  40.4 12.5 %collective-permute-start.22 = (bf16[256,256]{1,0:T(8,128)(2,1)S(1)}, bf16[256,256]{1,0:T(8,128)(2,1)S(1)}, u32[]{:S(2)}, u32[]{:S(2)}) collective-permute-start(bf16[256,256]{1,0:T(8,128)(2,1)S(1)} %get-tuple-element.28), channel_id=1, source_target_pairs={{0,5},{1,4},{2,7},{3,6},{4,1},{5,0},{6,3},{7,2},{8,13},{9,12},{10,... | collective-permute-start | bytes 393224 | tf_op jit(solution)/shard_map/ppermute | solution.py:246
  41.0 14.8 %collective-permute-start.18 = (bf16[64,128]{1,0:T(8,128)(2,1)S(1)}, bf16[64,128]{1,0:T(8,128)(2,1)S(1)}, u32[]{:S(2)}, u32[]{:S(2)}) collective-permute-start(bf16[64,128]{1,0:T(8,128)(2,1)S(1)} %fusion.10), channel_id=1, source_target_pairs={{0,6},{1,7},{2,4},{3,5},{4,2},{5,3},{6,0},{7,1},{8,14},{9,15},{10,... | collective-permute-start | bytes 49160 | tf_op jit(solution)/shard_map/ppermute | solution.py:246
  42.9 13.6 %collective-permute-start.17 = (bf16[64,128]{1,0:T(8,128)(2,1)S(1)}, bf16[64,128]{1,0:T(8,128)(2,1)S(1)}, u32[]{:S(2)}, u32[]{:S(2)}) collective-permute-start(bf16[64,128]{1,0:T(8,128)(2,1)S(1)} %fusion.10), channel_id=1, source_target_pairs={{0,5},{1,4},{2,7},{3,6},{4,1},{5,0},{6,3},{7,2},{8,13},{9,12},{10,... | collective-permute-start | bytes 49160 | tf_op jit(solution)/shard_map/ppermute | solution.py:246
  43.4 13.2 %collective-permute-start.16 = (bf16[64,128]{1,0:T(8,128)(2,1)S(1)}, bf16[64,128]{1,0:T(8,128)(2,1)S(1)}, u32[]{:S(2)}, u32[]{:S(2)}) collective-permute-start(bf16[64,128]{1,0:T(8,128)(2,1)S(1)} %fusion.10), channel_id=1, source_target_pairs={{0,3},{1,2},{2,1},{3,0},{4,7},{5,6},{6,5},{7,4},{8,11},{9,10},{10,... | collective-permute-start | bytes 49160 | tf_op jit(solution)/shard_map/ppermute | solution.py:246
  53.0 7.8 %collective-permute-start.26 = (bf16[256,256]{1,0:T(8,128)(2,1)S(1)}, bf16[256,256]{1,0:T(8,128)(2,1)S(1)}, u32[]{:S(2)}, u32[]{:S(2)}) collective-permute-start(bf16[256,256]{1,0:T(8,128)(2,1)S(1)} %fusion.3.refs_0_), channel_id=1, source_target_pairs={{0,24},{1,25},{2,26},{3,27},{4,28},{5,29},{6,30},{7,31},{8,16},{9,... | collective-permute-start | bytes 393224 | tf_op jit(solution)/shard_map/ppermute | solution.py:246
  55.4 7.7 %collective-permute-start.25 = (bf16[256,256]{1,0:T(8,128)(2,1)S(1)}, bf16[256,256]{1,0:T(8,128)(2,1)S(1)}, u32[]{:S(2)}, u32[]{:S(2)}) collective-permute-start(bf16[256,256]{1,0:T(8,128)(2,1)S(1)} %fusion.3.refs_0_), channel_id=1, source_target_pairs={{0,16},{1,17},{2,18},{3,19},{4,20},{5,21},{6,22},{7,23},{8,24},{9,... | collective-permute-start | bytes 393224 | tf_op jit(solution)/shard_map/ppermute | solution.py:246
  55.9 7.4 %collective-permute-start.24 = (bf16[256,256]{1,0:T(8,128)(2,1)S(1)}, bf16[256,256]{1,0:T(8,128)(2,1)S(1)}, u32[]{:S(2)}, u32[]{:S(2)}) collective-permute-start(bf16[256,256]{1,0:T(8,128)(2,1)S(1)} %fusion.3.refs_0_), channel_id=1, source_target_pairs={{0,8},{1,9},{2,10},{3,11},{4,12},{5,13},{6,14},{7,15},{8,0},{9,1},... | collective-permute-start | bytes 393224 | tf_op jit(solution)/shard_map/ppermute | solution.py:246
  56.5 1.5 %copy-start.5 = (s32[4096]{0:T(1024)S(1)}, s32[4096]{0:T(1024)}, u32[]{:S(2)}) copy-start(s32[4096]{0:T(1024)} %param.14) | copy-start | bytes 49156
  56.6 1.4 %copy-start.6 = (s32[32]{0:T(128)S(1)}, s32[32]{0:T(128)}, u32[]{:S(2)}) copy-start(s32[32]{0:T(128)} %owners_ref.1) | copy-start | bytes 388
  56.6 1.4 %collective-permute-start.19 = (bf16[4,64,128]{2,1,0:T(8,128)(2,1)S(1)}, bf16[4,64,128]{2,1,0:T(8,128)(2,1)S(1)}, u32[]{:S(2)}, u32[]{:S(2)}) collective-permute-start(bf16[4,64,128]{2,1,0:T(8,128)(2,1)S(1)} %pad_maximum_fusion.4.near), channel_id=1, source_target_pairs={{0,1},{1,0},{2,3},{3,2},{4,5},{5,4},{6,7},{7,6},{8,9},{9,8},{10,11... | collective-permute-start | bytes 196616 | tf_op jit(solution)/shard_map/ppermute | solution.py:246

commit v4 on v3

--- a/solution.py
+++ b/solution.py
@@ -144,7 +144,7 @@
     for k in range(pairs):
         chunk = pl.ds(pl.multiple_of((pair ^ k) * (2 * rows), 2 * rows), 2 * rows)
         term[...] = contract(hid[:, chunk], q_grad, 0, 0)
-        mine = core ^ odd(k)
+        mine = 1 ^ core ^ odd(k)
         keep_ref[k] = term[pl.ds(pl.multiple_of(mine * rows, rows), rows), :].astype(BF16)
         give_ref[k] = term[pl.ds(pl.multiple_of((1 - mine) * rows, rows), rows), :].astype(BF16)
 
@@ -285,7 +285,7 @@
     first = jnp.concatenate(first)
     joined = keep + got.astype(F32)
     sums = joined[0]
-    for k in range(1, pairs):
+    for k in [2, 1, *range(3, pairs)]:
         sums = sums + swap(joined[k].astype(BF16), 0, chip(k)).astype(F32)
     second = swap(first, 0, chip(1))
     far_first = swap(first, 0, 1)
@@ -295,7 +295,7 @@
         [sums[:, :channels] / jnp.maximum(counts, 1.0), sums[:, channels : 2 * channels]], axis=1
     ).astype(BF16)
     pooled = [pooled] + [swap(pooled, k, odd(k)) for k in range(1, parts)]
-    second, pooled[-1] = lax.optimization_barrier((second, pooled[-1]))
+    second, pooled = lax.optimization_barrier((second, pooled))
     near = jnp.concatenate([first, second])
     far = jnp.concatenate([far_first, swap(second, 0, 1)])
 
@@ -305,20 +305,21 @@
     unpooled = up[0].astype(F32)
     for k in range(1, parts):
         unpooled = unpooled + swap(up[k], k, odd(k)).astype(F32)
-    unpooled = unpooled.astype(BF16)
-    near = jnp.stack([unpooled] + [swap(unpooled, 0, chip(k)) for k in range(1, pairs)])
+    near = unpooled.astype(BF16)[None]
+    for k in [1 << i for i in range(pairs.bit_length() - 1)]:
+        near = jnp.concatenate([near, swap(near, 0, chip(k))])
     far = swap(near, 0, 1)
     particle_out = unpool(particles, clusters, owners, near, far)
 
     grad = joined[0]
-    for k in range(1, pairs):
+    for k in [pairs - 1, *range(1, pairs - 1)]:
         grad = grad + swap(joined[k].astype(BF16), 0, chip(k)).astype(F32)
     if n_group > parts:
         part_sum = grad.astype(BF16)
         for k in range(1, n_group // parts):
             grad = grad + swap(part_sum, k * parts, 0).astype(F32)
     grad = grad.astype(BF16)
-    qk_grad = spread([grad] + [swap(grad, k, 0) for k in range(1, parts)])
+    qk_grad = spread([swap(grad, k, 1) for k in range(parts)])
     return (particle_out, qk_grad)
 
 

time: 64.5 us -> 61.3 us (0.950)
  starting transfers between devices: 32.7 us -> 30.4 us
  waiting for transfers between devices: 19.8 us -> 18.7 us
    ppermute x27, starting transfers between devices: 32.7 us -> 30.4 us  [swap(): return lax.ppermute(x, ('group', 'shard'), pairs)]
    ppermute x27, waiting for transfers between devices: 19.8 us -> 18.7 us  [swap(): return lax.ppermute(x, ('group', 'shard'), pairs)]
  transfers between devices with their start and end apart: 27 -> 27, of which waited for: 13 -> 11; matrix products, arithmetic and copies ran while one was open for 1% -> 1% of each run, Pallas kernels for 9% -> 10%
where the time goes in v4:
time: 61.3 us; the launch traced here: 61.1 us
  starting transfers between devices  30.4 us (50%)
  waiting for transfers between devices  18.7 us (31%)
  Pallas kernels  10.2 us (17%)
  between operations  0.87 us (1%)
  other arithmetic  0.66 us (1%)
    ppermute x27, starting transfers between devices, swap(): return lax.ppermute(x, ('group', 'shard'), pairs)  30.4 us
    ppermute x27, waiting for transfers between devices, swap(): return lax.ppermute(x, ('group', 'shard'), pairs)  18.7 us
    pallas_call x1, Pallas kernels, attend(): pl.pallas_call(functools.partial(attend_kernel, parts), in_specs=[VMEM] *...  3.2 us
    pallas_call x1, Pallas kernels, pool(): pl.pallas_call(pool_kernel, in_specs=[whole] * 4, out_specs=[VMEM, VMEM],...  3.09 us
    pallas_call x1, Pallas kernels, unpool(): pl.pallas_call(unpool_kernel, grid_spec=pltpu.PrefetchScalarGridSpec(num_...  2.83 us
  transfers between devices with their start and end apart: 27, of which 11 were waited for; matrix products, arithmetic and copies ran while one was open for 1% of the time, Pallas kernels for 10%

profile of v4, /device:TPU:0, one launch (start us, length us, event | category | flops | bytes accessed | tf_op | source)
XLA Modules:
  0.0 61.1 jit_solution(15297485256604611297)
XLA Ops:
  0.6 2.4 %collective-permute-start.2 = (bf16[1,64,2048]{2,1,0:T(8,128)(2,1)}, bf16[1,64,2048]{2,1,0:T(8,128)(2,1)S(1)}, u32[]{:S(2)}, u32[]{:S(2)}) collective-permute-start(bf16[1,64,2048]{2,1,0:T(8,128)(2,1)} %bitcast.50), channel_id=1, source_target_pairs={{0,9},{1,8},{2,11},{3,10},{4,13},{5,12},{6,15},{7,14},{8,1},{9,0},... | collective-permute-start | bytes 786440 | tf_op jit(solution)/shard_map/ppermute | solution.py:246
  3.1 2.9 %collective-permute-start.1 = (bf16[1,256,256]{2,1,0:T(8,128)(2,1)S(1)}, bf16[1,256,256]{2,1,0:T(8,128)(2,1)S(1)}, u32[]{:S(2)}, u32[]{:S(2)}) collective-permute-start(bf16[1,256,256]{2,1,0:T(8,128)(2,1)S(1)} %dynamic-slice_bitcast_fusion), channel_id=1, source_target_pairs={{0,5},{1,4},{2,7},{3,6},{4,1},{5,0},{6,3},{7,2},{8,13},{9,12},{10,... | collective-permute-start | bytes 393224 | tf_op jit(solution)/shard_map/ppermute | solution.py:246
  6.0 3.1 %pool.1 = (f32[4,64,384]{2,1,0:T(8,128)}, bf16[4,64,384]{2,1,0:T(8,128)(2,1)}) custom-call(s32[32]{0:T(128)} %owners_ref.1, s32[32,128]{1,0:T(8,128)} %bitcast.53, bf16[4096,128]{1,0:T(8,128)(2,1)} %feat_ref.1, bf16[4096,128]{1,0:T(8,128)(2,1)} %grad_hbm.1), custom_call_target="tpu_custom_call" | custom-call | tf_op jit(solution)/shard_map/pool/pallas_call | solution.py:65
  9.2 0.1 collective-permute-start
  9.2 0.8 %collective-permute-done.2 = bf16[1,64,2048]{2,1,0:T(8,128)(2,1)S(1)} collective-permute-done((bf16[1,64,2048]{2,1,0:T(8,128)(2,1)}, bf16[1,64,2048]{2,1,0:T(8,128)(2,1)S(1)}, u32[]{:S(2)}, u32[]{:S(2)}) %collective-permute-start.2) | collective-permute-done | bytes 262176 | tf_op jit(solution)/shard_map/ppermute | solution.py:246
  10.1 0.1 pad_maximum_fusion
  10.1 2.2 %collective-permute-start.3 = (bf16[2,64,2048]{2,1,0:T(8,128)(2,1)S(1)}, bf16[2,64,2048]{2,1,0:T(8,128)(2,1)S(1)}, u32[]{:S(2)}, u32[]{:S(2)}) collective-permute-start(bf16[2,64,2048]{2,1,0:T(8,128)(2,1)S(1)} %pad_maximum_fusion), channel_id=1, source_target_pairs={{0,17},{1,16},{2,19},{3,18},{4,21},{5,20},{6,23},{7,22},{8,25},{9,... | collective-permute-start | bytes 1572872 | tf_op jit(solution)/shard_map/ppermute | solution.py:246
  12.3 0.1 fusion.13
  12.4 2.6 %collective-permute-start.5 = (bf16[64,384]{1,0:T(8,128)(2,1)S(1)}, bf16[64,384]{1,0:T(8,128)(2,1)S(1)}, u32[]{:S(2)}, u32[]{:S(2)}) collective-permute-start(bf16[64,384]{1,0:T(8,128)(2,1)S(1)} %get-tuple-element.37), channel_id=1, source_target_pairs={{0,5},{1,4},{2,7},{3,6},{4,1},{5,0},{6,3},{7,2},{8,13},{9,12},{10,... | collective-permute-start | bytes 147464 | tf_op jit(solution)/shard_map/ppermute | solution.py:246
  15.1 1.3 %collective-permute-start.7 = (bf16[64,384]{1,0:T(8,128)(2,1)S(1)}, bf16[64,384]{1,0:T(8,128)(2,1)S(1)}, u32[]{:S(2)}, u32[]{:S(2)}) collective-permute-start(bf16[64,384]{1,0:T(8,128)(2,1)S(1)} %get-tuple-element.38), channel_id=1, source_target_pairs={{0,6},{1,7},{2,4},{3,5},{4,2},{5,3},{6,0},{7,1},{8,14},{9,15},{10,... | collective-permute-start | bytes 147464 | tf_op jit(solution)/shard_map/ppermute | solution.py:246
  16.4 0.2 collective-permute-start.6
  16.6 1.7 %collective-permute-start.4 = (bf16[2,256,256]{2,1,0:T(8,128)(2,1)S(1)}, bf16[2,256,256]{2,1,0:T(8,128)(2,1)S(1)}, u32[]{:S(2)}, u32[]{:S(2)}) collective-permute-start(bf16[2,256,256]{2,1,0:T(8,128)(2,1)S(1)} %pad_maximum_fusion.3), channel_id=1, source_target_pairs={{0,3},{1,2},{2,1},{3,0},{4,7},{5,6},{6,5},{7,4},{8,11},{9,10},{10,... | collective-permute-start | bytes 786440 | tf_op jit(solution)/shard_map/ppermute | solution.py:246
  18.3 3.2 %collective-permute-done.7 = bf16[64,384]{1,0:T(8,128)(2,1)S(1)} collective-permute-done((bf16[64,384]{1,0:T(8,128)(2,1)S(1)}, bf16[64,384]{1,0:T(8,128)(2,1)S(1)}, u32[]{:S(2)}, u32[]{:S(2)}) %collective-permute-start.7) | collective-permute-done | bytes 49184 | tf_op jit(solution)/shard_map/ppermute | solution.py:246
  21.4 0.1 collective-permute-done.6
  21.5 0.1 slice_reduce_fusion
  21.7 0.1 fusion.7
  21.8 2.0 %collective-permute-start.10 = (bf16[64,256]{1,0:T(8,128)(2,1)S(1)}, bf16[64,256]{1,0:T(8,128)(2,1)S(1)}, u32[]{:S(2)}, u32[]{:S(2)}) collective-permute-start(bf16[64,256]{1,0:T(8,128)(2,1)S(1)} %pad_maximum_fusion.5.refs_4_), channel_id=1, source_target_pairs={{0,24},{1,25},{2,26},{3,27},{4,28},{5,29},{6,30},{7,31},{8,16},{9,... | collective-permute-start | bytes 98312 | tf_op jit(solution)/shard_map/ppermute | solution.py:246
  23.8 0.5 collective-permute-start.9
  24.3 0.8 %collective-permute-start.8 = (bf16[64,256]{1,0:T(8,128)(2,1)S(1)}, bf16[64,256]{1,0:T(8,128)(2,1)S(1)}, u32[]{:S(2)}, u32[]{:S(2)}) collective-permute-start(bf16[64,256]{1,0:T(8,128)(2,1)S(1)} %pad_maximum_fusion.5.refs_4_), channel_id=1, source_target_pairs={{0,9},{1,8},{2,11},{3,10},{4,13},{5,12},{6,15},{7,14},{8,1},{9,0},... | collective-permute-start | bytes 98312 | tf_op jit(solution)/shard_map/ppermute | solution.py:246
  25.0 1.6 %collective-permute-done.10.refs_7_ = bf16[64,256]{1,0:T(8,128)(2,1)S(1)} collective-permute-done((bf16[64,256]{1,0:T(8,128)(2,1)S(1)}, bf16[64,256]{1,0:T(8,128)(2,1)S(1)}, u32[]{:S(2)}, u32[]{:S(2)}) %collective-permute-start.10) | collective-permute-done | bytes 32800 | tf_op jit(solution)/shard_map/ppermute | solution.py:246
  26.7 0.8 %collective-permute-done.9.refs_6_ = bf16[64,256]{1,0:T(8,128)(2,1)S(1)} collective-permute-done((bf16[64,256]{1,0:T(8,128)(2,1)S(1)}, bf16[64,256]{1,0:T(8,128)(2,1)S(1)}, u32[]{:S(2)}, u32[]{:S(2)}) %collective-permute-start.9) | collective-permute-done | bytes 32800 | tf_op jit(solution)/shard_map/ppermute | solution.py:246
  27.4 0.2 collective-permute-done.8.refs_5_
  27.6 0.7 %collective-permute-start.12 = (bf16[2,256,256]{2,1,0:T(8,128)(2,1)S(1)}, bf16[2,256,256]{2,1,0:T(8,128)(2,1)S(1)}, u32[]{:S(2)}, u32[]{:S(2)}) collective-permute-start(bf16[2,256,256]{2,1,0:T(8,128)(2,1)S(1)} %collective-permute-done.4), channel_id=1, source_target_pairs={{0,1},{1,0},{2,3},{3,2},{4,5},{5,4},{6,7},{7,6},{8,9},{9,8},{10,11... | collective-permute-start | bytes 786440 | tf_op jit(solution)/shard_map/ppermute | solution.py:246
  28.3 0.1 pad_maximum_fusion.1.refs_8_
  28.4 1.0 %collective-permute-done.12 = bf16[2,256,256]{2,1,0:T(8,128)(2,1)S(1)} collective-permute-done((bf16[2,256,256]{2,1,0:T(8,128)(2,1)S(1)}, bf16[2,256,256]{2,1,0:T(8,128)(2,1)S(1)}, u32[]{:S(2)}, u32[]{:S(2)}) %collective-permute-start.12) | collective-permute-done | bytes 262176 | tf_op jit(solution)/shard_map/ppermute | solution.py:246
  29.5 0.1 copy-done.4
  29.6 3.2 %attend.1 = (bf16[4,64,128]{2,1,0:T(8,128)(2,1)S(1)}, bf16[4,256,256]{2,1,0:T(8,128)(2,1)S(1)}, bf16[4,256,256]{2,1,0:T(8,128)(2,1)S(1)}) custom-call(bf16[64,2048]{1,0:T(8,128)(2,1)S(1)} %copy-done.2, bf16[64,2048]{1,0:T(8,128)(2,1)S(1)} %bitcast.52, bf16[64,2048]{1,0:T(8,128)(2,1)S(1)} %get-tuple-element.36.refs_2_, ...), custom_call_target="tpu_custom_call" | custom-call | tf_op jit(solution)/shard_map/attend/pallas_call | solution.py:158
  32.8 0.4 collective-permute-start.19
  33.2 0.5 collective-permute-start.13
  33.7 1.8 %collective-permute-start.15 = (bf16[64,128]{1,0:T(8,128)(2,1)S(1)}, bf16[64,128]{1,0:T(8,128)(2,1)S(1)}, u32[]{:S(2)}, u32[]{:S(2)}) collective-permute-start(bf16[64,128]{1,0:T(8,128)(2,1)S(1)} %get-tuple-element.41), channel_id=1, source_target_pairs={{0,24},{1,25},{2,26},{3,27},{4,28},{5,29},{6,30},{7,31},{8,16},{9,... | collective-permute-start | bytes 49160 | tf_op jit(solution)/shard_map/ppermute | solution.py:246
  35.4 0.7 %collective-permute-start.14 = (bf16[64,128]{1,0:T(8,128)(2,1)S(1)}, bf16[64,128]{1,0:T(8,128)(2,1)S(1)}, u32[]{:S(2)}, u32[]{:S(2)}) collective-permute-start(bf16[64,128]{1,0:T(8,128)(2,1)S(1)} %get-tuple-element.42), channel_id=1, source_target_pairs={{0,17},{1,16},{2,19},{3,18},{4,21},{5,20},{6,23},{7,22},{8,25},{9,... | collective-permute-start | bytes 49160 | tf_op jit(solution)/shard_map/ppermute | solution.py:246
  36.1 0.1 fusion.12
  36.3 2.6 %collective-permute-start.20 = (bf16[256,256]{1,0:T(8,128)(2,1)S(1)}, bf16[256,256]{1,0:T(8,128)(2,1)S(1)}, u32[]{:S(2)}, u32[]{:S(2)}) collective-permute-start(bf16[256,256]{1,0:T(8,128)(2,1)S(1)} %get-tuple-element.32), channel_id=1, source_target_pairs={{0,6},{1,7},{2,4},{3,5},{4,2},{5,3},{6,0},{7,1},{8,14},{9,15},{10,... | collective-permute-start | bytes 393224 | tf_op jit(solution)/shard_map/ppermute | solution.py:246
  38.9 1.6 %collective-permute-start.21 = (bf16[256,256]{1,0:T(8,128)(2,1)S(1)}, bf16[256,256]{1,0:T(8,128)(2,1)S(1)}, u32[]{:S(2)}, u32[]{:S(2)}) collective-permute-start(bf16[256,256]{1,0:T(8,128)(2,1)S(1)} %get-tuple-element.34), channel_id=1, source_target_pairs={{0,3},{1,2},{2,1},{3,0},{4,7},{5,6},{6,5},{7,4},{8,11},{9,10},{10,... | collective-permute-start | bytes 393224 | tf_op jit(solution)/shard_map/ppermute | solution.py:246
  40.5 0.2 collective-permute-start.16
  40.7 7.6 %collective-permute-done.16 = bf16[1,64,128]{2,1,0:T(8,128)(2,1)S(1)} collective-permute-done((bf16[1,64,128]{2,1,0:T(8,128)(2,1)S(1)}, bf16[1,64,128]{2,1,0:T(8,128)(2,1)S(1)}, u32[]{:S(2)}, u32[]{:S(2)}) %collective-permute-start.16) | collective-permute-done | bytes 16416 | tf_op jit(solution)/shard_map/ppermute | solution.py:246
  48.4 1.7 %collective-permute-start.17 = (bf16[2,64,128]{2,1,0:T(8,128)(2,1)S(1)}, bf16[2,64,128]{2,1,0:T(8,128)(2,1)S(1)}, u32[]{:S(2)}, u32[]{:S(2)}) collective-permute-start(bf16[2,64,128]{2,1,0:T(8,128)(2,1)S(1)} %pad_maximum_fusion.6), channel_id=1, source_target_pairs={{0,5},{1,4},{2,7},{3,6},{4,1},{5,0},{6,3},{7,2},{8,13},{9,12},{10,... | collective-permute-start | bytes 98312 | tf_op jit(solution)/shard_map/ppermute | solution.py:246
  50.1 0.3 collective-permute-done.22
  50.4 0.1 fusion.3
  50.5 1.7 %collective-permute-start.26 = (bf16[256,256]{1,0:T(8,128)(2,1)S(1)}, bf16[256,256]{1,0:T(8,128)(2,1)S(1)}, u32[]{:S(2)}, u32[]{:S(2)}) collective-permute-start(bf16[256,256]{1,0:T(8,128)(2,1)S(1)} %fusion.3), channel_id=1, source_target_pairs={{0,25},{1,24},{2,27},{3,26},{4,29},{5,28},{6,31},{7,30},{8,17},{9,... | collective-permute-start | bytes 393224 | tf_op jit(solution)/shard_map/ppermute | solution.py:246
  52.2 0.5 collective-permute-start.25
  52.7 0.8 %collective-permute-start.24 = (bf16[256,256]{1,0:T(8,128)(2,1)S(1)}, bf16[256,256]{1,0:T(8,128)(2,1)S(1)}, u32[]{:S(2)}, u32[]{:S(2)}) collective-permute-start(bf16[256,256]{1,0:T(8,128)(2,1)S(1)} %fusion.3), channel_id=1, source_target_pairs={{0,9},{1,8},{2,11},{3,10},{4,13},{5,12},{6,15},{7,14},{8,1},{9,0},... | collective-permute-start | bytes 393224 | tf_op jit(solution)/shard_map/ppermute | solution.py:246
  53.5 0.4 collective-permute-start.23
  53.9 0.1 collective-permute-start.18
  54.1 1.2 %collective-permute-done.18.far = bf16[4,64,128]{2,1,0:T(8,128)(2,1)S(1)} collective-permute-done((bf16[4,64,128]{2,1,0:T(8,128)(2,1)S(1)}, bf16[4,64,128]{2,1,0:T(8,128)(2,1)S(1)}, u32[]{:S(2)}, u32[]{:S(2)}) %collective-permute-start.18) | collective-permute-done | bytes 65568 | tf_op jit(solution)/shard_map/ppermute | solution.py:246
  55.3 2.8 %unpool.1 = bf16[4096,128]{1,0:T(8,128)(2,1)} custom-call(s32[32]{0:T(128)S(1)} %copy-done.6, s32[32,128]{1,0:T(8,128)S(1)} %bitcast.54, bf16[4096,128]{1,0:T(8,128)(2,1)S(1)} %copy-done.1, bf16[4,64,128]{2,1,0:T(8,128)(2,1)S(1)} %pad_maximum_fusion.4.near, bf16[4,64,128]{2,1,0:T(8,128)(2,1)S(1)} %collective-permute-done.18.far), custom_call_target="tpu_custom_call" | custom-call | tf_op jit(solution)/shard_map/unpool/pallas_call | solution.py:202
  58.1 1.9 %collective-permute-done.25.refs_2_ = bf16[256,256]{1,0:T(8,128)(2,1)S(1)} collective-permute-done((bf16[256,256]{1,0:T(8,128)(2,1)S(1)}, bf16[256,256]{1,0:T(8,128)(2,1)S(1)}, u32[]{:S(2)}, u32[]{:S(2)}) %collective-permute-start.25) | collective-permute-done | bytes 131104 | tf_op jit(solution)/shard_map/ppermute | solution.py:246
  60.0 1.1 %spread.1 = f32[256,1024]{1,0:T(8,128)} custom-call(bf16[256,256]{1,0:T(8,128)(2,1)S(1)} %collective-permute-done.23.refs_0_, bf16[256,256]{1,0:T(8,128)(2,1)S(1)} %collective-permute-done.24.refs_1_, bf16[256,256]{1,0:T(8,128)(2,1)S(1)} %collective-permute-done.25.refs_2_, bf16[256,256]{1,0:T(8,128)(2,1)S(1)} %collective-permute-done.26.refs_3_), custom_call_target="tpu_custom_call" | custom-call | tf_op jit(solution)/shard_map/spread/pallas_call | solution.py:232
  (47 shorter events, 0.3 us)
Async XLA Ops:
  0.6 2.5 %copy-start = (bf16[256,1024]{1,0:T(8,128)(2,1)S(1)}, bf16[256,1024]{1,0:T(8,128)(2,1)}, u32[]{:S(2)}) copy-start(bf16[256,1024]{1,0:T(8,128)(2,1)} %param.9) | copy-start | bytes 1572868
  0.6 9.4 %collective-permute-start.2 = (bf16[1,64,2048]{2,1,0:T(8,128)(2,1)}, bf16[1,64,2048]{2,1,0:T(8,128)(2,1)S(1)}, u32[]{:S(2)}, u32[]{:S(2)}) collective-permute-start(bf16[1,64,2048]{2,1,0:T(8,128)(2,1)} %bitcast.50), channel_id=1, source_target_pairs={{0,9},{1,8},{2,11},{3,10},{4,13},{5,12},{6,15},{7,14},{8,1},{9,0},... | collective-permute-start | bytes 786440 | tf_op jit(solution)/shard_map/ppermute | solution.py:246
  3.1 9.2 %collective-permute-start.1 = (bf16[1,256,256]{2,1,0:T(8,128)(2,1)S(1)}, bf16[1,256,256]{2,1,0:T(8,128)(2,1)S(1)}, u32[]{:S(2)}, u32[]{:S(2)}) collective-permute-start(bf16[1,256,256]{2,1,0:T(8,128)(2,1)S(1)} %dynamic-slice_bitcast_fusion), channel_id=1, source_target_pairs={{0,5},{1,4},{2,7},{3,6},{4,1},{5,0},{6,3},{7,2},{8,13},{9,12},{10,... | collective-permute-start | bytes 393224 | tf_op jit(solution)/shard_map/ppermute | solution.py:246
  6.0 4.0 %copy-start.2 = (bf16[64,2048]{1,0:T(8,128)(2,1)S(1)}, bf16[64,2048]{1,0:T(8,128)(2,1)}, u32[]{:S(2)}) copy-start(bf16[64,2048]{1,0:T(8,128)(2,1)} %refs_0_.1) | copy-start | bytes 786436
  9.1 3.2 %copy-start.7 = (f32[4,64,384]{2,1,0:T(8,128)S(1)}, f32[4,64,384]{2,1,0:T(8,128)}, u32[]{:S(2)}) copy-start(f32[4,64,384]{2,1,0:T(8,128)} %get-tuple-element.18) | copy-start | bytes 1179652
  9.2 3.2 %collective-permute-start = (bf16[4,64,384]{2,1,0:T(8,128)(2,1)}, bf16[4,64,384]{2,1,0:T(8,128)(2,1)S(1)}, u32[]{:S(2)}, u32[]{:S(2)}) collective-permute-start(bf16[4,64,384]{2,1,0:T(8,128)(2,1)} %get-tuple-element.15), channel_id=1, source_target_pairs={{0,1},{1,0},{2,3},{3,2},{4,5},{5,4},{6,7},{7,6},{8,9},{9,8},{10,11... | collective-permute-start | bytes 589832 | tf_op jit(solution)/shard_map/ppermute | solution.py:246
  10.1 18.2 %collective-permute-start.3 = (bf16[2,64,2048]{2,1,0:T(8,128)(2,1)S(1)}, bf16[2,64,2048]{2,1,0:T(8,128)(2,1)S(1)}, u32[]{:S(2)}, u32[]{:S(2)}) collective-permute-start(bf16[2,64,2048]{2,1,0:T(8,128)(2,1)S(1)} %pad_maximum_fusion), channel_id=1, source_target_pairs={{0,17},{1,16},{2,19},{3,18},{4,21},{5,20},{6,23},{7,22},{8,25},{9,... | collective-permute-start | bytes 1572872 | tf_op jit(solution)/shard_map/ppermute | solution.py:246
  12.4 5.8 %collective-permute-start.5 = (bf16[64,384]{1,0:T(8,128)(2,1)S(1)}, bf16[64,384]{1,0:T(8,128)(2,1)S(1)}, u32[]{:S(2)}, u32[]{:S(2)}) collective-permute-start(bf16[64,384]{1,0:T(8,128)(2,1)S(1)} %get-tuple-element.37), channel_id=1, source_target_pairs={{0,5},{1,4},{2,7},{3,6},{4,1},{5,0},{6,3},{7,2},{8,13},{9,12},{10,... | collective-permute-start | bytes 147464 | tf_op jit(solution)/shard_map/ppermute | solution.py:246
  15.1 6.3 %collective-permute-start.7 = (bf16[64,384]{1,0:T(8,128)(2,1)S(1)}, bf16[64,384]{1,0:T(8,128)(2,1)S(1)}, u32[]{:S(2)}, u32[]{:S(2)}) collective-permute-start(bf16[64,384]{1,0:T(8,128)(2,1)S(1)} %get-tuple-element.38), channel_id=1, source_target_pairs={{0,6},{1,7},{2,4},{3,5},{4,2},{5,3},{6,0},{7,1},{8,14},{9,15},{10,... | collective-permute-start | bytes 147464 | tf_op jit(solution)/shard_map/ppermute | solution.py:246
  16.4 5.1 %collective-permute-start.6 = (bf16[64,384]{1,0:T(8,128)(2,1)S(1)}, bf16[64,384]{1,0:T(8,128)(2,1)S(1)}, u32[]{:S(2)}, u32[]{:S(2)}) collective-permute-start(bf16[64,384]{1,0:T(8,128)(2,1)S(1)} %get-tuple-element.39), channel_id=1, source_target_pairs={{0,3},{1,2},{2,1},{3,0},{4,7},{5,6},{6,5},{7,4},{8,11},{9,10},{10,... | collective-permute-start | bytes 147464 | tf_op jit(solution)/shard_map/ppermute | solution.py:246
  16.6 11.0 %collective-permute-start.4 = (bf16[2,256,256]{2,1,0:T(8,128)(2,1)S(1)}, bf16[2,256,256]{2,1,0:T(8,128)(2,1)S(1)}, u32[]{:S(2)}, u32[]{:S(2)}) collective-permute-start(bf16[2,256,256]{2,1,0:T(8,128)(2,1)S(1)} %pad_maximum_fusion.3), channel_id=1, source_target_pairs={{0,3},{1,2},{2,1},{3,0},{4,7},{5,6},{6,5},{7,4},{8,11},{9,10},{10,... | collective-permute-start | bytes 786440 | tf_op jit(solution)/shard_map/ppermute | solution.py:246
  21.8 4.9 %collective-permute-start.10 = (bf16[64,256]{1,0:T(8,128)(2,1)S(1)}, bf16[64,256]{1,0:T(8,128)(2,1)S(1)}, u32[]{:S(2)}, u32[]{:S(2)}) collective-permute-start(bf16[64,256]{1,0:T(8,128)(2,1)S(1)} %pad_maximum_fusion.5.refs_4_), channel_id=1, source_target_pairs={{0,24},{1,25},{2,26},{3,27},{4,28},{5,29},{6,30},{7,31},{8,16},{9,... | collective-permute-start | bytes 98312 | tf_op jit(solution)/shard_map/ppermute | solution.py:246
  23.8 3.7 %collective-permute-start.9 = (bf16[64,256]{1,0:T(8,128)(2,1)S(1)}, bf16[64,256]{1,0:T(8,128)(2,1)S(1)}, u32[]{:S(2)}, u32[]{:S(2)}) collective-permute-start(bf16[64,256]{1,0:T(8,128)(2,1)S(1)} %pad_maximum_fusion.5.refs_4_), channel_id=1, source_target_pairs={{0,17},{1,16},{2,19},{3,18},{4,21},{5,20},{6,23},{7,22},{8,25},{9,... | collective-permute-start | bytes 98312 | tf_op jit(solution)/shard_map/ppermute | solution.py:246
  24.3 3.3 %collective-permute-start.8 = (bf16[64,256]{1,0:T(8,128)(2,1)S(1)}, bf16[64,256]{1,0:T(8,128)(2,1)S(1)}, u32[]{:S(2)}, u32[]{:S(2)}) collective-permute-start(bf16[64,256]{1,0:T(8,128)(2,1)S(1)} %pad_maximum_fusion.5.refs_4_), channel_id=1, source_target_pairs={{0,9},{1,8},{2,11},{3,10},{4,13},{5,12},{6,15},{7,14},{8,1},{9,0},... | collective-permute-start | bytes 98312 | tf_op jit(solution)/shard_map/ppermute | solution.py:246
  26.6 1.8 %collective-permute-start.11 = (bf16[2,256,256]{2,1,0:T(8,128)(2,1)S(1)}, bf16[2,256,256]{2,1,0:T(8,128)(2,1)S(1)}, u32[]{:S(2)}, u32[]{:S(2)}) collective-permute-start(bf16[2,256,256]{2,1,0:T(8,128)(2,1)S(1)} %pad_maximum_fusion.3), channel_id=1, source_target_pairs={{0,1},{1,0},{2,3},{3,2},{4,5},{5,4},{6,7},{7,6},{8,9},{9,8},{10,11... | collective-permute-start | bytes 786440 | tf_op jit(solution)/shard_map/ppermute | solution.py:246
  27.6 1.8 %collective-permute-start.12 = (bf16[2,256,256]{2,1,0:T(8,128)(2,1)S(1)}, bf16[2,256,256]{2,1,0:T(8,128)(2,1)S(1)}, u32[]{:S(2)}, u32[]{:S(2)}) collective-permute-start(bf16[2,256,256]{2,1,0:T(8,128)(2,1)S(1)} %collective-permute-done.4), channel_id=1, source_target_pairs={{0,1},{1,0},{2,3},{3,2},{4,5},{5,4},{6,7},{7,6},{8,9},{9,8},{10,11... | collective-permute-start | bytes 786440 | tf_op jit(solution)/shard_map/ppermute | solution.py:246
  28.4 1.1 %copy-start.3 = (bf16[128,2048]{1,0:T(8,128)(2,1)S(1)}, bf16[128,2048]{1,0:T(8,128)(2,1)}, u32[]{:S(2)}) copy-start(bf16[128,2048]{1,0:T(8,128)(2,1)} %refs_10_.1) | copy-start | bytes 1572868
  28.4 1.2 %copy-start.4 = (bf16[2048,128]{1,0:T(8,128)(2,1)S(1)}, bf16[2048,128]{1,0:T(8,128)(2,1)}, u32[]{:S(2)}) copy-start(bf16[2048,128]{1,0:T(8,128)(2,1)} %refs_11_.1) | copy-start | bytes 1572868
  32.8 3.3 %collective-permute-start.19 = (bf16[4,256,256]{2,1,0:T(8,128)(2,1)S(1)}, bf16[4,256,256]{2,1,0:T(8,128)(2,1)S(1)}, u32[]{:S(2)}, u32[]{:S(2)}) collective-permute-start(bf16[4,256,256]{2,1,0:T(8,128)(2,1)S(1)} %get-tuple-element.27), channel_id=1, source_target_pairs={{0,1},{1,0},{2,3},{3,2},{4,5},{5,4},{6,7},{7,6},{8,9},{9,8},{10,11... | collective-permute-start | bytes 1572872 | tf_op jit(solution)/shard_map/ppermute | solution.py:246
  33.2 5.7 %collective-permute-start.13 = (bf16[64,128]{1,0:T(8,128)(2,1)S(1)}, bf16[64,128]{1,0:T(8,128)(2,1)S(1)}, u32[]{:S(2)}, u32[]{:S(2)}) collective-permute-start(bf16[64,128]{1,0:T(8,128)(2,1)S(1)} %get-tuple-element.40), channel_id=1, source_target_pairs={{0,9},{1,8},{2,11},{3,10},{4,13},{5,12},{6,15},{7,14},{8,1},{9,0},... | collective-permute-start | bytes 49160 | tf_op jit(solution)/shard_map/ppermute | solution.py:246
  33.7 6.8 %collective-permute-start.15 = (bf16[64,128]{1,0:T(8,128)(2,1)S(1)}, bf16[64,128]{1,0:T(8,128)(2,1)S(1)}, u32[]{:S(2)}, u32[]{:S(2)}) collective-permute-start(bf16[64,128]{1,0:T(8,128)(2,1)S(1)} %get-tuple-element.41), channel_id=1, source_target_pairs={{0,24},{1,25},{2,26},{3,27},{4,28},{5,29},{6,30},{7,31},{8,16},{9,... | collective-permute-start | bytes 49160 | tf_op jit(solution)/shard_map/ppermute | solution.py:246
  35.4 5.0 %collective-permute-start.14 = (bf16[64,128]{1,0:T(8,128)(2,1)S(1)}, bf16[64,128]{1,0:T(8,128)(2,1)S(1)}, u32[]{:S(2)}, u32[]{:S(2)}) collective-permute-start(bf16[64,128]{1,0:T(8,128)(2,1)S(1)} %get-tuple-element.42), channel_id=1, source_target_pairs={{0,17},{1,16},{2,19},{3,18},{4,21},{5,20},{6,23},{7,22},{8,25},{9,... | collective-permute-start | bytes 49160 | tf_op jit(solution)/shard_map/ppermute | solution.py:246
  36.2 19.0 %copy-start.1 = (bf16[4096,128]{1,0:T(8,128)(2,1)S(1)}, bf16[4096,128]{1,0:T(8,128)(2,1)}, u32[]{:S(2)}) copy-start(bf16[4096,128]{1,0:T(8,128)(2,1)} %feat_ref.1) | copy-start | bytes 3145732
  36.3 13.8 %collective-permute-start.20 = (bf16[256,256]{1,0:T(8,128)(2,1)S(1)}, bf16[256,256]{1,0:T(8,128)(2,1)S(1)}, u32[]{:S(2)}, u32[]{:S(2)}) collective-permute-start(bf16[256,256]{1,0:T(8,128)(2,1)S(1)} %get-tuple-element.32), channel_id=1, source_target_pairs={{0,6},{1,7},{2,4},{3,5},{4,2},{5,3},{6,0},{7,1},{8,14},{9,15},{10,... | collective-permute-start | bytes 393224 | tf_op jit(solution)/shard_map/ppermute | solution.py:246
  38.9 11.5 %collective-permute-start.22 = (bf16[256,256]{1,0:T(8,128)(2,1)S(1)}, bf16[256,256]{1,0:T(8,128)(2,1)S(1)}, u32[]{:S(2)}, u32[]{:S(2)}) collective-permute-start(bf16[256,256]{1,0:T(8,128)(2,1)S(1)} %get-tuple-element.33), channel_id=1, source_target_pairs={{0,5},{1,4},{2,7},{3,6},{4,1},{5,0},{6,3},{7,2},{8,13},{9,12},{10,... | collective-permute-start | bytes 393224 | tf_op jit(solution)/shard_map/ppermute | solution.py:246
  38.9 11.5 %collective-permute-start.21 = (bf16[256,256]{1,0:T(8,128)(2,1)S(1)}, bf16[256,256]{1,0:T(8,128)(2,1)S(1)}, u32[]{:S(2)}, u32[]{:S(2)}) collective-permute-start(bf16[256,256]{1,0:T(8,128)(2,1)S(1)} %get-tuple-element.34), channel_id=1, source_target_pairs={{0,3},{1,2},{2,1},{3,0},{4,7},{5,6},{6,5},{7,4},{8,11},{9,10},{10,... | collective-permute-start | bytes 393224 | tf_op jit(solution)/shard_map/ppermute | solution.py:246
  40.5 7.9 %collective-permute-start.16 = (bf16[1,64,128]{2,1,0:T(8,128)(2,1)S(1)}, bf16[1,64,128]{2,1,0:T(8,128)(2,1)S(1)}, u32[]{:S(2)}, u32[]{:S(2)}) collective-permute-start(bf16[1,64,128]{2,1,0:T(8,128)(2,1)S(1)} %fusion.11), channel_id=1, source_target_pairs={{0,3},{1,2},{2,1},{3,0},{4,7},{5,6},{6,5},{7,4},{8,11},{9,10},{10,... | collective-permute-start | bytes 49160 | tf_op jit(solution)/shard_map/ppermute | solution.py:246
  48.4 5.5 %collective-permute-start.17 = (bf16[2,64,128]{2,1,0:T(8,128)(2,1)S(1)}, bf16[2,64,128]{2,1,0:T(8,128)(2,1)S(1)}, u32[]{:S(2)}, u32[]{:S(2)}) collective-permute-start(bf16[2,64,128]{2,1,0:T(8,128)(2,1)S(1)} %pad_maximum_fusion.6), channel_id=1, source_target_pairs={{0,5},{1,4},{2,7},{3,6},{4,1},{5,0},{6,3},{7,2},{8,13},{9,12},{10,... | collective-permute-start | bytes 98312 | tf_op jit(solution)/shard_map/ppermute | solution.py:246
  50.5 4.8 %copy-start.5 = (s32[4096]{0:T(1024)S(1)}, s32[4096]{0:T(1024)}, u32[]{:S(2)}) copy-start(s32[4096]{0:T(1024)} %param.14) | copy-start | bytes 49156
  50.5 4.8 %copy-start.6 = (s32[32]{0:T(128)S(1)}, s32[32]{0:T(128)}, u32[]{:S(2)}) copy-start(s32[32]{0:T(128)} %owners_ref.1) | copy-start | bytes 388
  50.5 7.6 %collective-permute-start.26 = (bf16[256,256]{1,0:T(8,128)(2,1)S(1)}, bf16[256,256]{1,0:T(8,128)(2,1)S(1)}, u32[]{:S(2)}, u32[]{:S(2)}) collective-permute-start(bf16[256,256]{1,0:T(8,128)(2,1)S(1)} %fusion.3), channel_id=1, source_target_pairs={{0,25},{1,24},{2,27},{3,26},{4,29},{5,28},{6,31},{7,30},{8,17},{9,... | collective-permute-start | bytes 393224 | tf_op jit(solution)/shard_map/ppermute | solution.py:246
  52.2 7.8 %collective-permute-start.25 = (bf16[256,256]{1,0:T(8,128)(2,1)S(1)}, bf16[256,256]{1,0:T(8,128)(2,1)S(1)}, u32[]{:S(2)}, u32[]{:S(2)}) collective-permute-start(bf16[256,256]{1,0:T(8,128)(2,1)S(1)} %fusion.3), channel_id=1, source_target_pairs={{0,17},{1,16},{2,19},{3,18},{4,21},{5,20},{6,23},{7,22},{8,25},{9,... | collective-permute-start | bytes 393224 | tf_op jit(solution)/shard_map/ppermute | solution.py:246
  52.7 7.4 %collective-permute-start.24 = (bf16[256,256]{1,0:T(8,128)(2,1)S(1)}, bf16[256,256]{1,0:T(8,128)(2,1)S(1)}, u32[]{:S(2)}, u32[]{:S(2)}) collective-permute-start(bf16[256,256]{1,0:T(8,128)(2,1)S(1)} %fusion.3), channel_id=1, source_target_pairs={{0,9},{1,8},{2,11},{3,10},{4,13},{5,12},{6,15},{7,14},{8,1},{9,0},... | collective-permute-start | bytes 393224 | tf_op jit(solution)/shard_map/ppermute | solution.py:246
  53.5 6.5 %collective-permute-start.23 = (bf16[256,256]{1,0:T(8,128)(2,1)S(1)}, bf16[256,256]{1,0:T(8,128)(2,1)S(1)}, u32[]{:S(2)}, u32[]{:S(2)}) collective-permute-start(bf16[256,256]{1,0:T(8,128)(2,1)S(1)} %fusion.3), channel_id=1, source_target_pairs={{0,1},{1,0},{2,3},{3,2},{4,5},{5,4},{6,7},{7,6},{8,9},{9,8},{10,11... | collective-permute-start | bytes 393224 | tf_op jit(solution)/shard_map/ppermute | solution.py:246
  53.9 1.3 %collective-permute-start.18 = (bf16[4,64,128]{2,1,0:T(8,128)(2,1)S(1)}, bf16[4,64,128]{2,1,0:T(8,128)(2,1)S(1)}, u32[]{:S(2)}, u32[]{:S(2)}) collective-permute-start(bf16[4,64,128]{2,1,0:T(8,128)(2,1)S(1)} %pad_maximum_fusion.4.near), channel_id=1, source_target_pairs={{0,1},{1,0},{2,3},{3,2},{4,5},{5,4},{6,7},{7,6},{8,9},{9,8},{10,11... | collective-permute-start | bytes 196616 | tf_op jit(solution)/shard_map/ppermute | solution.py:246

commit v5 on v4

--- a/solution.py
+++ b/solution.py
@@ -79,23 +79,27 @@
     )(owners, clusters.reshape(num_blocks, rows), particles, cotangent)
 
 
-def attend_kernel(parts, *refs):
+def query_part(hid, near, far, pairs, begin, weight):
+    me = lax.axis_index("shard")
+    count, rows, _ = near.shape
+    total = None
+    for i in range(count):
+        mine = me ^ chip(reverse(begin + i, pairs))
+        core = lax.rem(mine, 2)
+        weight[i, pl.ds(pl.multiple_of(core * rows, rows), rows), :] = near[i]
+        weight[i, pl.ds(pl.multiple_of((1 - core) * rows, rows), rows), :] = far[i]
+        chunk = pl.ds(pl.multiple_of(lax.div(mine, 2) * (2 * rows), 2 * rows), 2 * rows)
+        term = jnp.dot(hid[:, chunk], weight[i], preferred_element_type=F32)
+        total = term if total is None else total + term
+    return total
+
+
+def hidden_kernel(parts, *refs):
     tok, pooled_refs = refs[:parts], refs[parts : 2 * parts]
-    near, far, w_in, w_out, up_ref, keep_ref, give_ref, weight, hid, term = refs[2 * parts :]
-    pairs, rows, cols = near.shape
+    near, far, w_in, hid, query, weight = refs[2 * parts :]
     t_rows, width = tok[0].shape
-    head_cols = cols * parts
     channels = w_in.shape[0]
-    group, me = lax.axis_index("group"), lax.axis_index("shard")
-    part = lax.rem(group, parts)
-    core = lax.rem(me, 2)
-    pair = lax.div(me, 2)
-    for k in range(pairs):
-        mine = me ^ chip(reverse(k, pairs))
-        weight[pl.ds(pl.multiple_of(mine * rows, rows), rows), :] = near[k]
-        weight[pl.ds(pl.multiple_of((mine ^ 1) * rows, rows), rows), :] = far[k]
     pooled = jnp.concatenate([r[:, :channels] for r in pooled_refs], axis=0)
-    pooled_grad = jnp.concatenate([r[:, channels:] for r in pooled_refs], axis=0)
     step = 512
     for n in range(0, width, step):
         wide = jnp.dot(pooled, w_in[:, n : n + step], preferred_element_type=F32)
@@ -104,14 +108,48 @@
             hid[span, n : n + step] = (
                 tok[k][:, n : n + step].astype(F32) + wide[span]
             ).astype(BF16)
-    queries = jnp.dot(hid[...], weight[...], preferred_element_type=F32).astype(BF16)
+    query[...] = query_part(hid, near, far, 2 * near.shape[0], 0, weight)
+
+
+def hidden(tok, pooled, near, far, w_in):
+    parts = len(tok)
+    t_rows, width = tok[0].shape
+    half, rows, cols = near.shape
+    return pl.pallas_call(
+        functools.partial(hidden_kernel, parts),
+        in_specs=[VMEM] * (2 * parts + 3),
+        out_specs=[VMEM] * 2,
+        out_shape=[
+            jax.ShapeDtypeStruct((parts * t_rows, width), BF16),
+            jax.ShapeDtypeStruct((parts * t_rows, cols), F32),
+        ],
+        scratch_shapes=[pltpu.VMEM((half, 2 * rows, cols), BF16)],
+        compiler_params=params(20),
+        name="hidden",
+    )(*tok, *pooled, near, far, w_in)
+
+
+def attend_kernel(parts, *refs):
+    pooled_refs = refs[:parts]
+    hid, query, near, far, w_out, up_ref, keep_ref, give_ref, weight, term = refs[parts:]
+    half_pairs, rows, cols = near.shape
+    pairs = 2 * half_pairs
+    total, width = hid.shape
+    t_rows = total // parts
+    head_cols = cols * parts
+    channels = w_out.shape[1]
+    group, me = lax.axis_index("group"), lax.axis_index("shard")
+    part = lax.rem(group, parts)
+    core = lax.rem(me, 2)
+    pair = lax.div(me, 2)
+    queries = (query[...] + query_part(hid, near, far, pairs, half_pairs, weight)).astype(BF16)
+    pooled_grad = jnp.concatenate([r[:, channels:] for r in pooled_refs], axis=0)
     first = pl.ds(pl.multiple_of(part * cols, cols), cols)
     values = hid[:, first]
     out_w = w_out[first, :]
     out_grad = contract(pooled_grad, out_w, 1, 1).astype(BF16)
     dim = head_cols // HEADS
     scale = 1.0 / math.sqrt(dim)
-    total = parts * t_rows
     row = lax.broadcasted_iota(jnp.int32, (total, total), 0)
     col = lax.broadcasted_iota(jnp.int32, (total, total), 1)
     same = lax.div(row, t_rows) == lax.div(col, t_rows)
@@ -149,25 +187,24 @@
         give_ref[k] = term[pl.ds(pl.multiple_of((1 - mine) * rows, rows), rows), :].astype(BF16)
 
 
-def attend(tok, pooled, near, far, w_in, w_out):
-    parts = len(tok)
-    t_rows, width = tok[0].shape
-    pairs, rows, cols = near.shape
-    channels = w_in.shape[0]
-    shape = jax.ShapeDtypeStruct((pairs, rows, cols), BF16)
+def attend(pooled, hid, query, near, far, w_out):
+    parts = len(pooled)
+    half, rows, cols = near.shape
+    channels = w_out.shape[1]
+    t_rows = pooled[0].shape[0]
+    shape = jax.ShapeDtypeStruct((2 * half, rows, cols), BF16)
     return pl.pallas_call(
         functools.partial(attend_kernel, parts),
-        in_specs=[VMEM] * (2 * parts + 4),
+        in_specs=[VMEM] * (parts + 5),
         out_specs=[VMEM] * 3,
         out_shape=[jax.ShapeDtypeStruct((parts, t_rows, channels), BF16), shape, shape],
         scratch_shapes=[
-            pltpu.VMEM((width, cols), BF16),
-            pltpu.VMEM((parts * t_rows, width), BF16),
+            pltpu.VMEM((half, 2 * rows, cols), BF16),
             pltpu.VMEM((2 * rows, cols), F32),
         ],
-        compiler_params=params(24),
+        compiler_params=params(20),
         name="attend",
-    )(*tok, *pooled, near, far, w_in, w_out)
+    )(*pooled, hid, query, near, far, w_out)
 
 
 def unpool_kernel(owners_ref, clusters_ref, feat_ref, near, far, out_ref, rows_ref):
@@ -296,10 +333,10 @@
     ).astype(BF16)
     pooled = [pooled] + [swap(pooled, k, odd(k)) for k in range(1, parts)]
     second, pooled = lax.optimization_barrier((second, pooled))
-    near = jnp.concatenate([first, second])
-    far = jnp.concatenate([far_first, swap(second, 0, 1)])
-
-    up, keep, give = attend([tok[0], tok_x[0]] + [tok[k] for k in range(2, parts)], pooled, near, far, w_in, w_out)
+    far_second = swap(second, 0, 1)
+    tok = [tok[0], tok_x[0]] + [tok[k] for k in range(2, parts)]
+    hid, query = hidden(tok, pooled, first, far_first, w_in)
+    up, keep, give = attend(pooled, hid, query, second, far_second, w_out)
 
     joined = keep.astype(F32) + swap(give, 0, 1).astype(F32)
     unpooled = up[0].astype(F32)

time: 61.3 us -> 60.4 us (0.985)
  waiting for transfers between devices: 18.7 us -> 17.7 us
    ppermute x27, waiting for transfers between devices: 18.7 us -> 17.7 us  [swap(): return lax.ppermute(x, ('group', 'shard'), pairs)]
    pallas_call x0 -> x1, Pallas kernels: none -> 0.93 us  [hidden(): pl.pallas_call(functools.partial(hidden_kernel, parts), in_specs=[VMEM] *...]
    pallas_call x1, Pallas kernels: 3.2 us -> 2.51 us  [attend(): pl.pallas_call(functools.partial(attend_kernel, parts), in_specs=[VMEM] *...]
  transfers between devices with their start and end apart: 27 -> 27, of which waited for: 11 -> 11; matrix products, arithmetic and copies ran while one was open for 1% -> 1% of each run, Pallas kernels for 10% -> 11%
where the time goes in v5:
time: 60.4 us; the launch traced here: 60.2 us
  starting transfers between devices  30.4 us (50%)
  waiting for transfers between devices  17.7 us (29%)
  Pallas kernels  10.4 us (17%)
  between operations  0.87 us (1%)
    ppermute x27, starting transfers between devices, swap(): return lax.ppermute(x, ('group', 'shard'), pairs)  30.4 us
    ppermute x27, waiting for transfers between devices, swap(): return lax.ppermute(x, ('group', 'shard'), pairs)  17.7 us
    pallas_call x1, Pallas kernels, pool(): pl.pallas_call(pool_kernel, in_specs=[whole] * 4, out_specs=[VMEM, VMEM],...  3.09 us
    pallas_call x1, Pallas kernels, unpool(): pl.pallas_call(unpool_kernel, grid_spec=pltpu.PrefetchScalarGridSpec(num_...  2.82 us
    pallas_call x1, Pallas kernels, attend(): pl.pallas_call(functools.partial(attend_kernel, parts), in_specs=[VMEM] *...  2.51 us
  transfers between devices with their start and end apart: 27, of which 11 were waited for; matrix products, arithmetic and copies ran while one was open for 1% of the time, Pallas kernels for 11%

profile of v5, /device:TPU:0, one launch (start us, length us, event | category | flops | bytes accessed | tf_op | source)
XLA Modules:
  0.0 60.2 jit_solution(13417694962728533729)
XLA Ops:
  0.6 0.0 copy-start
  0.6 2.4 %collective-permute-start.2 = (bf16[1,64,2048]{2,1,0:T(8,128)(2,1)}, bf16[1,64,2048]{2,1,0:T(8,128)(2,1)S(1)}, u32[]{:S(2)}, u32[]{:S(2)}) collective-permute-start(bf16[1,64,2048]{2,1,0:T(8,128)(2,1)} %bitcast.50), channel_id=1, source_target_pairs={{0,9},{1,8},{2,11},{3,10},{4,13},{5,12},{6,15},{7,14},{8,1},{9,0},... | collective-permute-start | bytes 786440 | tf_op jit(solution)/shard_map/ppermute | solution.py:283
  3.1 2.9 %collective-permute-start.1 = (bf16[1,256,256]{2,1,0:T(8,128)(2,1)S(1)}, bf16[1,256,256]{2,1,0:T(8,128)(2,1)S(1)}, u32[]{:S(2)}, u32[]{:S(2)}) collective-permute-start(bf16[1,256,256]{2,1,0:T(8,128)(2,1)S(1)} %dynamic-slice_bitcast_fusion), channel_id=1, source_target_pairs={{0,5},{1,4},{2,7},{3,6},{4,1},{5,0},{6,3},{7,2},{8,13},{9,12},{10,... | collective-permute-start | bytes 393224 | tf_op jit(solution)/shard_map/ppermute | solution.py:283
  6.0 3.1 %pool.1 = (f32[4,64,384]{2,1,0:T(8,128)}, bf16[4,64,384]{2,1,0:T(8,128)(2,1)}) custom-call(s32[32]{0:T(128)} %owners_ref.1, s32[32,128]{1,0:T(8,128)} %bitcast.53, bf16[4096,128]{1,0:T(8,128)(2,1)} %feat_ref.1, bf16[4096,128]{1,0:T(8,128)(2,1)} %grad_hbm.1), custom_call_target="tpu_custom_call" | custom-call | tf_op jit(solution)/shard_map/pool/pallas_call | solution.py:65
  9.2 0.1 collective-permute-start
  9.2 0.9 %collective-permute-done.2 = bf16[1,64,2048]{2,1,0:T(8,128)(2,1)S(1)} collective-permute-done((bf16[1,64,2048]{2,1,0:T(8,128)(2,1)}, bf16[1,64,2048]{2,1,0:T(8,128)(2,1)S(1)}, u32[]{:S(2)}, u32[]{:S(2)}) %collective-permute-start.2) | collective-permute-done | bytes 262176 | tf_op jit(solution)/shard_map/ppermute | solution.py:283
  10.1 0.1 pad_maximum_fusion
  10.1 2.2 %collective-permute-start.10 = (bf16[2,64,2048]{2,1,0:T(8,128)(2,1)S(1)}, bf16[2,64,2048]{2,1,0:T(8,128)(2,1)S(1)}, u32[]{:S(2)}, u32[]{:S(2)}) collective-permute-start(bf16[2,64,2048]{2,1,0:T(8,128)(2,1)S(1)} %pad_maximum_fusion), channel_id=1, source_target_pairs={{0,17},{1,16},{2,19},{3,18},{4,21},{5,20},{6,23},{7,22},{8,25},{9,... | collective-permute-start | bytes 1572872 | tf_op jit(solution)/shard_map/ppermute | solution.py:283
  12.3 0.1 fusion.13
  12.4 2.6 %collective-permute-start.4 = (bf16[64,384]{1,0:T(8,128)(2,1)S(1)}, bf16[64,384]{1,0:T(8,128)(2,1)S(1)}, u32[]{:S(2)}, u32[]{:S(2)}) collective-permute-start(bf16[64,384]{1,0:T(8,128)(2,1)S(1)} %get-tuple-element.41), channel_id=1, source_target_pairs={{0,5},{1,4},{2,7},{3,6},{4,1},{5,0},{6,3},{7,2},{8,13},{9,12},{10,... | collective-permute-start | bytes 147464 | tf_op jit(solution)/shard_map/ppermute | solution.py:283
  15.1 1.3 %collective-permute-start.6 = (bf16[64,384]{1,0:T(8,128)(2,1)S(1)}, bf16[64,384]{1,0:T(8,128)(2,1)S(1)}, u32[]{:S(2)}, u32[]{:S(2)}) collective-permute-start(bf16[64,384]{1,0:T(8,128)(2,1)S(1)} %get-tuple-element.42), channel_id=1, source_target_pairs={{0,6},{1,7},{2,4},{3,5},{4,2},{5,3},{6,0},{7,1},{8,14},{9,15},{10,... | collective-permute-start | bytes 147464 | tf_op jit(solution)/shard_map/ppermute | solution.py:283
  16.4 0.1 collective-permute-start.5
  16.6 1.7 %collective-permute-start.3 = (bf16[2,256,256]{2,1,0:T(8,128)(2,1)S(1)}, bf16[2,256,256]{2,1,0:T(8,128)(2,1)S(1)}, u32[]{:S(2)}, u32[]{:S(2)}) collective-permute-start(bf16[2,256,256]{2,1,0:T(8,128)(2,1)S(1)} %pad_maximum_fusion.1.refs_8_), channel_id=1, source_target_pairs={{0,3},{1,2},{2,1},{3,0},{4,7},{5,6},{6,5},{7,4},{8,11},{9,10},{10,... | collective-permute-start | bytes 786440 | tf_op jit(solution)/shard_map/ppermute | solution.py:283
  18.3 3.2 %collective-permute-done.6 = bf16[64,384]{1,0:T(8,128)(2,1)S(1)} collective-permute-done((bf16[64,384]{1,0:T(8,128)(2,1)S(1)}, bf16[64,384]{1,0:T(8,128)(2,1)S(1)}, u32[]{:S(2)}, u32[]{:S(2)}) %collective-permute-start.6) | collective-permute-done | bytes 49184 | tf_op jit(solution)/shard_map/ppermute | solution.py:283
  21.4 0.1 collective-permute-done.5
  21.5 0.1 slice_reduce_fusion
  21.7 0.1 fusion.7
  21.8 2.0 %collective-permute-start.9 = (bf16[64,256]{1,0:T(8,128)(2,1)S(1)}, bf16[64,256]{1,0:T(8,128)(2,1)S(1)}, u32[]{:S(2)}, u32[]{:S(2)}) collective-permute-start(bf16[64,256]{1,0:T(8,128)(2,1)S(1)} %pad_maximum_fusion.3.refs_4_.refs_0_), channel_id=1, source_target_pairs={{0,24},{1,25},{2,26},{3,27},{4,28},{5,29},{6,30},{7,31},{8,16},{9,... | collective-permute-start | bytes 98312 | tf_op jit(solution)/shard_map/ppermute | solution.py:283
  23.8 0.5 collective-permute-start.8
  24.3 0.8 %collective-permute-start.7 = (bf16[64,256]{1,0:T(8,128)(2,1)S(1)}, bf16[64,256]{1,0:T(8,128)(2,1)S(1)}, u32[]{:S(2)}, u32[]{:S(2)}) collective-permute-start(bf16[64,256]{1,0:T(8,128)(2,1)S(1)} %pad_maximum_fusion.3.refs_4_.refs_0_), channel_id=1, source_target_pairs={{0,9},{1,8},{2,11},{3,10},{4,13},{5,12},{6,15},{7,14},{8,1},{9,0},... | collective-permute-start | bytes 98312 | tf_op jit(solution)/shard_map/ppermute | solution.py:283
  25.1 1.6 %collective-permute-done.9.refs_7_.refs_3_ = bf16[64,256]{1,0:T(8,128)(2,1)S(1)} collective-permute-done((bf16[64,256]{1,0:T(8,128)(2,1)S(1)}, bf16[64,256]{1,0:T(8,128)(2,1)S(1)}, u32[]{:S(2)}, u32[]{:S(2)}) %collective-permute-start.9) | collective-permute-done | bytes 32800 | tf_op jit(solution)/shard_map/ppermute | solution.py:283
  26.7 0.8 %collective-permute-done.8.refs_6_.refs_2_ = bf16[64,256]{1,0:T(8,128)(2,1)S(1)} collective-permute-done((bf16[64,256]{1,0:T(8,128)(2,1)S(1)}, bf16[64,256]{1,0:T(8,128)(2,1)S(1)}, u32[]{:S(2)}, u32[]{:S(2)}) %collective-permute-start.8) | collective-permute-done | bytes 32800 | tf_op jit(solution)/shard_map/ppermute | solution.py:283
  27.4 0.2 collective-permute-done.7.refs_5_.refs_1_
  27.6 0.7 %collective-permute-start.12 = (bf16[2,256,256]{2,1,0:T(8,128)(2,1)S(1)}, bf16[2,256,256]{2,1,0:T(8,128)(2,1)S(1)}, u32[]{:S(2)}, u32[]{:S(2)}) collective-permute-start(bf16[2,256,256]{2,1,0:T(8,128)(2,1)S(1)} %collective-permute-done.3.refs_6_), channel_id=1, source_target_pairs={{0,1},{1,0},{2,3},{3,2},{4,5},{5,4},{6,7},{7,6},{8,9},{9,8},{10,11... | collective-permute-start | bytes 786440 | tf_op jit(solution)/shard_map/ppermute | solution.py:283
  28.4 0.9 %hidden.1 = (bf16[256,2048]{1,0:T(8,128)(2,1)S(1)}, f32[256,256]{1,0:T(8,128)S(1)}) custom-call(bf16[64,2048]{1,0:T(8,128)(2,1)S(1)} %copy-done.2, bf16[64,2048]{1,0:T(8,128)(2,1)S(1)} %bitcast.52, bf16[64,2048]{1,0:T(8,128)(2,1)S(1)} %get-tuple-element.40.refs_2_, bf16[64,2048]{1,0:T(8,128)(2,1)S(1)} %get-tuple-element.39.refs_3_, ...), custom_call_target="tpu_custom_call" | custom-call | tf_op jit(solution)/shard_map/hidden/pallas_call | solution.py:118
  29.3 0.1 collective-permute-done.12.refs_7_
  29.5 2.5 %attend.1 = (bf16[4,64,128]{2,1,0:T(8,128)(2,1)S(1)}, bf16[4,256,256]{2,1,0:T(8,128)(2,1)S(1)}, bf16[4,256,256]{2,1,0:T(8,128)(2,1)S(1)}) custom-call(bf16[64,256]{1,0:T(8,128)(2,1)S(1)} %pad_maximum_fusion.3.refs_4_.refs_0_, bf16[64,256]{1,0:T(8,128)(2,1)S(1)} %collective-permute-done.7.refs_5_.refs_1_, ...), custom_call_target="tpu_custom_call" | custom-call | tf_op jit(solution)/shard_map/attend/pallas_call | solution.py:196
  32.0 0.4 collective-permute-start.19
  32.4 1.2 %collective-permute-start.13 = (bf16[64,128]{1,0:T(8,128)(2,1)S(1)}, bf16[64,128]{1,0:T(8,128)(2,1)S(1)}, u32[]{:S(2)}, u32[]{:S(2)}) collective-permute-start(bf16[64,128]{1,0:T(8,128)(2,1)S(1)} %get-tuple-element.44), channel_id=1, source_target_pairs={{0,9},{1,8},{2,11},{3,10},{4,13},{5,12},{6,15},{7,14},{8,1},{9,0},... | collective-permute-start | bytes 49160 | tf_op jit(solution)/shard_map/ppermute | solution.py:283
  33.6 1.0 %collective-permute-start.15 = (bf16[64,128]{1,0:T(8,128)(2,1)S(1)}, bf16[64,128]{1,0:T(8,128)(2,1)S(1)}, u32[]{:S(2)}, u32[]{:S(2)}) collective-permute-start(bf16[64,128]{1,0:T(8,128)(2,1)S(1)} %get-tuple-element.45), channel_id=1, source_target_pairs={{0,24},{1,25},{2,26},{3,27},{4,28},{5,29},{6,30},{7,31},{8,16},{9,... | collective-permute-start | bytes 49160 | tf_op jit(solution)/shard_map/ppermute | solution.py:283
  34.6 0.7 %collective-permute-start.14 = (bf16[64,128]{1,0:T(8,128)(2,1)S(1)}, bf16[64,128]{1,0:T(8,128)(2,1)S(1)}, u32[]{:S(2)}, u32[]{:S(2)}) collective-permute-start(bf16[64,128]{1,0:T(8,128)(2,1)S(1)} %get-tuple-element.46), channel_id=1, source_target_pairs={{0,17},{1,16},{2,19},{3,18},{4,21},{5,20},{6,23},{7,22},{8,25},{9,... | collective-permute-start | bytes 49160 | tf_op jit(solution)/shard_map/ppermute | solution.py:283
  35.3 0.1 fusion.12
  35.5 2.6 %collective-permute-start.20 = (bf16[256,256]{1,0:T(8,128)(2,1)S(1)}, bf16[256,256]{1,0:T(8,128)(2,1)S(1)}, u32[]{:S(2)}, u32[]{:S(2)}) collective-permute-start(bf16[256,256]{1,0:T(8,128)(2,1)S(1)} %get-tuple-element.36), channel_id=1, source_target_pairs={{0,6},{1,7},{2,4},{3,5},{4,2},{5,3},{6,0},{7,1},{8,14},{9,15},{10,... | collective-permute-start | bytes 393224 | tf_op jit(solution)/shard_map/ppermute | solution.py:283
  38.1 1.6 %collective-permute-start.21 = (bf16[256,256]{1,0:T(8,128)(2,1)S(1)}, bf16[256,256]{1,0:T(8,128)(2,1)S(1)}, u32[]{:S(2)}, u32[]{:S(2)}) collective-permute-start(bf16[256,256]{1,0:T(8,128)(2,1)S(1)} %get-tuple-element.38), channel_id=1, source_target_pairs={{0,3},{1,2},{2,1},{3,0},{4,7},{5,6},{6,5},{7,4},{8,11},{9,10},{10,... | collective-permute-start | bytes 393224 | tf_op jit(solution)/shard_map/ppermute | solution.py:283
  39.7 0.3 collective-permute-start.16
  40.0 7.6 %collective-permute-done.16 = bf16[1,64,128]{2,1,0:T(8,128)(2,1)S(1)} collective-permute-done((bf16[1,64,128]{2,1,0:T(8,128)(2,1)S(1)}, bf16[1,64,128]{2,1,0:T(8,128)(2,1)S(1)}, u32[]{:S(2)}, u32[]{:S(2)}) %collective-permute-start.16) | collective-permute-done | bytes 16416 | tf_op jit(solution)/shard_map/ppermute | solution.py:283
  47.6 1.7 %collective-permute-start.17 = (bf16[2,64,128]{2,1,0:T(8,128)(2,1)S(1)}, bf16[2,64,128]{2,1,0:T(8,128)(2,1)S(1)}, u32[]{:S(2)}, u32[]{:S(2)}) collective-permute-start(bf16[2,64,128]{2,1,0:T(8,128)(2,1)S(1)} %pad_maximum_fusion.4), channel_id=1, source_target_pairs={{0,5},{1,4},{2,7},{3,6},{4,1},{5,0},{6,3},{7,2},{8,13},{9,12},{10,... | collective-permute-start | bytes 98312 | tf_op jit(solution)/shard_map/ppermute | solution.py:283
  49.3 0.2 collective-permute-done.22
  49.5 0.1 fusion.3
  49.6 1.8 %collective-permute-start.26 = (bf16[256,256]{1,0:T(8,128)(2,1)S(1)}, bf16[256,256]{1,0:T(8,128)(2,1)S(1)}, u32[]{:S(2)}, u32[]{:S(2)}) collective-permute-start(bf16[256,256]{1,0:T(8,128)(2,1)S(1)} %fusion.3), channel_id=1, source_target_pairs={{0,25},{1,24},{2,27},{3,26},{4,29},{5,28},{6,31},{7,30},{8,17},{9,... | collective-permute-start | bytes 393224 | tf_op jit(solution)/shard_map/ppermute | solution.py:283
  51.4 1.1 %collective-permute-start.25 = (bf16[256,256]{1,0:T(8,128)(2,1)S(1)}, bf16[256,256]{1,0:T(8,128)(2,1)S(1)}, u32[]{:S(2)}, u32[]{:S(2)}) collective-permute-start(bf16[256,256]{1,0:T(8,128)(2,1)S(1)} %fusion.3), channel_id=1, source_target_pairs={{0,17},{1,16},{2,19},{3,18},{4,21},{5,20},{6,23},{7,22},{8,25},{9,... | collective-permute-start | bytes 393224 | tf_op jit(solution)/shard_map/ppermute | solution.py:283
  52.5 0.1 collective-permute-start.24
  52.6 0.4 collective-permute-start.23
  53.0 0.1 collective-permute-start.18
  53.2 1.2 %collective-permute-done.18.far = bf16[4,64,128]{2,1,0:T(8,128)(2,1)S(1)} collective-permute-done((bf16[4,64,128]{2,1,0:T(8,128)(2,1)S(1)}, bf16[4,64,128]{2,1,0:T(8,128)(2,1)S(1)}, u32[]{:S(2)}, u32[]{:S(2)}) %collective-permute-start.18) | collective-permute-done | bytes 65568 | tf_op jit(solution)/shard_map/ppermute | solution.py:283
  54.4 2.8 %unpool.1 = bf16[4096,128]{1,0:T(8,128)(2,1)} custom-call(s32[32]{0:T(128)S(1)} %copy-done.6, s32[32,128]{1,0:T(8,128)S(1)} %bitcast.54, bf16[4096,128]{1,0:T(8,128)(2,1)S(1)} %copy-done.1, bf16[4,64,128]{2,1,0:T(8,128)(2,1)S(1)} %pad_maximum_fusion.2.near, bf16[4,64,128]{2,1,0:T(8,128)(2,1)S(1)} %collective-permute-done.18.far), custom_call_target="tpu_custom_call" | custom-call | tf_op jit(solution)/shard_map/unpool/pallas_call | solution.py:239
  57.2 1.9 %collective-permute-done.25.refs_2_ = bf16[256,256]{1,0:T(8,128)(2,1)S(1)} collective-permute-done((bf16[256,256]{1,0:T(8,128)(2,1)S(1)}, bf16[256,256]{1,0:T(8,128)(2,1)S(1)}, u32[]{:S(2)}, u32[]{:S(2)}) %collective-permute-start.25) | collective-permute-done | bytes 131104 | tf_op jit(solution)/shard_map/ppermute | solution.py:283
  59.1 1.1 %spread.1 = f32[256,1024]{1,0:T(8,128)} custom-call(bf16[256,256]{1,0:T(8,128)(2,1)S(1)} %collective-permute-done.23.refs_0_, bf16[256,256]{1,0:T(8,128)(2,1)S(1)} %collective-permute-done.24.refs_1_, bf16[256,256]{1,0:T(8,128)(2,1)S(1)} %collective-permute-done.25.refs_2_, bf16[256,256]{1,0:T(8,128)(2,1)S(1)} %collective-permute-done.26.refs_3_), custom_call_target="tpu_custom_call" | custom-call | tf_op jit(solution)/shard_map/spread/pallas_call | solution.py:269
  (46 shorter events, 0.3 us)
Async XLA Ops:
  0.6 2.5 %copy-start = (bf16[256,1024]{1,0:T(8,128)(2,1)S(1)}, bf16[256,1024]{1,0:T(8,128)(2,1)}, u32[]{:S(2)}) copy-start(bf16[256,1024]{1,0:T(8,128)(2,1)} %param.9) | copy-start | bytes 1572868
  0.6 9.4 %collective-permute-start.2 = (bf16[1,64,2048]{2,1,0:T(8,128)(2,1)}, bf16[1,64,2048]{2,1,0:T(8,128)(2,1)S(1)}, u32[]{:S(2)}, u32[]{:S(2)}) collective-permute-start(bf16[1,64,2048]{2,1,0:T(8,128)(2,1)} %bitcast.50), channel_id=1, source_target_pairs={{0,9},{1,8},{2,11},{3,10},{4,13},{5,12},{6,15},{7,14},{8,1},{9,0},... | collective-permute-start | bytes 786440 | tf_op jit(solution)/shard_map/ppermute | solution.py:283
  3.1 9.2 %collective-permute-start.1 = (bf16[1,256,256]{2,1,0:T(8,128)(2,1)S(1)}, bf16[1,256,256]{2,1,0:T(8,128)(2,1)S(1)}, u32[]{:S(2)}, u32[]{:S(2)}) collective-permute-start(bf16[1,256,256]{2,1,0:T(8,128)(2,1)S(1)} %dynamic-slice_bitcast_fusion), channel_id=1, source_target_pairs={{0,5},{1,4},{2,7},{3,6},{4,1},{5,0},{6,3},{7,2},{8,13},{9,12},{10,... | collective-permute-start | bytes 393224 | tf_op jit(solution)/shard_map/ppermute | solution.py:283
  6.0 4.0 %copy-start.2 = (bf16[64,2048]{1,0:T(8,128)(2,1)S(1)}, bf16[64,2048]{1,0:T(8,128)(2,1)}, u32[]{:S(2)}) copy-start(bf16[64,2048]{1,0:T(8,128)(2,1)} %refs_0_.1) | copy-start | bytes 786436
  9.1 3.2 %copy-start.7 = (f32[4,64,384]{2,1,0:T(8,128)S(1)}, f32[4,64,384]{2,1,0:T(8,128)}, u32[]{:S(2)}) copy-start(f32[4,64,384]{2,1,0:T(8,128)} %get-tuple-element.19) | copy-start | bytes 1179652
  9.2 3.2 %collective-permute-start = (bf16[4,64,384]{2,1,0:T(8,128)(2,1)}, bf16[4,64,384]{2,1,0:T(8,128)(2,1)S(1)}, u32[]{:S(2)}, u32[]{:S(2)}) collective-permute-start(bf16[4,64,384]{2,1,0:T(8,128)(2,1)} %get-tuple-element.17), channel_id=1, source_target_pairs={{0,1},{1,0},{2,3},{3,2},{4,5},{5,4},{6,7},{7,6},{8,9},{9,8},{10,11... | collective-permute-start | bytes 589832 | tf_op jit(solution)/shard_map/ppermute | solution.py:283
  10.1 18.2 %collective-permute-start.10 = (bf16[2,64,2048]{2,1,0:T(8,128)(2,1)S(1)}, bf16[2,64,2048]{2,1,0:T(8,128)(2,1)S(1)}, u32[]{:S(2)}, u32[]{:S(2)}) collective-permute-start(bf16[2,64,2048]{2,1,0:T(8,128)(2,1)S(1)} %pad_maximum_fusion), channel_id=1, source_target_pairs={{0,17},{1,16},{2,19},{3,18},{4,21},{5,20},{6,23},{7,22},{8,25},{9,... | collective-permute-start | bytes 1572872 | tf_op jit(solution)/shard_map/ppermute | solution.py:283
  12.4 5.8 %collective-permute-start.4 = (bf16[64,384]{1,0:T(8,128)(2,1)S(1)}, bf16[64,384]{1,0:T(8,128)(2,1)S(1)}, u32[]{:S(2)}, u32[]{:S(2)}) collective-permute-start(bf16[64,384]{1,0:T(8,128)(2,1)S(1)} %get-tuple-element.41), channel_id=1, source_target_pairs={{0,5},{1,4},{2,7},{3,6},{4,1},{5,0},{6,3},{7,2},{8,13},{9,12},{10,... | collective-permute-start | bytes 147464 | tf_op jit(solution)/shard_map/ppermute | solution.py:283
  15.1 6.3 %collective-permute-start.6 = (bf16[64,384]{1,0:T(8,128)(2,1)S(1)}, bf16[64,384]{1,0:T(8,128)(2,1)S(1)}, u32[]{:S(2)}, u32[]{:S(2)}) collective-permute-start(bf16[64,384]{1,0:T(8,128)(2,1)S(1)} %get-tuple-element.42), channel_id=1, source_target_pairs={{0,6},{1,7},{2,4},{3,5},{4,2},{5,3},{6,0},{7,1},{8,14},{9,15},{10,... | collective-permute-start | bytes 147464 | tf_op jit(solution)/shard_map/ppermute | solution.py:283
  16.4 5.1 %collective-permute-start.5 = (bf16[64,384]{1,0:T(8,128)(2,1)S(1)}, bf16[64,384]{1,0:T(8,128)(2,1)S(1)}, u32[]{:S(2)}, u32[]{:S(2)}) collective-permute-start(bf16[64,384]{1,0:T(8,128)(2,1)S(1)} %get-tuple-element.43), channel_id=1, source_target_pairs={{0,3},{1,2},{2,1},{3,0},{4,7},{5,6},{6,5},{7,4},{8,11},{9,10},{10,... | collective-permute-start | bytes 147464 | tf_op jit(solution)/shard_map/ppermute | solution.py:283
  16.6 11.0 %collective-permute-start.3 = (bf16[2,256,256]{2,1,0:T(8,128)(2,1)S(1)}, bf16[2,256,256]{2,1,0:T(8,128)(2,1)S(1)}, u32[]{:S(2)}, u32[]{:S(2)}) collective-permute-start(bf16[2,256,256]{2,1,0:T(8,128)(2,1)S(1)} %pad_maximum_fusion.1.refs_8_), channel_id=1, source_target_pairs={{0,3},{1,2},{2,1},{3,0},{4,7},{5,6},{6,5},{7,4},{8,11},{9,10},{10,... | collective-permute-start | bytes 786440 | tf_op jit(solution)/shard_map/ppermute | solution.py:283
  21.8 6.6 %copy-start.3 = (bf16[128,2048]{1,0:T(8,128)(2,1)S(1)}, bf16[128,2048]{1,0:T(8,128)(2,1)}, u32[]{:S(2)}) copy-start(bf16[128,2048]{1,0:T(8,128)(2,1)} %refs_10_.1) | copy-start | bytes 1572868
  21.8 4.9 %collective-permute-start.9 = (bf16[64,256]{1,0:T(8,128)(2,1)S(1)}, bf16[64,256]{1,0:T(8,128)(2,1)S(1)}, u32[]{:S(2)}, u32[]{:S(2)}) collective-permute-start(bf16[64,256]{1,0:T(8,128)(2,1)S(1)} %pad_maximum_fusion.3.refs_4_.refs_0_), channel_id=1, source_target_pairs={{0,24},{1,25},{2,26},{3,27},{4,28},{5,29},{6,30},{7,31},{8,16},{9,... | collective-permute-start | bytes 98312 | tf_op jit(solution)/shard_map/ppermute | solution.py:283
  23.8 3.7 %collective-permute-start.8 = (bf16[64,256]{1,0:T(8,128)(2,1)S(1)}, bf16[64,256]{1,0:T(8,128)(2,1)S(1)}, u32[]{:S(2)}, u32[]{:S(2)}) collective-permute-start(bf16[64,256]{1,0:T(8,128)(2,1)S(1)} %pad_maximum_fusion.3.refs_4_.refs_0_), channel_id=1, source_target_pairs={{0,17},{1,16},{2,19},{3,18},{4,21},{5,20},{6,23},{7,22},{8,25},{9,... | collective-permute-start | bytes 98312 | tf_op jit(solution)/shard_map/ppermute | solution.py:283
  24.3 3.3 %collective-permute-start.7 = (bf16[64,256]{1,0:T(8,128)(2,1)S(1)}, bf16[64,256]{1,0:T(8,128)(2,1)S(1)}, u32[]{:S(2)}, u32[]{:S(2)}) collective-permute-start(bf16[64,256]{1,0:T(8,128)(2,1)S(1)} %pad_maximum_fusion.3.refs_4_.refs_0_), channel_id=1, source_target_pairs={{0,9},{1,8},{2,11},{3,10},{4,13},{5,12},{6,15},{7,14},{8,1},{9,0},... | collective-permute-start | bytes 98312 | tf_op jit(solution)/shard_map/ppermute | solution.py:283
  26.7 1.7 %collective-permute-start.11 = (bf16[2,256,256]{2,1,0:T(8,128)(2,1)S(1)}, bf16[2,256,256]{2,1,0:T(8,128)(2,1)S(1)}, u32[]{:S(2)}, u32[]{:S(2)}) collective-permute-start(bf16[2,256,256]{2,1,0:T(8,128)(2,1)S(1)} %pad_maximum_fusion.1.refs_8_), channel_id=1, source_target_pairs={{0,1},{1,0},{2,3},{3,2},{4,5},{5,4},{6,7},{7,6},{8,9},{9,8},{10,11... | collective-permute-start | bytes 786440 | tf_op jit(solution)/shard_map/ppermute | solution.py:283
  27.6 1.8 %collective-permute-start.12 = (bf16[2,256,256]{2,1,0:T(8,128)(2,1)S(1)}, bf16[2,256,256]{2,1,0:T(8,128)(2,1)S(1)}, u32[]{:S(2)}, u32[]{:S(2)}) collective-permute-start(bf16[2,256,256]{2,1,0:T(8,128)(2,1)S(1)} %collective-permute-done.3.refs_6_), channel_id=1, source_target_pairs={{0,1},{1,0},{2,3},{3,2},{4,5},{5,4},{6,7},{7,6},{8,9},{9,8},{10,11... | collective-permute-start | bytes 786440 | tf_op jit(solution)/shard_map/ppermute | solution.py:283
  28.4 1.1 %copy-start.4 = (bf16[2048,128]{1,0:T(8,128)(2,1)S(1)}, bf16[2048,128]{1,0:T(8,128)(2,1)}, u32[]{:S(2)}) copy-start(bf16[2048,128]{1,0:T(8,128)(2,1)} %refs_8_.1) | copy-start | bytes 1572868
  32.0 3.4 %collective-permute-start.19 = (bf16[4,256,256]{2,1,0:T(8,128)(2,1)S(1)}, bf16[4,256,256]{2,1,0:T(8,128)(2,1)S(1)}, u32[]{:S(2)}, u32[]{:S(2)}) collective-permute-start(bf16[4,256,256]{2,1,0:T(8,128)(2,1)S(1)} %get-tuple-element.31), channel_id=1, source_target_pairs={{0,1},{1,0},{2,3},{3,2},{4,5},{5,4},{6,7},{7,6},{8,9},{9,8},{10,11... | collective-permute-start | bytes 1572872 | tf_op jit(solution)/shard_map/ppermute | solution.py:283
  32.4 5.7 %collective-permute-start.13 = (bf16[64,128]{1,0:T(8,128)(2,1)S(1)}, bf16[64,128]{1,0:T(8,128)(2,1)S(1)}, u32[]{:S(2)}, u32[]{:S(2)}) collective-permute-start(bf16[64,128]{1,0:T(8,128)(2,1)S(1)} %get-tuple-element.44), channel_id=1, source_target_pairs={{0,9},{1,8},{2,11},{3,10},{4,13},{5,12},{6,15},{7,14},{8,1},{9,0},... | collective-permute-start | bytes 49160 | tf_op jit(solution)/shard_map/ppermute | solution.py:283
  33.6 6.1 %collective-permute-start.15 = (bf16[64,128]{1,0:T(8,128)(2,1)S(1)}, bf16[64,128]{1,0:T(8,128)(2,1)S(1)}, u32[]{:S(2)}, u32[]{:S(2)}) collective-permute-start(bf16[64,128]{1,0:T(8,128)(2,1)S(1)} %get-tuple-element.45), channel_id=1, source_target_pairs={{0,24},{1,25},{2,26},{3,27},{4,28},{5,29},{6,30},{7,31},{8,16},{9,... | collective-permute-start | bytes 49160 | tf_op jit(solution)/shard_map/ppermute | solution.py:283
  34.6 5.1 %collective-permute-start.14 = (bf16[64,128]{1,0:T(8,128)(2,1)S(1)}, bf16[64,128]{1,0:T(8,128)(2,1)S(1)}, u32[]{:S(2)}, u32[]{:S(2)}) collective-permute-start(bf16[64,128]{1,0:T(8,128)(2,1)S(1)} %get-tuple-element.46), channel_id=1, source_target_pairs={{0,17},{1,16},{2,19},{3,18},{4,21},{5,20},{6,23},{7,22},{8,25},{9,... | collective-permute-start | bytes 49160 | tf_op jit(solution)/shard_map/ppermute | solution.py:283
  35.5 18.9 %copy-start.1 = (bf16[4096,128]{1,0:T(8,128)(2,1)S(1)}, bf16[4096,128]{1,0:T(8,128)(2,1)}, u32[]{:S(2)}) copy-start(bf16[4096,128]{1,0:T(8,128)(2,1)} %feat_ref.1) | copy-start | bytes 3145732
  35.5 13.8 %collective-permute-start.20 = (bf16[256,256]{1,0:T(8,128)(2,1)S(1)}, bf16[256,256]{1,0:T(8,128)(2,1)S(1)}, u32[]{:S(2)}, u32[]{:S(2)}) collective-permute-start(bf16[256,256]{1,0:T(8,128)(2,1)S(1)} %get-tuple-element.36), channel_id=1, source_target_pairs={{0,6},{1,7},{2,4},{3,5},{4,2},{5,3},{6,0},{7,1},{8,14},{9,15},{10,... | collective-permute-start | bytes 393224 | tf_op jit(solution)/shard_map/ppermute | solution.py:283
  38.1 11.4 %collective-permute-start.22 = (bf16[256,256]{1,0:T(8,128)(2,1)S(1)}, bf16[256,256]{1,0:T(8,128)(2,1)S(1)}, u32[]{:S(2)}, u32[]{:S(2)}) collective-permute-start(bf16[256,256]{1,0:T(8,128)(2,1)S(1)} %get-tuple-element.37), channel_id=1, source_target_pairs={{0,5},{1,4},{2,7},{3,6},{4,1},{5,0},{6,3},{7,2},{8,13},{9,12},{10,... | collective-permute-start | bytes 393224 | tf_op jit(solution)/shard_map/ppermute | solution.py:283
  38.1 11.3 %collective-permute-start.21 = (bf16[256,256]{1,0:T(8,128)(2,1)S(1)}, bf16[256,256]{1,0:T(8,128)(2,1)S(1)}, u32[]{:S(2)}, u32[]{:S(2)}) collective-permute-start(bf16[256,256]{1,0:T(8,128)(2,1)S(1)} %get-tuple-element.38), channel_id=1, source_target_pairs={{0,3},{1,2},{2,1},{3,0},{4,7},{5,6},{6,5},{7,4},{8,11},{9,10},{10,... | collective-permute-start | bytes 393224 | tf_op jit(solution)/shard_map/ppermute | solution.py:283
  39.7 7.8 %collective-permute-start.16 = (bf16[1,64,128]{2,1,0:T(8,128)(2,1)S(1)}, bf16[1,64,128]{2,1,0:T(8,128)(2,1)S(1)}, u32[]{:S(2)}, u32[]{:S(2)}) collective-permute-start(bf16[1,64,128]{2,1,0:T(8,128)(2,1)S(1)} %fusion.11), channel_id=1, source_target_pairs={{0,3},{1,2},{2,1},{3,0},{4,7},{5,6},{6,5},{7,4},{8,11},{9,10},{10,... | collective-permute-start | bytes 49160 | tf_op jit(solution)/shard_map/ppermute | solution.py:283
  47.6 5.4 %collective-permute-start.17 = (bf16[2,64,128]{2,1,0:T(8,128)(2,1)S(1)}, bf16[2,64,128]{2,1,0:T(8,128)(2,1)S(1)}, u32[]{:S(2)}, u32[]{:S(2)}) collective-permute-start(bf16[2,64,128]{2,1,0:T(8,128)(2,1)S(1)} %pad_maximum_fusion.4), channel_id=1, source_target_pairs={{0,5},{1,4},{2,7},{3,6},{4,1},{5,0},{6,3},{7,2},{8,13},{9,12},{10,... | collective-permute-start | bytes 98312 | tf_op jit(solution)/shard_map/ppermute | solution.py:283
  49.6 4.8 %copy-start.5 = (s32[4096]{0:T(1024)S(1)}, s32[4096]{0:T(1024)}, u32[]{:S(2)}) copy-start(s32[4096]{0:T(1024)} %param.14) | copy-start | bytes 49156
  49.6 4.8 %copy-start.6 = (s32[32]{0:T(128)S(1)}, s32[32]{0:T(128)}, u32[]{:S(2)}) copy-start(s32[32]{0:T(128)} %owners_ref.1) | copy-start | bytes 388
  49.6 7.6 %collective-permute-start.26 = (bf16[256,256]{1,0:T(8,128)(2,1)S(1)}, bf16[256,256]{1,0:T(8,128)(2,1)S(1)}, u32[]{:S(2)}, u32[]{:S(2)}) collective-permute-start(bf16[256,256]{1,0:T(8,128)(2,1)S(1)} %fusion.3), channel_id=1, source_target_pairs={{0,25},{1,24},{2,27},{3,26},{4,29},{5,28},{6,31},{7,30},{8,17},{9,... | collective-permute-start | bytes 393224 | tf_op jit(solution)/shard_map/ppermute | solution.py:283
  51.4 7.7 %collective-permute-start.25 = (bf16[256,256]{1,0:T(8,128)(2,1)S(1)}, bf16[256,256]{1,0:T(8,128)(2,1)S(1)}, u32[]{:S(2)}, u32[]{:S(2)}) collective-permute-start(bf16[256,256]{1,0:T(8,128)(2,1)S(1)} %fusion.3), channel_id=1, source_target_pairs={{0,17},{1,16},{2,19},{3,18},{4,21},{5,20},{6,23},{7,22},{8,25},{9,... | collective-permute-start | bytes 393224 | tf_op jit(solution)/shard_map/ppermute | solution.py:283
  52.5 6.7 %collective-permute-start.24 = (bf16[256,256]{1,0:T(8,128)(2,1)S(1)}, bf16[256,256]{1,0:T(8,128)(2,1)S(1)}, u32[]{:S(2)}, u32[]{:S(2)}) collective-permute-start(bf16[256,256]{1,0:T(8,128)(2,1)S(1)} %fusion.3), channel_id=1, source_target_pairs={{0,9},{1,8},{2,11},{3,10},{4,13},{5,12},{6,15},{7,14},{8,1},{9,0},... | collective-permute-start | bytes 393224 | tf_op jit(solution)/shard_map/ppermute | solution.py:283
  52.6 6.5 %collective-permute-start.23 = (bf16[256,256]{1,0:T(8,128)(2,1)S(1)}, bf16[256,256]{1,0:T(8,128)(2,1)S(1)}, u32[]{:S(2)}, u32[]{:S(2)}) collective-permute-start(bf16[256,256]{1,0:T(8,128)(2,1)S(1)} %fusion.3), channel_id=1, source_target_pairs={{0,1},{1,0},{2,3},{3,2},{4,5},{5,4},{6,7},{7,6},{8,9},{9,8},{10,11... | collective-permute-start | bytes 393224 | tf_op jit(solution)/shard_map/ppermute | solution.py:283
  53.0 1.3 %collective-permute-start.18 = (bf16[4,64,128]{2,1,0:T(8,128)(2,1)S(1)}, bf16[4,64,128]{2,1,0:T(8,128)(2,1)S(1)}, u32[]{:S(2)}, u32[]{:S(2)}) collective-permute-start(bf16[4,64,128]{2,1,0:T(8,128)(2,1)S(1)} %pad_maximum_fusion.2.near), channel_id=1, source_target_pairs={{0,1},{1,0},{2,3},{3,2},{4,5},{5,4},{6,7},{7,6},{8,9},{9,8},{10,11... | collective-permute-start | bytes 196616 | tf_op jit(solution)/shard_map/ppermute | solution.py:283

commit v6 on v5

--- a/solution.py
+++ b/solution.py
@@ -75,6 +75,7 @@
             pltpu.VMEM((num_blocks, rows), jnp.int32),
         ],
         compiler_params=params(60),
+        cost_estimate=pl.CostEstimate(flops=0, bytes_accessed=3000000, transcendentals=0),
         name="pool",
     )(owners, clusters.reshape(num_blocks, rows), particles, cotangent)
 
@@ -203,6 +204,7 @@
             pltpu.VMEM((2 * rows, cols), F32),
         ],
         compiler_params=params(20),
+        cost_estimate=pl.CostEstimate(flops=0, bytes_accessed=3000000, transcendentals=0),
         name="attend",
     )(*pooled, hid, query, near, far, w_out)
 
@@ -301,18 +303,17 @@
     parts = math.gcd(n_group, 4)
     pairs = n_shard // 2
     t_rows = tokens.shape[0]
+    channels = particles.shape[1]
     cols = w_qk.shape[1] // parts
     part = lax.rem(lax.axis_index("group"), parts)
 
     w_own = lax.dynamic_slice_in_dim(w_qk, part * cols, cols, axis=1)
-
     bits = [pairs >> i for i in range(1, pairs.bit_length())]
     first = [w_own[None]]
     for k in bits[:-1]:
         first.append(swap(jnp.concatenate(first), 0, chip(k)))
-    tok = tokens[None]
-    tok_x = swap(tok, 1, 1)
-    tok = jnp.concatenate([tok, tok_x])
+    tok_x = swap(tokens[None], 1, 1)
+    tok = jnp.concatenate([tokens[None], tok_x])
     for k in [1 << i for i in range(1, parts.bit_length() - 1)]:
         tok = jnp.concatenate([tok, swap(tok, k, 1)])
 
@@ -321,12 +322,12 @@
     got, first[-1], tok_x = lax.optimization_barrier((got, first[-1], tok_x))
     first = jnp.concatenate(first)
     joined = keep + got.astype(F32)
+    got = [swap(joined[k].astype(BF16), 0, chip(k)) for k in [2, 1, *range(3, pairs)]]
+    far_first = swap(first, 0, 1)
+    second = swap(first, 0, chip(1))
     sums = joined[0]
-    for k in [2, 1, *range(3, pairs)]:
-        sums = sums + swap(joined[k].astype(BF16), 0, chip(k)).astype(F32)
-    second = swap(first, 0, chip(1))
-    far_first = swap(first, 0, 1)
-    channels = particles.shape[1]
+    for piece in got:
+        sums = sums + piece.astype(F32)
     counts = jnp.sum(sums[:, 2 * channels :], axis=1, keepdims=True)
     pooled = jnp.concatenate(
         [sums[:, :channels] / jnp.maximum(counts, 1.0), sums[:, channels : 2 * channels]], axis=1
@@ -334,13 +335,13 @@
     pooled = [pooled] + [swap(pooled, k, odd(k)) for k in range(1, parts)]
     second, pooled = lax.optimization_barrier((second, pooled))
     far_second = swap(second, 0, 1)
-    tok = [tok[0], tok_x[0]] + [tok[k] for k in range(2, parts)]
+    tok = [tokens, tok_x[0]] + [tok[k] for k in range(2, parts)]
     hid, query = hidden(tok, pooled, first, far_first, w_in)
     up, keep, give = attend(pooled, hid, query, second, far_second, w_out)
-
     joined = keep.astype(F32) + swap(give, 0, 1).astype(F32)
+
     unpooled = up[0].astype(F32)
-    for k in range(1, parts):
+    for k in [*range(2, parts), 1]:
         unpooled = unpooled + swap(up[k], k, odd(k)).astype(F32)
     near = unpooled.astype(BF16)[None]
     for k in [1 << i for i in range(pairs.bit_length() - 1)]:
@@ -351,12 +352,15 @@
     grad = joined[0]
     for k in [pairs - 1, *range(1, pairs - 1)]:
         grad = grad + swap(joined[k].astype(BF16), 0, chip(k)).astype(F32)
+    grad = grad.astype(BF16)
     if n_group > parts:
-        part_sum = grad.astype(BF16)
+        part_sum = grad
+        grad = grad.astype(F32)
         for k in range(1, n_group // parts):
             grad = grad + swap(part_sum, k * parts, 0).astype(F32)
-    grad = grad.astype(BF16)
-    qk_grad = spread([swap(grad, k, 1) for k in range(parts)])
+        grad = grad.astype(BF16)
+    pieces = {k: swap(grad, k, 1) for k in [*range(1, parts), 0]}
+    qk_grad = spread([pieces[k] for k in range(parts)])
     return (particle_out, qk_grad)
 
 

time: 60.4 us -> 59.9 us (level)
  waiting for transfers between devices: 17.7 us -> 16.7 us
    ppermute x27, waiting for transfers between devices: 17.7 us -> 16.7 us  [swap(): return lax.ppermute(x, ('group', 'shard'), pairs)]
  transfers between devices with their start and end apart: 27 -> 27, of which waited for: 11 -> 10; matrix products, arithmetic and copies ran while one was open for 1% -> 1% of each run, Pallas kernels for 11% -> 11%
where the time goes in v6:
time: 59.9 us; the launch traced here: 59.7 us
  starting transfers between devices  31 us (52%)
  waiting for transfers between devices  16.7 us (28%)
  Pallas kernels  10.4 us (17%)
  between operations  0.87 us (1%)
    ppermute x27, starting transfers between devices, swap(): return lax.ppermute(x, ('group', 'shard'), pairs)  31 us
    ppermute x27, waiting for transfers between devices, swap(): return lax.ppermute(x, ('group', 'shard'), pairs)  16.7 us
    pallas_call x1, Pallas kernels, pool(): pl.pallas_call(pool_kernel, in_specs=[whole] * 4, out_specs=[VMEM, VMEM],...  3.09 us
    pallas_call x1, Pallas kernels, unpool(): pl.pallas_call(unpool_kernel, grid_spec=pltpu.PrefetchScalarGridSpec(num_...  2.82 us
    pallas_call x1, Pallas kernels, attend(): pl.pallas_call(functools.partial(attend_kernel, parts), in_specs=[VMEM] *...  2.51 us
  transfers between devices with their start and end apart: 27, of which 10 were waited for; matrix products, arithmetic and copies ran while one was open for 1% of the time, Pallas kernels for 11%

profile of v6, /device:TPU:0, one launch (start us, length us, event | category | flops | bytes accessed | tf_op | source)
XLA Modules:
  0.0 59.7 jit_solution(15016313322698253498)
XLA Ops:
  0.6 0.0 copy-start
  0.6 2.4 %collective-permute-start.2 = (bf16[1,64,2048]{2,1,0:T(8,128)(2,1)}, bf16[1,64,2048]{2,1,0:T(8,128)(2,1)S(1)}, u32[]{:S(2)}, u32[]{:S(2)}) collective-permute-start(bf16[1,64,2048]{2,1,0:T(8,128)(2,1)} %bitcast.50), channel_id=1, source_target_pairs={{0,9},{1,8},{2,11},{3,10},{4,13},{5,12},{6,15},{7,14},{8,1},{9,0},... | collective-permute-start | bytes 786440 | tf_op jit(solution)/shard_map/ppermute | solution.py:285
  3.1 2.9 %collective-permute-start.1 = (bf16[1,256,256]{2,1,0:T(8,128)(2,1)S(1)}, bf16[1,256,256]{2,1,0:T(8,128)(2,1)S(1)}, u32[]{:S(2)}, u32[]{:S(2)}) collective-permute-start(bf16[1,256,256]{2,1,0:T(8,128)(2,1)S(1)} %dynamic-slice_bitcast_fusion), channel_id=1, source_target_pairs={{0,5},{1,4},{2,7},{3,6},{4,1},{5,0},{6,3},{7,2},{8,13},{9,12},{10,... | collective-permute-start | bytes 393224 | tf_op jit(solution)/shard_map/ppermute | solution.py:285
  6.0 3.1 %pool.1 = (f32[4,64,384]{2,1,0:T(8,128)}, bf16[4,64,384]{2,1,0:T(8,128)(2,1)}) custom-call(s32[32]{0:T(128)} %owners_ref.1, s32[32,128]{1,0:T(8,128)} %bitcast.53, bf16[4096,128]{1,0:T(8,128)(2,1)} %feat_ref.1, bf16[4096,128]{1,0:T(8,128)(2,1)} %grad_hbm.1), custom_call_target="tpu_custom_call" | custom-call | bytes 3000000 | tf_op jit(solution)/shard_map/pool/pallas_call | solution.py:65
  9.2 0.1 collective-permute-start
  9.2 0.8 %collective-permute-done.2 = bf16[1,64,2048]{2,1,0:T(8,128)(2,1)S(1)} collective-permute-done((bf16[1,64,2048]{2,1,0:T(8,128)(2,1)}, bf16[1,64,2048]{2,1,0:T(8,128)(2,1)S(1)}, u32[]{:S(2)}, u32[]{:S(2)}) %collective-permute-start.2) | collective-permute-done | bytes 262176 | tf_op jit(solution)/shard_map/ppermute | solution.py:285
  10.1 0.1 pad_maximum_fusion
  10.1 2.2 %collective-permute-start.10 = (bf16[2,64,2048]{2,1,0:T(8,128)(2,1)S(1)}, bf16[2,64,2048]{2,1,0:T(8,128)(2,1)S(1)}, u32[]{:S(2)}, u32[]{:S(2)}) collective-permute-start(bf16[2,64,2048]{2,1,0:T(8,128)(2,1)S(1)} %pad_maximum_fusion), channel_id=1, source_target_pairs={{0,17},{1,16},{2,19},{3,18},{4,21},{5,20},{6,23},{7,22},{8,25},{9,... | collective-permute-start | bytes 1572872 | tf_op jit(solution)/shard_map/ppermute | solution.py:285
  12.3 0.0 collective-permute-done.1
  12.3 0.1 fusion.13
  12.4 2.6 %collective-permute-start.4 = (bf16[64,384]{1,0:T(8,128)(2,1)S(1)}, bf16[64,384]{1,0:T(8,128)(2,1)S(1)}, u32[]{:S(2)}, u32[]{:S(2)}) collective-permute-start(bf16[64,384]{1,0:T(8,128)(2,1)S(1)} %get-tuple-element.41), channel_id=1, source_target_pairs={{0,5},{1,4},{2,7},{3,6},{4,1},{5,0},{6,3},{7,2},{8,13},{9,12},{10,... | collective-permute-start | bytes 147464 | tf_op jit(solution)/shard_map/ppermute | solution.py:285
  15.1 1.3 %collective-permute-start.6 = (bf16[64,384]{1,0:T(8,128)(2,1)S(1)}, bf16[64,384]{1,0:T(8,128)(2,1)S(1)}, u32[]{:S(2)}, u32[]{:S(2)}) collective-permute-start(bf16[64,384]{1,0:T(8,128)(2,1)S(1)} %get-tuple-element.42), channel_id=1, source_target_pairs={{0,6},{1,7},{2,4},{3,5},{4,2},{5,3},{6,0},{7,1},{8,14},{9,15},{10,... | collective-permute-start | bytes 147464 | tf_op jit(solution)/shard_map/ppermute | solution.py:285
  16.4 0.1 collective-permute-start.5
  16.6 1.7 %collective-permute-start.3 = (bf16[2,256,256]{2,1,0:T(8,128)(2,1)S(1)}, bf16[2,256,256]{2,1,0:T(8,128)(2,1)S(1)}, u32[]{:S(2)}, u32[]{:S(2)}) collective-permute-start(bf16[2,256,256]{2,1,0:T(8,128)(2,1)S(1)} %pad_maximum_fusion.1.refs_8_), channel_id=1, source_target_pairs={{0,3},{1,2},{2,1},{3,0},{4,7},{5,6},{6,5},{7,4},{8,11},{9,10},{10,... | collective-permute-start | bytes 786440 | tf_op jit(solution)/shard_map/ppermute | solution.py:285
  18.3 3.2 %collective-permute-done.6 = bf16[64,384]{1,0:T(8,128)(2,1)S(1)} collective-permute-done((bf16[64,384]{1,0:T(8,128)(2,1)S(1)}, bf16[64,384]{1,0:T(8,128)(2,1)S(1)}, u32[]{:S(2)}, u32[]{:S(2)}) %collective-permute-start.6) | collective-permute-done | bytes 49184 | tf_op jit(solution)/shard_map/ppermute | solution.py:285
  21.4 0.1 collective-permute-done.5
  21.5 0.1 slice_reduce_fusion
  21.7 0.1 fusion.7
  21.8 2.0 %collective-permute-start.9 = (bf16[64,256]{1,0:T(8,128)(2,1)S(1)}, bf16[64,256]{1,0:T(8,128)(2,1)S(1)}, u32[]{:S(2)}, u32[]{:S(2)}) collective-permute-start(bf16[64,256]{1,0:T(8,128)(2,1)S(1)} %pad_maximum_fusion.3.refs_4_.refs_0_), channel_id=1, source_target_pairs={{0,24},{1,25},{2,26},{3,27},{4,28},{5,29},{6,30},{7,31},{8,16},{9,... | collective-permute-start | bytes 98312 | tf_op jit(solution)/shard_map/ppermute | solution.py:285
  23.8 0.5 collective-permute-start.8
  24.3 0.8 %collective-permute-start.7 = (bf16[64,256]{1,0:T(8,128)(2,1)S(1)}, bf16[64,256]{1,0:T(8,128)(2,1)S(1)}, u32[]{:S(2)}, u32[]{:S(2)}) collective-permute-start(bf16[64,256]{1,0:T(8,128)(2,1)S(1)} %pad_maximum_fusion.3.refs_4_.refs_0_), channel_id=1, source_target_pairs={{0,9},{1,8},{2,11},{3,10},{4,13},{5,12},{6,15},{7,14},{8,1},{9,0},... | collective-permute-start | bytes 98312 | tf_op jit(solution)/shard_map/ppermute | solution.py:285
  25.1 1.6 %collective-permute-done.9.refs_7_.refs_3_ = bf16[64,256]{1,0:T(8,128)(2,1)S(1)} collective-permute-done((bf16[64,256]{1,0:T(8,128)(2,1)S(1)}, bf16[64,256]{1,0:T(8,128)(2,1)S(1)}, u32[]{:S(2)}, u32[]{:S(2)}) %collective-permute-start.9) | collective-permute-done | bytes 32800 | tf_op jit(solution)/shard_map/ppermute | solution.py:285
  26.7 0.8 %collective-permute-done.8.refs_6_.refs_2_ = bf16[64,256]{1,0:T(8,128)(2,1)S(1)} collective-permute-done((bf16[64,256]{1,0:T(8,128)(2,1)S(1)}, bf16[64,256]{1,0:T(8,128)(2,1)S(1)}, u32[]{:S(2)}, u32[]{:S(2)}) %collective-permute-start.8) | collective-permute-done | bytes 32800 | tf_op jit(solution)/shard_map/ppermute | solution.py:285
  27.4 0.2 collective-permute-done.7.refs_5_.refs_1_
  27.6 0.7 %collective-permute-start.12 = (bf16[2,256,256]{2,1,0:T(8,128)(2,1)S(1)}, bf16[2,256,256]{2,1,0:T(8,128)(2,1)S(1)}, u32[]{:S(2)}, u32[]{:S(2)}) collective-permute-start(bf16[2,256,256]{2,1,0:T(8,128)(2,1)S(1)} %collective-permute-done.3.refs_6_), channel_id=1, source_target_pairs={{0,1},{1,0},{2,3},{3,2},{4,5},{5,4},{6,7},{7,6},{8,9},{9,8},{10,11... | collective-permute-start | bytes 786440 | tf_op jit(solution)/shard_map/ppermute | solution.py:285
  28.4 0.9 %hidden.1 = (bf16[256,2048]{1,0:T(8,128)(2,1)S(1)}, f32[256,256]{1,0:T(8,128)S(1)}) custom-call(bf16[64,2048]{1,0:T(8,128)(2,1)S(1)} %copy-done.2, bf16[64,2048]{1,0:T(8,128)(2,1)S(1)} %bitcast.52, bf16[64,2048]{1,0:T(8,128)(2,1)S(1)} %get-tuple-element.40.refs_2_, bf16[64,2048]{1,0:T(8,128)(2,1)S(1)} %get-tuple-element.39.refs_3_, ...), custom_call_target="tpu_custom_call" | custom-call | tf_op jit(solution)/shard_map/hidden/pallas_call | solution.py:119
  29.3 0.1 collective-permute-done.12.refs_7_
  29.5 2.5 %attend.1 = (bf16[4,64,128]{2,1,0:T(8,128)(2,1)S(1)}, bf16[4,256,256]{2,1,0:T(8,128)(2,1)S(1)}, bf16[4,256,256]{2,1,0:T(8,128)(2,1)S(1)}) custom-call(bf16[64,256]{1,0:T(8,128)(2,1)S(1)} %pad_maximum_fusion.3.refs_4_.refs_0_, bf16[64,256]{1,0:T(8,128)(2,1)S(1)} %collective-permute-done.7.refs_5_.refs_1_, ...), custom_call_target="tpu_custom_call" | custom-call | bytes 3000000 | tf_op jit(solution)/shard_map/attend/pallas_call | solution.py:197
  32.0 0.4 collective-permute-start.19
  32.4 0.7 %collective-permute-start.13 = (bf16[64,128]{1,0:T(8,128)(2,1)S(1)}, bf16[64,128]{1,0:T(8,128)(2,1)S(1)}, u32[]{:S(2)}, u32[]{:S(2)}) collective-permute-start(bf16[64,128]{1,0:T(8,128)(2,1)S(1)} %get-tuple-element.44), channel_id=1, source_target_pairs={{0,17},{1,16},{2,19},{3,18},{4,21},{5,20},{6,23},{7,22},{8,25},{9,... | collective-permute-start | bytes 49160 | tf_op jit(solution)/shard_map/ppermute | solution.py:285
  33.1 1.1 %collective-permute-start.15 = (bf16[64,128]{1,0:T(8,128)(2,1)S(1)}, bf16[64,128]{1,0:T(8,128)(2,1)S(1)}, u32[]{:S(2)}, u32[]{:S(2)}) collective-permute-start(bf16[64,128]{1,0:T(8,128)(2,1)S(1)} %get-tuple-element.45), channel_id=1, source_target_pairs={{0,9},{1,8},{2,11},{3,10},{4,13},{5,12},{6,15},{7,14},{8,1},{9,0},... | collective-permute-start | bytes 49160 | tf_op jit(solution)/shard_map/ppermute | solution.py:285
  34.2 1.4 %collective-permute-start.14 = (bf16[64,128]{1,0:T(8,128)(2,1)S(1)}, bf16[64,128]{1,0:T(8,128)(2,1)S(1)}, u32[]{:S(2)}, u32[]{:S(2)}) collective-permute-start(bf16[64,128]{1,0:T(8,128)(2,1)S(1)} %get-tuple-element.46), channel_id=1, source_target_pairs={{0,24},{1,25},{2,26},{3,27},{4,28},{5,29},{6,30},{7,31},{8,16},{9,... | collective-permute-start | bytes 49160 | tf_op jit(solution)/shard_map/ppermute | solution.py:285
  35.6 0.1 fusion.12
  35.8 2.6 %collective-permute-start.20 = (bf16[256,256]{1,0:T(8,128)(2,1)S(1)}, bf16[256,256]{1,0:T(8,128)(2,1)S(1)}, u32[]{:S(2)}, u32[]{:S(2)}) collective-permute-start(bf16[256,256]{1,0:T(8,128)(2,1)S(1)} %get-tuple-element.36), channel_id=1, source_target_pairs={{0,6},{1,7},{2,4},{3,5},{4,2},{5,3},{6,0},{7,1},{8,14},{9,15},{10,... | collective-permute-start | bytes 393224 | tf_op jit(solution)/shard_map/ppermute | solution.py:285
  38.4 1.6 %collective-permute-start.21 = (bf16[256,256]{1,0:T(8,128)(2,1)S(1)}, bf16[256,256]{1,0:T(8,128)(2,1)S(1)}, u32[]{:S(2)}, u32[]{:S(2)}) collective-permute-start(bf16[256,256]{1,0:T(8,128)(2,1)S(1)} %get-tuple-element.38), channel_id=1, source_target_pairs={{0,3},{1,2},{2,1},{3,0},{4,7},{5,6},{6,5},{7,4},{8,11},{9,10},{10,... | collective-permute-start | bytes 393224 | tf_op jit(solution)/shard_map/ppermute | solution.py:285
  40.0 0.3 collective-permute-start.16
  40.3 7.0 %collective-permute-done.16 = bf16[1,64,128]{2,1,0:T(8,128)(2,1)S(1)} collective-permute-done((bf16[1,64,128]{2,1,0:T(8,128)(2,1)S(1)}, bf16[1,64,128]{2,1,0:T(8,128)(2,1)S(1)}, u32[]{:S(2)}, u32[]{:S(2)}) %collective-permute-start.16) | collective-permute-done | bytes 16416 | tf_op jit(solution)/shard_map/ppermute | solution.py:285
  47.2 1.7 %collective-permute-start.17 = (bf16[2,64,128]{2,1,0:T(8,128)(2,1)S(1)}, bf16[2,64,128]{2,1,0:T(8,128)(2,1)S(1)}, u32[]{:S(2)}, u32[]{:S(2)}) collective-permute-start(bf16[2,64,128]{2,1,0:T(8,128)(2,1)S(1)} %pad_maximum_fusion.4), channel_id=1, source_target_pairs={{0,5},{1,4},{2,7},{3,6},{4,1},{5,0},{6,3},{7,2},{8,13},{9,12},{10,... | collective-permute-start | bytes 98312 | tf_op jit(solution)/shard_map/ppermute | solution.py:285
  49.0 0.1 fusion.3
  49.1 2.0 %collective-permute-start.26 = (bf16[256,256]{1,0:T(8,128)(2,1)S(1)}, bf16[256,256]{1,0:T(8,128)(2,1)S(1)}, u32[]{:S(2)}, u32[]{:S(2)}) collective-permute-start(bf16[256,256]{1,0:T(8,128)(2,1)S(1)} %fusion.3), channel_id=1, source_target_pairs={{0,25},{1,24},{2,27},{3,26},{4,29},{5,28},{6,31},{7,30},{8,17},{9,... | collective-permute-start | bytes 393224 | tf_op jit(solution)/shard_map/ppermute | solution.py:285
  51.1 0.7 %collective-permute-start.25 = (bf16[256,256]{1,0:T(8,128)(2,1)S(1)}, bf16[256,256]{1,0:T(8,128)(2,1)S(1)}, u32[]{:S(2)}, u32[]{:S(2)}) collective-permute-start(bf16[256,256]{1,0:T(8,128)(2,1)S(1)} %fusion.3), channel_id=1, source_target_pairs={{0,17},{1,16},{2,19},{3,18},{4,21},{5,20},{6,23},{7,22},{8,25},{9,... | collective-permute-start | bytes 393224 | tf_op jit(solution)/shard_map/ppermute | solution.py:285
  51.8 0.5 collective-permute-start.24
  52.3 0.2 collective-permute-start.23
  52.5 0.4 collective-permute-start.18
  52.9 0.9 %collective-permute-done.18.far = bf16[4,64,128]{2,1,0:T(8,128)(2,1)S(1)} collective-permute-done((bf16[4,64,128]{2,1,0:T(8,128)(2,1)S(1)}, bf16[4,64,128]{2,1,0:T(8,128)(2,1)S(1)}, u32[]{:S(2)}, u32[]{:S(2)}) %collective-permute-start.18) | collective-permute-done | bytes 65568 | tf_op jit(solution)/shard_map/ppermute | solution.py:285
  53.8 2.8 %unpool.1 = bf16[4096,128]{1,0:T(8,128)(2,1)} custom-call(s32[32]{0:T(128)S(1)} %copy-done.6, s32[32,128]{1,0:T(8,128)S(1)} %bitcast.54, bf16[4096,128]{1,0:T(8,128)(2,1)S(1)} %copy-done.1, bf16[4,64,128]{2,1,0:T(8,128)(2,1)S(1)} %pad_maximum_fusion.2.near, bf16[4,64,128]{2,1,0:T(8,128)(2,1)S(1)} %collective-permute-done.18.far), custom_call_target="tpu_custom_call" | custom-call | tf_op jit(solution)/shard_map/unpool/pallas_call | solution.py:241
  56.6 2.0 %collective-permute-done.25.refs_2_ = bf16[256,256]{1,0:T(8,128)(2,1)S(1)} collective-permute-done((bf16[256,256]{1,0:T(8,128)(2,1)S(1)}, bf16[256,256]{1,0:T(8,128)(2,1)S(1)}, u32[]{:S(2)}, u32[]{:S(2)}) %collective-permute-start.25) | collective-permute-done | bytes 131104 | tf_op jit(solution)/shard_map/ppermute | solution.py:285
  58.7 1.1 %spread.1 = f32[256,1024]{1,0:T(8,128)} custom-call(bf16[256,256]{1,0:T(8,128)(2,1)S(1)} %collective-permute-done.23.refs_0_, bf16[256,256]{1,0:T(8,128)(2,1)S(1)} %collective-permute-done.24.refs_1_, bf16[256,256]{1,0:T(8,128)(2,1)S(1)} %collective-permute-done.25.refs_2_, bf16[256,256]{1,0:T(8,128)(2,1)S(1)} %collective-permute-done.26.refs_3_), custom_call_target="tpu_custom_call" | custom-call | tf_op jit(solution)/shard_map/spread/pallas_call | solution.py:271
  (46 shorter events, 0.3 us)
Async XLA Ops:
  0.6 2.5 %copy-start = (bf16[256,1024]{1,0:T(8,128)(2,1)S(1)}, bf16[256,1024]{1,0:T(8,128)(2,1)}, u32[]{:S(2)}) copy-start(bf16[256,1024]{1,0:T(8,128)(2,1)} %param.9) | copy-start | bytes 1572868
  0.6 9.4 %collective-permute-start.2 = (bf16[1,64,2048]{2,1,0:T(8,128)(2,1)}, bf16[1,64,2048]{2,1,0:T(8,128)(2,1)S(1)}, u32[]{:S(2)}, u32[]{:S(2)}) collective-permute-start(bf16[1,64,2048]{2,1,0:T(8,128)(2,1)} %bitcast.50), channel_id=1, source_target_pairs={{0,9},{1,8},{2,11},{3,10},{4,13},{5,12},{6,15},{7,14},{8,1},{9,0},... | collective-permute-start | bytes 786440 | tf_op jit(solution)/shard_map/ppermute | solution.py:285
  3.1 9.2 %collective-permute-start.1 = (bf16[1,256,256]{2,1,0:T(8,128)(2,1)S(1)}, bf16[1,256,256]{2,1,0:T(8,128)(2,1)S(1)}, u32[]{:S(2)}, u32[]{:S(2)}) collective-permute-start(bf16[1,256,256]{2,1,0:T(8,128)(2,1)S(1)} %dynamic-slice_bitcast_fusion), channel_id=1, source_target_pairs={{0,5},{1,4},{2,7},{3,6},{4,1},{5,0},{6,3},{7,2},{8,13},{9,12},{10,... | collective-permute-start | bytes 393224 | tf_op jit(solution)/shard_map/ppermute | solution.py:285
  6.0 4.0 %copy-start.2 = (bf16[64,2048]{1,0:T(8,128)(2,1)S(1)}, bf16[64,2048]{1,0:T(8,128)(2,1)}, u32[]{:S(2)}) copy-start(bf16[64,2048]{1,0:T(8,128)(2,1)} %refs_0_.1) | copy-start | bytes 786436
  9.1 3.2 %copy-start.7 = (f32[4,64,384]{2,1,0:T(8,128)S(1)}, f32[4,64,384]{2,1,0:T(8,128)}, u32[]{:S(2)}) copy-start(f32[4,64,384]{2,1,0:T(8,128)} %get-tuple-element.19) | copy-start | bytes 1179652
  9.2 3.2 %collective-permute-start = (bf16[4,64,384]{2,1,0:T(8,128)(2,1)}, bf16[4,64,384]{2,1,0:T(8,128)(2,1)S(1)}, u32[]{:S(2)}, u32[]{:S(2)}) collective-permute-start(bf16[4,64,384]{2,1,0:T(8,128)(2,1)} %get-tuple-element.17), channel_id=1, source_target_pairs={{0,1},{1,0},{2,3},{3,2},{4,5},{5,4},{6,7},{7,6},{8,9},{9,8},{10,11... | collective-permute-start | bytes 589832 | tf_op jit(solution)/shard_map/ppermute | solution.py:285
  10.1 18.2 %collective-permute-start.10 = (bf16[2,64,2048]{2,1,0:T(8,128)(2,1)S(1)}, bf16[2,64,2048]{2,1,0:T(8,128)(2,1)S(1)}, u32[]{:S(2)}, u32[]{:S(2)}) collective-permute-start(bf16[2,64,2048]{2,1,0:T(8,128)(2,1)S(1)} %pad_maximum_fusion), channel_id=1, source_target_pairs={{0,17},{1,16},{2,19},{3,18},{4,21},{5,20},{6,23},{7,22},{8,25},{9,... | collective-permute-start | bytes 1572872 | tf_op jit(solution)/shard_map/ppermute | solution.py:285
  12.4 5.8 %collective-permute-start.4 = (bf16[64,384]{1,0:T(8,128)(2,1)S(1)}, bf16[64,384]{1,0:T(8,128)(2,1)S(1)}, u32[]{:S(2)}, u32[]{:S(2)}) collective-permute-start(bf16[64,384]{1,0:T(8,128)(2,1)S(1)} %get-tuple-element.41), channel_id=1, source_target_pairs={{0,5},{1,4},{2,7},{3,6},{4,1},{5,0},{6,3},{7,2},{8,13},{9,12},{10,... | collective-permute-start | bytes 147464 | tf_op jit(solution)/shard_map/ppermute | solution.py:285
  15.1 6.3 %collective-permute-start.6 = (bf16[64,384]{1,0:T(8,128)(2,1)S(1)}, bf16[64,384]{1,0:T(8,128)(2,1)S(1)}, u32[]{:S(2)}, u32[]{:S(2)}) collective-permute-start(bf16[64,384]{1,0:T(8,128)(2,1)S(1)} %get-tuple-element.42), channel_id=1, source_target_pairs={{0,6},{1,7},{2,4},{3,5},{4,2},{5,3},{6,0},{7,1},{8,14},{9,15},{10,... | collective-permute-start | bytes 147464 | tf_op jit(solution)/shard_map/ppermute | solution.py:285
  16.4 5.1 %collective-permute-start.5 = (bf16[64,384]{1,0:T(8,128)(2,1)S(1)}, bf16[64,384]{1,0:T(8,128)(2,1)S(1)}, u32[]{:S(2)}, u32[]{:S(2)}) collective-permute-start(bf16[64,384]{1,0:T(8,128)(2,1)S(1)} %get-tuple-element.43), channel_id=1, source_target_pairs={{0,3},{1,2},{2,1},{3,0},{4,7},{5,6},{6,5},{7,4},{8,11},{9,10},{10,... | collective-permute-start | bytes 147464 | tf_op jit(solution)/shard_map/ppermute | solution.py:285
  16.6 11.0 %collective-permute-start.3 = (bf16[2,256,256]{2,1,0:T(8,128)(2,1)S(1)}, bf16[2,256,256]{2,1,0:T(8,128)(2,1)S(1)}, u32[]{:S(2)}, u32[]{:S(2)}) collective-permute-start(bf16[2,256,256]{2,1,0:T(8,128)(2,1)S(1)} %pad_maximum_fusion.1.refs_8_), channel_id=1, source_target_pairs={{0,3},{1,2},{2,1},{3,0},{4,7},{5,6},{6,5},{7,4},{8,11},{9,10},{10,... | collective-permute-start | bytes 786440 | tf_op jit(solution)/shard_map/ppermute | solution.py:285
  21.8 6.6 %copy-start.3 = (bf16[128,2048]{1,0:T(8,128)(2,1)S(1)}, bf16[128,2048]{1,0:T(8,128)(2,1)}, u32[]{:S(2)}) copy-start(bf16[128,2048]{1,0:T(8,128)(2,1)} %refs_10_.1) | copy-start | bytes 1572868
  21.8 4.9 %collective-permute-start.9 = (bf16[64,256]{1,0:T(8,128)(2,1)S(1)}, bf16[64,256]{1,0:T(8,128)(2,1)S(1)}, u32[]{:S(2)}, u32[]{:S(2)}) collective-permute-start(bf16[64,256]{1,0:T(8,128)(2,1)S(1)} %pad_maximum_fusion.3.refs_4_.refs_0_), channel_id=1, source_target_pairs={{0,24},{1,25},{2,26},{3,27},{4,28},{5,29},{6,30},{7,31},{8,16},{9,... | collective-permute-start | bytes 98312 | tf_op jit(solution)/shard_map/ppermute | solution.py:285
  23.8 3.7 %collective-permute-start.8 = (bf16[64,256]{1,0:T(8,128)(2,1)S(1)}, bf16[64,256]{1,0:T(8,128)(2,1)S(1)}, u32[]{:S(2)}, u32[]{:S(2)}) collective-permute-start(bf16[64,256]{1,0:T(8,128)(2,1)S(1)} %pad_maximum_fusion.3.refs_4_.refs_0_), channel_id=1, source_target_pairs={{0,17},{1,16},{2,19},{3,18},{4,21},{5,20},{6,23},{7,22},{8,25},{9,... | collective-permute-start | bytes 98312 | tf_op jit(solution)/shard_map/ppermute | solution.py:285
  24.3 3.3 %collective-permute-start.7 = (bf16[64,256]{1,0:T(8,128)(2,1)S(1)}, bf16[64,256]{1,0:T(8,128)(2,1)S(1)}, u32[]{:S(2)}, u32[]{:S(2)}) collective-permute-start(bf16[64,256]{1,0:T(8,128)(2,1)S(1)} %pad_maximum_fusion.3.refs_4_.refs_0_), channel_id=1, source_target_pairs={{0,9},{1,8},{2,11},{3,10},{4,13},{5,12},{6,15},{7,14},{8,1},{9,0},... | collective-permute-start | bytes 98312 | tf_op jit(solution)/shard_map/ppermute | solution.py:285
  26.7 1.7 %collective-permute-start.11 = (bf16[2,256,256]{2,1,0:T(8,128)(2,1)S(1)}, bf16[2,256,256]{2,1,0:T(8,128)(2,1)S(1)}, u32[]{:S(2)}, u32[]{:S(2)}) collective-permute-start(bf16[2,256,256]{2,1,0:T(8,128)(2,1)S(1)} %pad_maximum_fusion.1.refs_8_), channel_id=1, source_target_pairs={{0,1},{1,0},{2,3},{3,2},{4,5},{5,4},{6,7},{7,6},{8,9},{9,8},{10,11... | collective-permute-start | bytes 786440 | tf_op jit(solution)/shard_map/ppermute | solution.py:285
  27.6 1.8 %collective-permute-start.12 = (bf16[2,256,256]{2,1,0:T(8,128)(2,1)S(1)}, bf16[2,256,256]{2,1,0:T(8,128)(2,1)S(1)}, u32[]{:S(2)}, u32[]{:S(2)}) collective-permute-start(bf16[2,256,256]{2,1,0:T(8,128)(2,1)S(1)} %collective-permute-done.3.refs_6_), channel_id=1, source_target_pairs={{0,1},{1,0},{2,3},{3,2},{4,5},{5,4},{6,7},{7,6},{8,9},{9,8},{10,11... | collective-permute-start | bytes 786440 | tf_op jit(solution)/shard_map/ppermute | solution.py:285
  28.4 1.1 %copy-start.4 = (bf16[2048,128]{1,0:T(8,128)(2,1)S(1)}, bf16[2048,128]{1,0:T(8,128)(2,1)}, u32[]{:S(2)}) copy-start(bf16[2048,128]{1,0:T(8,128)(2,1)} %refs_8_.1) | copy-start | bytes 1572868
  32.0 3.6 %collective-permute-start.19 = (bf16[4,256,256]{2,1,0:T(8,128)(2,1)S(1)}, bf16[4,256,256]{2,1,0:T(8,128)(2,1)S(1)}, u32[]{:S(2)}, u32[]{:S(2)}) collective-permute-start(bf16[4,256,256]{2,1,0:T(8,128)(2,1)S(1)} %get-tuple-element.31), channel_id=1, source_target_pairs={{0,1},{1,0},{2,3},{3,2},{4,5},{5,4},{6,7},{7,6},{8,9},{9,8},{10,11... | collective-permute-start | bytes 1572872 | tf_op jit(solution)/shard_map/ppermute | solution.py:285
  32.4 6.0 %collective-permute-start.13 = (bf16[64,128]{1,0:T(8,128)(2,1)S(1)}, bf16[64,128]{1,0:T(8,128)(2,1)S(1)}, u32[]{:S(2)}, u32[]{:S(2)}) collective-permute-start(bf16[64,128]{1,0:T(8,128)(2,1)S(1)} %get-tuple-element.44), channel_id=1, source_target_pairs={{0,17},{1,16},{2,19},{3,18},{4,21},{5,20},{6,23},{7,22},{8,25},{9,... | collective-permute-start | bytes 49160 | tf_op jit(solution)/shard_map/ppermute | solution.py:285
  33.1 6.9 %collective-permute-start.15 = (bf16[64,128]{1,0:T(8,128)(2,1)S(1)}, bf16[64,128]{1,0:T(8,128)(2,1)S(1)}, u32[]{:S(2)}, u32[]{:S(2)}) collective-permute-start(bf16[64,128]{1,0:T(8,128)(2,1)S(1)} %get-tuple-element.45), channel_id=1, source_target_pairs={{0,9},{1,8},{2,11},{3,10},{4,13},{5,12},{6,15},{7,14},{8,1},{9,0},... | collective-permute-start | bytes 49160 | tf_op jit(solution)/shard_map/ppermute | solution.py:285
  34.2 5.8 %collective-permute-start.14 = (bf16[64,128]{1,0:T(8,128)(2,1)S(1)}, bf16[64,128]{1,0:T(8,128)(2,1)S(1)}, u32[]{:S(2)}, u32[]{:S(2)}) collective-permute-start(bf16[64,128]{1,0:T(8,128)(2,1)S(1)} %get-tuple-element.46), channel_id=1, source_target_pairs={{0,24},{1,25},{2,26},{3,27},{4,28},{5,29},{6,30},{7,31},{8,16},{9,... | collective-permute-start | bytes 49160 | tf_op jit(solution)/shard_map/ppermute | solution.py:285
  35.8 18.1 %copy-start.1 = (bf16[4096,128]{1,0:T(8,128)(2,1)S(1)}, bf16[4096,128]{1,0:T(8,128)(2,1)}, u32[]{:S(2)}) copy-start(bf16[4096,128]{1,0:T(8,128)(2,1)} %feat_ref.1) | copy-start | bytes 3145732
  35.8 13.2 %collective-permute-start.20 = (bf16[256,256]{1,0:T(8,128)(2,1)S(1)}, bf16[256,256]{1,0:T(8,128)(2,1)S(1)}, u32[]{:S(2)}, u32[]{:S(2)}) collective-permute-start(bf16[256,256]{1,0:T(8,128)(2,1)S(1)} %get-tuple-element.36), channel_id=1, source_target_pairs={{0,6},{1,7},{2,4},{3,5},{4,2},{5,3},{6,0},{7,1},{8,14},{9,15},{10,... | collective-permute-start | bytes 393224 | tf_op jit(solution)/shard_map/ppermute | solution.py:285
  38.4 10.6 %collective-permute-start.22 = (bf16[256,256]{1,0:T(8,128)(2,1)S(1)}, bf16[256,256]{1,0:T(8,128)(2,1)S(1)}, u32[]{:S(2)}, u32[]{:S(2)}) collective-permute-start(bf16[256,256]{1,0:T(8,128)(2,1)S(1)} %get-tuple-element.37), channel_id=1, source_target_pairs={{0,5},{1,4},{2,7},{3,6},{4,1},{5,0},{6,3},{7,2},{8,13},{9,12},{10,... | collective-permute-start | bytes 393224 | tf_op jit(solution)/shard_map/ppermute | solution.py:285
  38.4 10.6 %collective-permute-start.21 = (bf16[256,256]{1,0:T(8,128)(2,1)S(1)}, bf16[256,256]{1,0:T(8,128)(2,1)S(1)}, u32[]{:S(2)}, u32[]{:S(2)}) collective-permute-start(bf16[256,256]{1,0:T(8,128)(2,1)S(1)} %get-tuple-element.38), channel_id=1, source_target_pairs={{0,3},{1,2},{2,1},{3,0},{4,7},{5,6},{6,5},{7,4},{8,11},{9,10},{10,... | collective-permute-start | bytes 393224 | tf_op jit(solution)/shard_map/ppermute | solution.py:285
  40.0 7.2 %collective-permute-start.16 = (bf16[1,64,128]{2,1,0:T(8,128)(2,1)S(1)}, bf16[1,64,128]{2,1,0:T(8,128)(2,1)S(1)}, u32[]{:S(2)}, u32[]{:S(2)}) collective-permute-start(bf16[1,64,128]{2,1,0:T(8,128)(2,1)S(1)} %fusion.11), channel_id=1, source_target_pairs={{0,3},{1,2},{2,1},{3,0},{4,7},{5,6},{6,5},{7,4},{8,11},{9,10},{10,... | collective-permute-start | bytes 49160 | tf_op jit(solution)/shard_map/ppermute | solution.py:285
  47.2 5.2 %collective-permute-start.17 = (bf16[2,64,128]{2,1,0:T(8,128)(2,1)S(1)}, bf16[2,64,128]{2,1,0:T(8,128)(2,1)S(1)}, u32[]{:S(2)}, u32[]{:S(2)}) collective-permute-start(bf16[2,64,128]{2,1,0:T(8,128)(2,1)S(1)} %pad_maximum_fusion.4), channel_id=1, source_target_pairs={{0,5},{1,4},{2,7},{3,6},{4,1},{5,0},{6,3},{7,2},{8,13},{9,12},{10,... | collective-permute-start | bytes 98312 | tf_op jit(solution)/shard_map/ppermute | solution.py:285
  49.1 4.8 %copy-start.5 = (s32[4096]{0:T(1024)S(1)}, s32[4096]{0:T(1024)}, u32[]{:S(2)}) copy-start(s32[4096]{0:T(1024)} %param.14) | copy-start | bytes 49156
  49.1 4.7 %copy-start.6 = (s32[32]{0:T(128)S(1)}, s32[32]{0:T(128)}, u32[]{:S(2)}) copy-start(s32[32]{0:T(128)} %owners_ref.1) | copy-start | bytes 388
  49.1 7.6 %collective-permute-start.26 = (bf16[256,256]{1,0:T(8,128)(2,1)S(1)}, bf16[256,256]{1,0:T(8,128)(2,1)S(1)}, u32[]{:S(2)}, u32[]{:S(2)}) collective-permute-start(bf16[256,256]{1,0:T(8,128)(2,1)S(1)} %fusion.3), channel_id=1, source_target_pairs={{0,25},{1,24},{2,27},{3,26},{4,29},{5,28},{6,31},{7,30},{8,17},{9,... | collective-permute-start | bytes 393224 | tf_op jit(solution)/shard_map/ppermute | solution.py:285
  51.1 7.5 %collective-permute-start.25 = (bf16[256,256]{1,0:T(8,128)(2,1)S(1)}, bf16[256,256]{1,0:T(8,128)(2,1)S(1)}, u32[]{:S(2)}, u32[]{:S(2)}) collective-permute-start(bf16[256,256]{1,0:T(8,128)(2,1)S(1)} %fusion.3), channel_id=1, source_target_pairs={{0,17},{1,16},{2,19},{3,18},{4,21},{5,20},{6,23},{7,22},{8,25},{9,... | collective-permute-start | bytes 393224 | tf_op jit(solution)/shard_map/ppermute | solution.py:285
  51.8 6.9 %collective-permute-start.24 = (bf16[256,256]{1,0:T(8,128)(2,1)S(1)}, bf16[256,256]{1,0:T(8,128)(2,1)S(1)}, u32[]{:S(2)}, u32[]{:S(2)}) collective-permute-start(bf16[256,256]{1,0:T(8,128)(2,1)S(1)} %fusion.3), channel_id=1, source_target_pairs={{0,9},{1,8},{2,11},{3,10},{4,13},{5,12},{6,15},{7,14},{8,1},{9,0},... | collective-permute-start | bytes 393224 | tf_op jit(solution)/shard_map/ppermute | solution.py:285
  52.3 6.4 %collective-permute-start.23 = (bf16[256,256]{1,0:T(8,128)(2,1)S(1)}, bf16[256,256]{1,0:T(8,128)(2,1)S(1)}, u32[]{:S(2)}, u32[]{:S(2)}) collective-permute-start(bf16[256,256]{1,0:T(8,128)(2,1)S(1)} %fusion.3), channel_id=1, source_target_pairs={{0,1},{1,0},{2,3},{3,2},{4,5},{5,4},{6,7},{7,6},{8,9},{9,8},{10,11... | collective-permute-start | bytes 393224 | tf_op jit(solution)/shard_map/ppermute | solution.py:285
  52.5 1.3 %collective-permute-start.18 = (bf16[4,64,128]{2,1,0:T(8,128)(2,1)S(1)}, bf16[4,64,128]{2,1,0:T(8,128)(2,1)S(1)}, u32[]{:S(2)}, u32[]{:S(2)}) collective-permute-start(bf16[4,64,128]{2,1,0:T(8,128)(2,1)S(1)} %pad_maximum_fusion.2.near), channel_id=1, source_target_pairs={{0,1},{1,0},{2,3},{3,2},{4,5},{5,4},{6,7},{7,6},{8,9},{9,8},{10,11... | collective-permute-start | bytes 196616 | tf_op jit(solution)/shard_map/ppermute | solution.py:285

commit v7 on v6

--- a/solution.py
+++ b/solution.py
@@ -86,11 +86,17 @@
     total = None
     for i in range(count):
         mine = me ^ chip(reverse(begin + i, pairs))
-        core = lax.rem(mine, 2)
-        weight[i, pl.ds(pl.multiple_of(core * rows, rows), rows), :] = near[i]
-        weight[i, pl.ds(pl.multiple_of((1 - core) * rows, rows), rows), :] = far[i]
-        chunk = pl.ds(pl.multiple_of(lax.div(mine, 2) * (2 * rows), 2 * rows), 2 * rows)
-        term = jnp.dot(hid[:, chunk], weight[i], preferred_element_type=F32)
+        if rows % 128 == 0:
+            term = 0.0
+            for piece, owner in ((near, mine), (far, mine ^ 1)):
+                chunk = pl.ds(pl.multiple_of(owner * rows, rows), rows)
+                term += jnp.dot(hid[:, chunk], piece[i], preferred_element_type=F32)
+        else:
+            core = lax.rem(mine, 2)
+            weight[i, pl.ds(pl.multiple_of(core * rows, rows), rows), :] = near[i]
+            weight[i, pl.ds(pl.multiple_of((1 - core) * rows, rows), rows), :] = far[i]
+            chunk = pl.ds(pl.multiple_of(lax.div(mine, 2) * (2 * rows), 2 * rows), 2 * rows)
+            term = jnp.dot(hid[:, chunk], weight[i], preferred_element_type=F32)
         total = term if total is None else total + term
     return total
 
@@ -181,11 +187,16 @@
     for k in range(parts):
         up_ref[k] = up[k * t_rows : (k + 1) * t_rows].astype(BF16)
     for k in range(pairs):
-        chunk = pl.ds(pl.multiple_of((pair ^ k) * (2 * rows), 2 * rows), 2 * rows)
-        term[...] = contract(hid[:, chunk], q_grad, 0, 0)
         mine = 1 ^ core ^ odd(k)
-        keep_ref[k] = term[pl.ds(pl.multiple_of(mine * rows, rows), rows), :].astype(BF16)
-        give_ref[k] = term[pl.ds(pl.multiple_of((1 - mine) * rows, rows), rows), :].astype(BF16)
+        if rows % 128 == 0:
+            for out_ref, owner in ((keep_ref, mine), (give_ref, 1 - mine)):
+                chunk = pl.ds(pl.multiple_of((pair ^ k) * (2 * rows) + owner * rows, rows), rows)
+                out_ref[k] = contract(hid[:, chunk], q_grad, 0, 0).astype(BF16)
+        else:
+            chunk = pl.ds(pl.multiple_of((pair ^ k) * (2 * rows), 2 * rows), 2 * rows)
+            term[...] = contract(hid[:, chunk], q_grad, 0, 0)
+            keep_ref[k] = term[pl.ds(pl.multiple_of(mine * rows, rows), rows), :].astype(BF16)
+            give_ref[k] = term[pl.ds(pl.multiple_of((1 - mine) * rows, rows), rows), :].astype(BF16)
 
 
 def attend(pooled, hid, query, near, far, w_out):

time: 59.9 us -> 59.7 us (level)
  transfers between devices with their start and end apart: 27 -> 27, of which waited for: 10 -> 10; matrix products, arithmetic and copies ran while one was open for 1% -> 1% of each run, Pallas kernels for 11% -> 12%
where the time goes in v7:
time: 59.7 us; the launch traced here: 59.5 us
  starting transfers between devices  31 us (52%)
  waiting for transfers between devices  16.8 us (28%)
  Pallas kernels  10.2 us (17%)
  between operations  0.87 us (1%)
    ppermute x27, starting transfers between devices, swap(): return lax.ppermute(x, ('group', 'shard'), pairs)  31 us
    ppermute x27, waiting for transfers between devices, swap(): return lax.ppermute(x, ('group', 'shard'), pairs)  16.8 us
    pallas_call x1, Pallas kernels, pool(): pl.pallas_call(pool_kernel, in_specs=[whole] * 4, out_specs=[VMEM, VMEM],...  3.09 us
    pallas_call x1, Pallas kernels, unpool(): pl.pallas_call(unpool_kernel, grid_spec=pltpu.PrefetchScalarGridSpec(num_...  2.83 us
    pallas_call x1, Pallas kernels, attend(): pl.pallas_call(functools.partial(attend_kernel, parts), in_specs=[VMEM] *...  2.27 us
  transfers between devices with their start and end apart: 27, of which 10 were waited for; matrix products, arithmetic and copies ran while one was open for 1% of the time, Pallas kernels for 12%

profile of v7, /device:TPU:0, one launch (start us, length us, event | category | flops | bytes accessed | tf_op | source)
XLA Modules:
  0.0 59.5 jit_solution(14479175934915937419)
XLA Ops:
  0.6 0.0 copy-start
  0.6 2.4 %collective-permute-start.2 = (bf16[1,64,2048]{2,1,0:T(8,128)(2,1)}, bf16[1,64,2048]{2,1,0:T(8,128)(2,1)S(1)}, u32[]{:S(2)}, u32[]{:S(2)}) collective-permute-start(bf16[1,64,2048]{2,1,0:T(8,128)(2,1)} %bitcast.50), channel_id=1, source_target_pairs={{0,9},{1,8},{2,11},{3,10},{4,13},{5,12},{6,15},{7,14},{8,1},{9,0},... | collective-permute-start | bytes 786440 | tf_op jit(solution)/shard_map/ppermute | solution.py:296
  3.1 2.9 %collective-permute-start.1 = (bf16[1,256,256]{2,1,0:T(8,128)(2,1)S(1)}, bf16[1,256,256]{2,1,0:T(8,128)(2,1)S(1)}, u32[]{:S(2)}, u32[]{:S(2)}) collective-permute-start(bf16[1,256,256]{2,1,0:T(8,128)(2,1)S(1)} %dynamic-slice_bitcast_fusion), channel_id=1, source_target_pairs={{0,5},{1,4},{2,7},{3,6},{4,1},{5,0},{6,3},{7,2},{8,13},{9,12},{10,... | collective-permute-start | bytes 393224 | tf_op jit(solution)/shard_map/ppermute | solution.py:296
  6.0 3.1 %pool.1 = (f32[4,64,384]{2,1,0:T(8,128)}, bf16[4,64,384]{2,1,0:T(8,128)(2,1)}) custom-call(s32[32]{0:T(128)} %owners_ref.1, s32[32,128]{1,0:T(8,128)} %bitcast.53, bf16[4096,128]{1,0:T(8,128)(2,1)} %feat_ref.1, bf16[4096,128]{1,0:T(8,128)(2,1)} %grad_hbm.1), custom_call_target="tpu_custom_call" | custom-call | bytes 3000000 | tf_op jit(solution)/shard_map/pool/pallas_call | solution.py:65
  9.2 0.1 collective-permute-start
  9.2 0.9 %collective-permute-done.2 = bf16[1,64,2048]{2,1,0:T(8,128)(2,1)S(1)} collective-permute-done((bf16[1,64,2048]{2,1,0:T(8,128)(2,1)}, bf16[1,64,2048]{2,1,0:T(8,128)(2,1)S(1)}, u32[]{:S(2)}, u32[]{:S(2)}) %collective-permute-start.2) | collective-permute-done | bytes 262176 | tf_op jit(solution)/shard_map/ppermute | solution.py:296
  10.1 0.1 pad_maximum_fusion
  10.1 2.2 %collective-permute-start.10 = (bf16[2,64,2048]{2,1,0:T(8,128)(2,1)S(1)}, bf16[2,64,2048]{2,1,0:T(8,128)(2,1)S(1)}, u32[]{:S(2)}, u32[]{:S(2)}) collective-permute-start(bf16[2,64,2048]{2,1,0:T(8,128)(2,1)S(1)} %pad_maximum_fusion), channel_id=1, source_target_pairs={{0,17},{1,16},{2,19},{3,18},{4,21},{5,20},{6,23},{7,22},{8,25},{9,... | collective-permute-start | bytes 1572872 | tf_op jit(solution)/shard_map/ppermute | solution.py:296
  12.3 0.0 collective-permute-done.1
  12.3 0.1 fusion.13
  12.4 2.6 %collective-permute-start.4 = (bf16[64,384]{1,0:T(8,128)(2,1)S(1)}, bf16[64,384]{1,0:T(8,128)(2,1)S(1)}, u32[]{:S(2)}, u32[]{:S(2)}) collective-permute-start(bf16[64,384]{1,0:T(8,128)(2,1)S(1)} %get-tuple-element.41), channel_id=1, source_target_pairs={{0,5},{1,4},{2,7},{3,6},{4,1},{5,0},{6,3},{7,2},{8,13},{9,12},{10,... | collective-permute-start | bytes 147464 | tf_op jit(solution)/shard_map/ppermute | solution.py:296
  15.1 1.3 %collective-permute-start.6 = (bf16[64,384]{1,0:T(8,128)(2,1)S(1)}, bf16[64,384]{1,0:T(8,128)(2,1)S(1)}, u32[]{:S(2)}, u32[]{:S(2)}) collective-permute-start(bf16[64,384]{1,0:T(8,128)(2,1)S(1)} %get-tuple-element.42), channel_id=1, source_target_pairs={{0,6},{1,7},{2,4},{3,5},{4,2},{5,3},{6,0},{7,1},{8,14},{9,15},{10,... | collective-permute-start | bytes 147464 | tf_op jit(solution)/shard_map/ppermute | solution.py:296
  16.4 0.1 collective-permute-start.5
  16.6 1.7 %collective-permute-start.3 = (bf16[2,256,256]{2,1,0:T(8,128)(2,1)S(1)}, bf16[2,256,256]{2,1,0:T(8,128)(2,1)S(1)}, u32[]{:S(2)}, u32[]{:S(2)}) collective-permute-start(bf16[2,256,256]{2,1,0:T(8,128)(2,1)S(1)} %pad_maximum_fusion.1.refs_8_), channel_id=1, source_target_pairs={{0,3},{1,2},{2,1},{3,0},{4,7},{5,6},{6,5},{7,4},{8,11},{9,10},{10,... | collective-permute-start | bytes 786440 | tf_op jit(solution)/shard_map/ppermute | solution.py:296
  18.3 3.2 %collective-permute-done.6 = bf16[64,384]{1,0:T(8,128)(2,1)S(1)} collective-permute-done((bf16[64,384]{1,0:T(8,128)(2,1)S(1)}, bf16[64,384]{1,0:T(8,128)(2,1)S(1)}, u32[]{:S(2)}, u32[]{:S(2)}) %collective-permute-start.6) | collective-permute-done | bytes 49184 | tf_op jit(solution)/shard_map/ppermute | solution.py:296
  21.4 0.1 collective-permute-done.5
  21.5 0.1 slice_reduce_fusion
  21.7 0.1 fusion.7
  21.8 2.0 %collective-permute-start.9 = (bf16[64,256]{1,0:T(8,128)(2,1)S(1)}, bf16[64,256]{1,0:T(8,128)(2,1)S(1)}, u32[]{:S(2)}, u32[]{:S(2)}) collective-permute-start(bf16[64,256]{1,0:T(8,128)(2,1)S(1)} %pad_maximum_fusion.3.refs_4_.refs_0_), channel_id=1, source_target_pairs={{0,24},{1,25},{2,26},{3,27},{4,28},{5,29},{6,30},{7,31},{8,16},{9,... | collective-permute-start | bytes 98312 | tf_op jit(solution)/shard_map/ppermute | solution.py:296
  23.8 0.5 collective-permute-start.8
  24.3 0.8 %collective-permute-start.7 = (bf16[64,256]{1,0:T(8,128)(2,1)S(1)}, bf16[64,256]{1,0:T(8,128)(2,1)S(1)}, u32[]{:S(2)}, u32[]{:S(2)}) collective-permute-start(bf16[64,256]{1,0:T(8,128)(2,1)S(1)} %pad_maximum_fusion.3.refs_4_.refs_0_), channel_id=1, source_target_pairs={{0,9},{1,8},{2,11},{3,10},{4,13},{5,12},{6,15},{7,14},{8,1},{9,0},... | collective-permute-start | bytes 98312 | tf_op jit(solution)/shard_map/ppermute | solution.py:296
  25.1 1.6 %collective-permute-done.9.refs_7_.refs_3_ = bf16[64,256]{1,0:T(8,128)(2,1)S(1)} collective-permute-done((bf16[64,256]{1,0:T(8,128)(2,1)S(1)}, bf16[64,256]{1,0:T(8,128)(2,1)S(1)}, u32[]{:S(2)}, u32[]{:S(2)}) %collective-permute-start.9) | collective-permute-done | bytes 32800 | tf_op jit(solution)/shard_map/ppermute | solution.py:296
  26.7 0.8 %collective-permute-done.8.refs_6_.refs_2_ = bf16[64,256]{1,0:T(8,128)(2,1)S(1)} collective-permute-done((bf16[64,256]{1,0:T(8,128)(2,1)S(1)}, bf16[64,256]{1,0:T(8,128)(2,1)S(1)}, u32[]{:S(2)}, u32[]{:S(2)}) %collective-permute-start.8) | collective-permute-done | bytes 32800 | tf_op jit(solution)/shard_map/ppermute | solution.py:296
  27.4 0.2 collective-permute-done.7.refs_5_.refs_1_
  27.6 0.7 %collective-permute-start.12 = (bf16[2,256,256]{2,1,0:T(8,128)(2,1)S(1)}, bf16[2,256,256]{2,1,0:T(8,128)(2,1)S(1)}, u32[]{:S(2)}, u32[]{:S(2)}) collective-permute-start(bf16[2,256,256]{2,1,0:T(8,128)(2,1)S(1)} %collective-permute-done.3.refs_6_), channel_id=1, source_target_pairs={{0,1},{1,0},{2,3},{3,2},{4,5},{5,4},{6,7},{7,6},{8,9},{9,8},{10,11... | collective-permute-start | bytes 786440 | tf_op jit(solution)/shard_map/ppermute | solution.py:296
  28.4 0.9 %hidden.1 = (bf16[256,2048]{1,0:T(8,128)(2,1)S(1)}, f32[256,256]{1,0:T(8,128)S(1)}) custom-call(bf16[64,2048]{1,0:T(8,128)(2,1)S(1)} %copy-done.2, bf16[64,2048]{1,0:T(8,128)(2,1)S(1)} %bitcast.52, bf16[64,2048]{1,0:T(8,128)(2,1)S(1)} %get-tuple-element.40.refs_2_, bf16[64,2048]{1,0:T(8,128)(2,1)S(1)} %get-tuple-element.39.refs_3_, ...), custom_call_target="tpu_custom_call" | custom-call | tf_op jit(solution)/shard_map/hidden/pallas_call | solution.py:125
  29.3 0.1 collective-permute-done.12.refs_7_
  29.5 2.3 %attend.1 = (bf16[4,64,128]{2,1,0:T(8,128)(2,1)S(1)}, bf16[4,256,256]{2,1,0:T(8,128)(2,1)S(1)}, bf16[4,256,256]{2,1,0:T(8,128)(2,1)S(1)}) custom-call(bf16[64,256]{1,0:T(8,128)(2,1)S(1)} %pad_maximum_fusion.3.refs_4_.refs_0_, bf16[64,256]{1,0:T(8,128)(2,1)S(1)} %collective-permute-done.7.refs_5_.refs_1_, ...), custom_call_target="tpu_custom_call" | custom-call | bytes 3000000 | tf_op jit(solution)/shard_map/attend/pallas_call | solution.py:208
  31.7 0.4 collective-permute-start.19
  32.2 0.7 %collective-permute-start.13 = (bf16[64,128]{1,0:T(8,128)(2,1)S(1)}, bf16[64,128]{1,0:T(8,128)(2,1)S(1)}, u32[]{:S(2)}, u32[]{:S(2)}) collective-permute-start(bf16[64,128]{1,0:T(8,128)(2,1)S(1)} %get-tuple-element.44), channel_id=1, source_target_pairs={{0,17},{1,16},{2,19},{3,18},{4,21},{5,20},{6,23},{7,22},{8,25},{9,... | collective-permute-start | bytes 49160 | tf_op jit(solution)/shard_map/ppermute | solution.py:296
  32.9 1.1 %collective-permute-start.15 = (bf16[64,128]{1,0:T(8,128)(2,1)S(1)}, bf16[64,128]{1,0:T(8,128)(2,1)S(1)}, u32[]{:S(2)}, u32[]{:S(2)}) collective-permute-start(bf16[64,128]{1,0:T(8,128)(2,1)S(1)} %get-tuple-element.45), channel_id=1, source_target_pairs={{0,9},{1,8},{2,11},{3,10},{4,13},{5,12},{6,15},{7,14},{8,1},{9,0},... | collective-permute-start | bytes 49160 | tf_op jit(solution)/shard_map/ppermute | solution.py:296
  34.0 1.4 %collective-permute-start.14 = (bf16[64,128]{1,0:T(8,128)(2,1)S(1)}, bf16[64,128]{1,0:T(8,128)(2,1)S(1)}, u32[]{:S(2)}, u32[]{:S(2)}) collective-permute-start(bf16[64,128]{1,0:T(8,128)(2,1)S(1)} %get-tuple-element.46), channel_id=1, source_target_pairs={{0,24},{1,25},{2,26},{3,27},{4,28},{5,29},{6,30},{7,31},{8,16},{9,... | collective-permute-start | bytes 49160 | tf_op jit(solution)/shard_map/ppermute | solution.py:296
  35.4 0.1 fusion.12
  35.6 2.6 %collective-permute-start.20 = (bf16[256,256]{1,0:T(8,128)(2,1)S(1)}, bf16[256,256]{1,0:T(8,128)(2,1)S(1)}, u32[]{:S(2)}, u32[]{:S(2)}) collective-permute-start(bf16[256,256]{1,0:T(8,128)(2,1)S(1)} %get-tuple-element.36), channel_id=1, source_target_pairs={{0,6},{1,7},{2,4},{3,5},{4,2},{5,3},{6,0},{7,1},{8,14},{9,15},{10,... | collective-permute-start | bytes 393224 | tf_op jit(solution)/shard_map/ppermute | solution.py:296
  38.2 1.6 %collective-permute-start.21 = (bf16[256,256]{1,0:T(8,128)(2,1)S(1)}, bf16[256,256]{1,0:T(8,128)(2,1)S(1)}, u32[]{:S(2)}, u32[]{:S(2)}) collective-permute-start(bf16[256,256]{1,0:T(8,128)(2,1)S(1)} %get-tuple-element.38), channel_id=1, source_target_pairs={{0,3},{1,2},{2,1},{3,0},{4,7},{5,6},{6,5},{7,4},{8,11},{9,10},{10,... | collective-permute-start | bytes 393224 | tf_op jit(solution)/shard_map/ppermute | solution.py:296
  39.8 0.2 collective-permute-start.16
  40.0 7.0 %collective-permute-done.16 = bf16[1,64,128]{2,1,0:T(8,128)(2,1)S(1)} collective-permute-done((bf16[1,64,128]{2,1,0:T(8,128)(2,1)S(1)}, bf16[1,64,128]{2,1,0:T(8,128)(2,1)S(1)}, u32[]{:S(2)}, u32[]{:S(2)}) %collective-permute-start.16) | collective-permute-done | bytes 16416 | tf_op jit(solution)/shard_map/ppermute | solution.py:296
  47.0 1.8 %collective-permute-start.17 = (bf16[2,64,128]{2,1,0:T(8,128)(2,1)S(1)}, bf16[2,64,128]{2,1,0:T(8,128)(2,1)S(1)}, u32[]{:S(2)}, u32[]{:S(2)}) collective-permute-start(bf16[2,64,128]{2,1,0:T(8,128)(2,1)S(1)} %pad_maximum_fusion.4), channel_id=1, source_target_pairs={{0,5},{1,4},{2,7},{3,6},{4,1},{5,0},{6,3},{7,2},{8,13},{9,12},{10,... | collective-permute-start | bytes 98312 | tf_op jit(solution)/shard_map/ppermute | solution.py:296
  48.8 0.1 fusion.3
  48.9 2.0 %collective-permute-start.26 = (bf16[256,256]{1,0:T(8,128)(2,1)S(1)}, bf16[256,256]{1,0:T(8,128)(2,1)S(1)}, u32[]{:S(2)}, u32[]{:S(2)}) collective-permute-start(bf16[256,256]{1,0:T(8,128)(2,1)S(1)} %fusion.3), channel_id=1, source_target_pairs={{0,25},{1,24},{2,27},{3,26},{4,29},{5,28},{6,31},{7,30},{8,17},{9,... | collective-permute-start | bytes 393224 | tf_op jit(solution)/shard_map/ppermute | solution.py:296
  50.9 0.7 %collective-permute-start.25 = (bf16[256,256]{1,0:T(8,128)(2,1)S(1)}, bf16[256,256]{1,0:T(8,128)(2,1)S(1)}, u32[]{:S(2)}, u32[]{:S(2)}) collective-permute-start(bf16[256,256]{1,0:T(8,128)(2,1)S(1)} %fusion.3), channel_id=1, source_target_pairs={{0,17},{1,16},{2,19},{3,18},{4,21},{5,20},{6,23},{7,22},{8,25},{9,... | collective-permute-start | bytes 393224 | tf_op jit(solution)/shard_map/ppermute | solution.py:296
  51.5 0.5 collective-permute-start.24
  52.0 0.2 collective-permute-start.23
  52.3 0.4 collective-permute-start.18
  52.6 1.0 %collective-permute-done.18.far = bf16[4,64,128]{2,1,0:T(8,128)(2,1)S(1)} collective-permute-done((bf16[4,64,128]{2,1,0:T(8,128)(2,1)S(1)}, bf16[4,64,128]{2,1,0:T(8,128)(2,1)S(1)}, u32[]{:S(2)}, u32[]{:S(2)}) %collective-permute-start.18) | collective-permute-done | bytes 65568 | tf_op jit(solution)/shard_map/ppermute | solution.py:296
  53.6 2.8 %unpool.1 = bf16[4096,128]{1,0:T(8,128)(2,1)} custom-call(s32[32]{0:T(128)S(1)} %copy-done.6, s32[32,128]{1,0:T(8,128)S(1)} %bitcast.54, bf16[4096,128]{1,0:T(8,128)(2,1)S(1)} %copy-done.1, bf16[4,64,128]{2,1,0:T(8,128)(2,1)S(1)} %pad_maximum_fusion.2.near, bf16[4,64,128]{2,1,0:T(8,128)(2,1)S(1)} %collective-permute-done.18.far), custom_call_target="tpu_custom_call" | custom-call | tf_op jit(solution)/shard_map/unpool/pallas_call | solution.py:252
  56.4 2.0 %collective-permute-done.25.refs_2_ = bf16[256,256]{1,0:T(8,128)(2,1)S(1)} collective-permute-done((bf16[256,256]{1,0:T(8,128)(2,1)S(1)}, bf16[256,256]{1,0:T(8,128)(2,1)S(1)}, u32[]{:S(2)}, u32[]{:S(2)}) %collective-permute-start.25) | collective-permute-done | bytes 131104 | tf_op jit(solution)/shard_map/ppermute | solution.py:296
  58.4 1.1 %spread.1 = f32[256,1024]{1,0:T(8,128)} custom-call(bf16[256,256]{1,0:T(8,128)(2,1)S(1)} %collective-permute-done.23.refs_0_, bf16[256,256]{1,0:T(8,128)(2,1)S(1)} %collective-permute-done.24.refs_1_, bf16[256,256]{1,0:T(8,128)(2,1)S(1)} %collective-permute-done.25.refs_2_, bf16[256,256]{1,0:T(8,128)(2,1)S(1)} %collective-permute-done.26.refs_3_), custom_call_target="tpu_custom_call" | custom-call | tf_op jit(solution)/shard_map/spread/pallas_call | solution.py:282
  (46 shorter events, 0.3 us)
Async XLA Ops:
  0.6 2.5 %copy-start = (bf16[256,1024]{1,0:T(8,128)(2,1)S(1)}, bf16[256,1024]{1,0:T(8,128)(2,1)}, u32[]{:S(2)}) copy-start(bf16[256,1024]{1,0:T(8,128)(2,1)} %param.9) | copy-start | bytes 1572868
  0.6 9.4 %collective-permute-start.2 = (bf16[1,64,2048]{2,1,0:T(8,128)(2,1)}, bf16[1,64,2048]{2,1,0:T(8,128)(2,1)S(1)}, u32[]{:S(2)}, u32[]{:S(2)}) collective-permute-start(bf16[1,64,2048]{2,1,0:T(8,128)(2,1)} %bitcast.50), channel_id=1, source_target_pairs={{0,9},{1,8},{2,11},{3,10},{4,13},{5,12},{6,15},{7,14},{8,1},{9,0},... | collective-permute-start | bytes 786440 | tf_op jit(solution)/shard_map/ppermute | solution.py:296
  3.1 9.2 %collective-permute-start.1 = (bf16[1,256,256]{2,1,0:T(8,128)(2,1)S(1)}, bf16[1,256,256]{2,1,0:T(8,128)(2,1)S(1)}, u32[]{:S(2)}, u32[]{:S(2)}) collective-permute-start(bf16[1,256,256]{2,1,0:T(8,128)(2,1)S(1)} %dynamic-slice_bitcast_fusion), channel_id=1, source_target_pairs={{0,5},{1,4},{2,7},{3,6},{4,1},{5,0},{6,3},{7,2},{8,13},{9,12},{10,... | collective-permute-start | bytes 393224 | tf_op jit(solution)/shard_map/ppermute | solution.py:296
  6.0 4.0 %copy-start.2 = (bf16[64,2048]{1,0:T(8,128)(2,1)S(1)}, bf16[64,2048]{1,0:T(8,128)(2,1)}, u32[]{:S(2)}) copy-start(bf16[64,2048]{1,0:T(8,128)(2,1)} %refs_0_.1) | copy-start | bytes 786436
  9.1 3.2 %copy-start.7 = (f32[4,64,384]{2,1,0:T(8,128)S(1)}, f32[4,64,384]{2,1,0:T(8,128)}, u32[]{:S(2)}) copy-start(f32[4,64,384]{2,1,0:T(8,128)} %get-tuple-element.19) | copy-start | bytes 1179652
  9.2 3.2 %collective-permute-start = (bf16[4,64,384]{2,1,0:T(8,128)(2,1)}, bf16[4,64,384]{2,1,0:T(8,128)(2,1)S(1)}, u32[]{:S(2)}, u32[]{:S(2)}) collective-permute-start(bf16[4,64,384]{2,1,0:T(8,128)(2,1)} %get-tuple-element.17), channel_id=1, source_target_pairs={{0,1},{1,0},{2,3},{3,2},{4,5},{5,4},{6,7},{7,6},{8,9},{9,8},{10,11... | collective-permute-start | bytes 589832 | tf_op jit(solution)/shard_map/ppermute | solution.py:296
  10.1 18.2 %collective-permute-start.10 = (bf16[2,64,2048]{2,1,0:T(8,128)(2,1)S(1)}, bf16[2,64,2048]{2,1,0:T(8,128)(2,1)S(1)}, u32[]{:S(2)}, u32[]{:S(2)}) collective-permute-start(bf16[2,64,2048]{2,1,0:T(8,128)(2,1)S(1)} %pad_maximum_fusion), channel_id=1, source_target_pairs={{0,17},{1,16},{2,19},{3,18},{4,21},{5,20},{6,23},{7,22},{8,25},{9,... | collective-permute-start | bytes 1572872 | tf_op jit(solution)/shard_map/ppermute | solution.py:296
  12.4 5.8 %collective-permute-start.4 = (bf16[64,384]{1,0:T(8,128)(2,1)S(1)}, bf16[64,384]{1,0:T(8,128)(2,1)S(1)}, u32[]{:S(2)}, u32[]{:S(2)}) collective-permute-start(bf16[64,384]{1,0:T(8,128)(2,1)S(1)} %get-tuple-element.41), channel_id=1, source_target_pairs={{0,5},{1,4},{2,7},{3,6},{4,1},{5,0},{6,3},{7,2},{8,13},{9,12},{10,... | collective-permute-start | bytes 147464 | tf_op jit(solution)/shard_map/ppermute | solution.py:296
  15.1 6.3 %collective-permute-start.6 = (bf16[64,384]{1,0:T(8,128)(2,1)S(1)}, bf16[64,384]{1,0:T(8,128)(2,1)S(1)}, u32[]{:S(2)}, u32[]{:S(2)}) collective-permute-start(bf16[64,384]{1,0:T(8,128)(2,1)S(1)} %get-tuple-element.42), channel_id=1, source_target_pairs={{0,6},{1,7},{2,4},{3,5},{4,2},{5,3},{6,0},{7,1},{8,14},{9,15},{10,... | collective-permute-start | bytes 147464 | tf_op jit(solution)/shard_map/ppermute | solution.py:296
  16.4 5.1 %collective-permute-start.5 = (bf16[64,384]{1,0:T(8,128)(2,1)S(1)}, bf16[64,384]{1,0:T(8,128)(2,1)S(1)}, u32[]{:S(2)}, u32[]{:S(2)}) collective-permute-start(bf16[64,384]{1,0:T(8,128)(2,1)S(1)} %get-tuple-element.43), channel_id=1, source_target_pairs={{0,3},{1,2},{2,1},{3,0},{4,7},{5,6},{6,5},{7,4},{8,11},{9,10},{10,... | collective-permute-start | bytes 147464 | tf_op jit(solution)/shard_map/ppermute | solution.py:296
  16.6 11.0 %collective-permute-start.3 = (bf16[2,256,256]{2,1,0:T(8,128)(2,1)S(1)}, bf16[2,256,256]{2,1,0:T(8,128)(2,1)S(1)}, u32[]{:S(2)}, u32[]{:S(2)}) collective-permute-start(bf16[2,256,256]{2,1,0:T(8,128)(2,1)S(1)} %pad_maximum_fusion.1.refs_8_), channel_id=1, source_target_pairs={{0,3},{1,2},{2,1},{3,0},{4,7},{5,6},{6,5},{7,4},{8,11},{9,10},{10,... | collective-permute-start | bytes 786440 | tf_op jit(solution)/shard_map/ppermute | solution.py:296
  21.8 6.6 %copy-start.3 = (bf16[128,2048]{1,0:T(8,128)(2,1)S(1)}, bf16[128,2048]{1,0:T(8,128)(2,1)}, u32[]{:S(2)}) copy-start(bf16[128,2048]{1,0:T(8,128)(2,1)} %refs_10_.1) | copy-start | bytes 1572868
  21.8 4.9 %collective-permute-start.9 = (bf16[64,256]{1,0:T(8,128)(2,1)S(1)}, bf16[64,256]{1,0:T(8,128)(2,1)S(1)}, u32[]{:S(2)}, u32[]{:S(2)}) collective-permute-start(bf16[64,256]{1,0:T(8,128)(2,1)S(1)} %pad_maximum_fusion.3.refs_4_.refs_0_), channel_id=1, source_target_pairs={{0,24},{1,25},{2,26},{3,27},{4,28},{5,29},{6,30},{7,31},{8,16},{9,... | collective-permute-start | bytes 98312 | tf_op jit(solution)/shard_map/ppermute | solution.py:296
  23.8 3.7 %collective-permute-start.8 = (bf16[64,256]{1,0:T(8,128)(2,1)S(1)}, bf16[64,256]{1,0:T(8,128)(2,1)S(1)}, u32[]{:S(2)}, u32[]{:S(2)}) collective-permute-start(bf16[64,256]{1,0:T(8,128)(2,1)S(1)} %pad_maximum_fusion.3.refs_4_.refs_0_), channel_id=1, source_target_pairs={{0,17},{1,16},{2,19},{3,18},{4,21},{5,20},{6,23},{7,22},{8,25},{9,... | collective-permute-start | bytes 98312 | tf_op jit(solution)/shard_map/ppermute | solution.py:296
  24.3 3.3 %collective-permute-start.7 = (bf16[64,256]{1,0:T(8,128)(2,1)S(1)}, bf16[64,256]{1,0:T(8,128)(2,1)S(1)}, u32[]{:S(2)}, u32[]{:S(2)}) collective-permute-start(bf16[64,256]{1,0:T(8,128)(2,1)S(1)} %pad_maximum_fusion.3.refs_4_.refs_0_), channel_id=1, source_target_pairs={{0,9},{1,8},{2,11},{3,10},{4,13},{5,12},{6,15},{7,14},{8,1},{9,0},... | collective-permute-start | bytes 98312 | tf_op jit(solution)/shard_map/ppermute | solution.py:296
  26.7 1.7 %collective-permute-start.11 = (bf16[2,256,256]{2,1,0:T(8,128)(2,1)S(1)}, bf16[2,256,256]{2,1,0:T(8,128)(2,1)S(1)}, u32[]{:S(2)}, u32[]{:S(2)}) collective-permute-start(bf16[2,256,256]{2,1,0:T(8,128)(2,1)S(1)} %pad_maximum_fusion.1.refs_8_), channel_id=1, source_target_pairs={{0,1},{1,0},{2,3},{3,2},{4,5},{5,4},{6,7},{7,6},{8,9},{9,8},{10,11... | collective-permute-start | bytes 786440 | tf_op jit(solution)/shard_map/ppermute | solution.py:296
  27.6 1.8 %collective-permute-start.12 = (bf16[2,256,256]{2,1,0:T(8,128)(2,1)S(1)}, bf16[2,256,256]{2,1,0:T(8,128)(2,1)S(1)}, u32[]{:S(2)}, u32[]{:S(2)}) collective-permute-start(bf16[2,256,256]{2,1,0:T(8,128)(2,1)S(1)} %collective-permute-done.3.refs_6_), channel_id=1, source_target_pairs={{0,1},{1,0},{2,3},{3,2},{4,5},{5,4},{6,7},{7,6},{8,9},{9,8},{10,11... | collective-permute-start | bytes 786440 | tf_op jit(solution)/shard_map/ppermute | solution.py:296
  28.4 1.1 %copy-start.4 = (bf16[2048,128]{1,0:T(8,128)(2,1)S(1)}, bf16[2048,128]{1,0:T(8,128)(2,1)}, u32[]{:S(2)}) copy-start(bf16[2048,128]{1,0:T(8,128)(2,1)} %refs_8_.1) | copy-start | bytes 1572868
  31.7 3.6 %collective-permute-start.19 = (bf16[4,256,256]{2,1,0:T(8,128)(2,1)S(1)}, bf16[4,256,256]{2,1,0:T(8,128)(2,1)S(1)}, u32[]{:S(2)}, u32[]{:S(2)}) collective-permute-start(bf16[4,256,256]{2,1,0:T(8,128)(2,1)S(1)} %get-tuple-element.31), channel_id=1, source_target_pairs={{0,1},{1,0},{2,3},{3,2},{4,5},{5,4},{6,7},{7,6},{8,9},{9,8},{10,11... | collective-permute-start | bytes 1572872 | tf_op jit(solution)/shard_map/ppermute | solution.py:296
  32.2 6.0 %collective-permute-start.13 = (bf16[64,128]{1,0:T(8,128)(2,1)S(1)}, bf16[64,128]{1,0:T(8,128)(2,1)S(1)}, u32[]{:S(2)}, u32[]{:S(2)}) collective-permute-start(bf16[64,128]{1,0:T(8,128)(2,1)S(1)} %get-tuple-element.44), channel_id=1, source_target_pairs={{0,17},{1,16},{2,19},{3,18},{4,21},{5,20},{6,23},{7,22},{8,25},{9,... | collective-permute-start | bytes 49160 | tf_op jit(solution)/shard_map/ppermute | solution.py:296
  32.9 6.8 %collective-permute-start.15 = (bf16[64,128]{1,0:T(8,128)(2,1)S(1)}, bf16[64,128]{1,0:T(8,128)(2,1)S(1)}, u32[]{:S(2)}, u32[]{:S(2)}) collective-permute-start(bf16[64,128]{1,0:T(8,128)(2,1)S(1)} %get-tuple-element.45), channel_id=1, source_target_pairs={{0,9},{1,8},{2,11},{3,10},{4,13},{5,12},{6,15},{7,14},{8,1},{9,0},... | collective-permute-start | bytes 49160 | tf_op jit(solution)/shard_map/ppermute | solution.py:296
  34.0 5.8 %collective-permute-start.14 = (bf16[64,128]{1,0:T(8,128)(2,1)S(1)}, bf16[64,128]{1,0:T(8,128)(2,1)S(1)}, u32[]{:S(2)}, u32[]{:S(2)}) collective-permute-start(bf16[64,128]{1,0:T(8,128)(2,1)S(1)} %get-tuple-element.46), channel_id=1, source_target_pairs={{0,24},{1,25},{2,26},{3,27},{4,28},{5,29},{6,30},{7,31},{8,16},{9,... | collective-permute-start | bytes 49160 | tf_op jit(solution)/shard_map/ppermute | solution.py:296
  35.5 18.1 %copy-start.1 = (bf16[4096,128]{1,0:T(8,128)(2,1)S(1)}, bf16[4096,128]{1,0:T(8,128)(2,1)}, u32[]{:S(2)}) copy-start(bf16[4096,128]{1,0:T(8,128)(2,1)} %feat_ref.1) | copy-start | bytes 3145732
  35.6 13.2 %collective-permute-start.20 = (bf16[256,256]{1,0:T(8,128)(2,1)S(1)}, bf16[256,256]{1,0:T(8,128)(2,1)S(1)}, u32[]{:S(2)}, u32[]{:S(2)}) collective-permute-start(bf16[256,256]{1,0:T(8,128)(2,1)S(1)} %get-tuple-element.36), channel_id=1, source_target_pairs={{0,6},{1,7},{2,4},{3,5},{4,2},{5,3},{6,0},{7,1},{8,14},{9,15},{10,... | collective-permute-start | bytes 393224 | tf_op jit(solution)/shard_map/ppermute | solution.py:296
  38.2 10.6 %collective-permute-start.22 = (bf16[256,256]{1,0:T(8,128)(2,1)S(1)}, bf16[256,256]{1,0:T(8,128)(2,1)S(1)}, u32[]{:S(2)}, u32[]{:S(2)}) collective-permute-start(bf16[256,256]{1,0:T(8,128)(2,1)S(1)} %get-tuple-element.37), channel_id=1, source_target_pairs={{0,5},{1,4},{2,7},{3,6},{4,1},{5,0},{6,3},{7,2},{8,13},{9,12},{10,... | collective-permute-start | bytes 393224 | tf_op jit(solution)/shard_map/ppermute | solution.py:296
  38.2 10.6 %collective-permute-start.21 = (bf16[256,256]{1,0:T(8,128)(2,1)S(1)}, bf16[256,256]{1,0:T(8,128)(2,1)S(1)}, u32[]{:S(2)}, u32[]{:S(2)}) collective-permute-start(bf16[256,256]{1,0:T(8,128)(2,1)S(1)} %get-tuple-element.38), channel_id=1, source_target_pairs={{0,3},{1,2},{2,1},{3,0},{4,7},{5,6},{6,5},{7,4},{8,11},{9,10},{10,... | collective-permute-start | bytes 393224 | tf_op jit(solution)/shard_map/ppermute | solution.py:296
  39.8 7.2 %collective-permute-start.16 = (bf16[1,64,128]{2,1,0:T(8,128)(2,1)S(1)}, bf16[1,64,128]{2,1,0:T(8,128)(2,1)S(1)}, u32[]{:S(2)}, u32[]{:S(2)}) collective-permute-start(bf16[1,64,128]{2,1,0:T(8,128)(2,1)S(1)} %fusion.11), channel_id=1, source_target_pairs={{0,3},{1,2},{2,1},{3,0},{4,7},{5,6},{6,5},{7,4},{8,11},{9,10},{10,... | collective-permute-start | bytes 49160 | tf_op jit(solution)/shard_map/ppermute | solution.py:296
  47.0 5.3 %collective-permute-start.17 = (bf16[2,64,128]{2,1,0:T(8,128)(2,1)S(1)}, bf16[2,64,128]{2,1,0:T(8,128)(2,1)S(1)}, u32[]{:S(2)}, u32[]{:S(2)}) collective-permute-start(bf16[2,64,128]{2,1,0:T(8,128)(2,1)S(1)} %pad_maximum_fusion.4), channel_id=1, source_target_pairs={{0,5},{1,4},{2,7},{3,6},{4,1},{5,0},{6,3},{7,2},{8,13},{9,12},{10,... | collective-permute-start | bytes 98312 | tf_op jit(solution)/shard_map/ppermute | solution.py:296
  48.8 4.8 %copy-start.5 = (s32[4096]{0:T(1024)S(1)}, s32[4096]{0:T(1024)}, u32[]{:S(2)}) copy-start(s32[4096]{0:T(1024)} %param.14) | copy-start | bytes 49156
  48.8 4.7 %copy-start.6 = (s32[32]{0:T(128)S(1)}, s32[32]{0:T(128)}, u32[]{:S(2)}) copy-start(s32[32]{0:T(128)} %owners_ref.1) | copy-start | bytes 388
  48.9 7.6 %collective-permute-start.26 = (bf16[256,256]{1,0:T(8,128)(2,1)S(1)}, bf16[256,256]{1,0:T(8,128)(2,1)S(1)}, u32[]{:S(2)}, u32[]{:S(2)}) collective-permute-start(bf16[256,256]{1,0:T(8,128)(2,1)S(1)} %fusion.3), channel_id=1, source_target_pairs={{0,25},{1,24},{2,27},{3,26},{4,29},{5,28},{6,31},{7,30},{8,17},{9,... | collective-permute-start | bytes 393224 | tf_op jit(solution)/shard_map/ppermute | solution.py:296
  50.9 7.5 %collective-permute-start.25 = (bf16[256,256]{1,0:T(8,128)(2,1)S(1)}, bf16[256,256]{1,0:T(8,128)(2,1)S(1)}, u32[]{:S(2)}, u32[]{:S(2)}) collective-permute-start(bf16[256,256]{1,0:T(8,128)(2,1)S(1)} %fusion.3), channel_id=1, source_target_pairs={{0,17},{1,16},{2,19},{3,18},{4,21},{5,20},{6,23},{7,22},{8,25},{9,... | collective-permute-start | bytes 393224 | tf_op jit(solution)/shard_map/ppermute | solution.py:296
  51.5 6.9 %collective-permute-start.24 = (bf16[256,256]{1,0:T(8,128)(2,1)S(1)}, bf16[256,256]{1,0:T(8,128)(2,1)S(1)}, u32[]{:S(2)}, u32[]{:S(2)}) collective-permute-start(bf16[256,256]{1,0:T(8,128)(2,1)S(1)} %fusion.3), channel_id=1, source_target_pairs={{0,9},{1,8},{2,11},{3,10},{4,13},{5,12},{6,15},{7,14},{8,1},{9,0},... | collective-permute-start | bytes 393224 | tf_op jit(solution)/shard_map/ppermute | solution.py:296
  52.0 6.4 %collective-permute-start.23 = (bf16[256,256]{1,0:T(8,128)(2,1)S(1)}, bf16[256,256]{1,0:T(8,128)(2,1)S(1)}, u32[]{:S(2)}, u32[]{:S(2)}) collective-permute-start(bf16[256,256]{1,0:T(8,128)(2,1)S(1)} %fusion.3), channel_id=1, source_target_pairs={{0,1},{1,0},{2,3},{3,2},{4,5},{5,4},{6,7},{7,6},{8,9},{9,8},{10,11... | collective-permute-start | bytes 393224 | tf_op jit(solution)/shard_map/ppermute | solution.py:296
  52.3 1.3 %collective-permute-start.18 = (bf16[4,64,128]{2,1,0:T(8,128)(2,1)S(1)}, bf16[4,64,128]{2,1,0:T(8,128)(2,1)S(1)}, u32[]{:S(2)}, u32[]{:S(2)}) collective-permute-start(bf16[4,64,128]{2,1,0:T(8,128)(2,1)S(1)} %pad_maximum_fusion.2.near), channel_id=1, source_target_pairs={{0,1},{1,0},{2,3},{3,2},{4,5},{5,4},{6,7},{7,6},{8,9},{9,8},{10,11... | collective-permute-start | bytes 196616 | tf_op jit(solution)/shard_map/ppermute | solution.py:296

commit v8 on v7

--- a/solution.py
+++ b/solution.py
@@ -361,7 +361,7 @@
     particle_out = unpool(particles, clusters, owners, near, far)
 
     grad = joined[0]
-    for k in [pairs - 1, *range(1, pairs - 1)]:
+    for k in [pairs - 1, *range(pairs - 2, 0, -1)]:
         grad = grad + swap(joined[k].astype(BF16), 0, chip(k)).astype(F32)
     grad = grad.astype(BF16)
     if n_group > parts:

time: 59.7 us -> 59.6 us (level)
  starting transfers between devices: 31 us -> 29.6 us
  waiting for transfers between devices: 16.8 us -> 18 us
    ppermute x27, starting transfers between devices: 31 us -> 29.6 us  [swap(): return lax.ppermute(x, ('group', 'shard'), pairs)]
    ppermute x27, waiting for transfers between devices: 16.8 us -> 18 us  [swap(): return lax.ppermute(x, ('group', 'shard'), pairs)]
  transfers between devices with their start and end apart: 27 -> 27, of which waited for: 10 -> 11; matrix products, arithmetic and copies ran while one was open for 1% -> 1% of each run, Pallas kernels for 12% -> 12%
where the time goes in v8:
time: 59.6 us; the launch traced here: 59.4 us
  starting transfers between devices  29.6 us (50%)
  waiting for transfers between devices  18 us (30%)
  Pallas kernels  10.2 us (17%)
  between operations  0.87 us (1%)
    ppermute x27, starting transfers between devices, swap(): return lax.ppermute(x, ('group', 'shard'), pairs)  29.6 us
    ppermute x27, waiting for transfers between devices, swap(): return lax.ppermute(x, ('group', 'shard'), pairs)  18 us
    pallas_call x1, Pallas kernels, pool(): pl.pallas_call(pool_kernel, in_specs=[whole] * 4, out_specs=[VMEM, VMEM],...  3.09 us
    pallas_call x1, Pallas kernels, unpool(): pl.pallas_call(unpool_kernel, grid_spec=pltpu.PrefetchScalarGridSpec(num_...  2.83 us
    pallas_call x1, Pallas kernels, attend(): pl.pallas_call(functools.partial(attend_kernel, parts), in_specs=[VMEM] *...  2.27 us
  transfers between devices with their start and end apart: 27, of which 11 were waited for; matrix products, arithmetic and copies ran while one was open for 1% of the time, Pallas kernels for 12%

profile of v8, /device:TPU:0, one launch (start us, length us, event | category | flops | bytes accessed | tf_op | source)
XLA Modules:
  0.0 59.4 jit_solution(14666786093737435816)
XLA Ops:
  0.6 0.0 copy-start
  0.6 2.4 %collective-permute-start.2 = (bf16[1,64,2048]{2,1,0:T(8,128)(2,1)}, bf16[1,64,2048]{2,1,0:T(8,128)(2,1)S(1)}, u32[]{:S(2)}, u32[]{:S(2)}) collective-permute-start(bf16[1,64,2048]{2,1,0:T(8,128)(2,1)} %bitcast.50), channel_id=1, source_target_pairs={{0,9},{1,8},{2,11},{3,10},{4,13},{5,12},{6,15},{7,14},{8,1},{9,0},... | collective-permute-start | bytes 786440 | tf_op jit(solution)/shard_map/ppermute | solution.py:296
  3.1 2.9 %collective-permute-start.1 = (bf16[1,256,256]{2,1,0:T(8,128)(2,1)S(1)}, bf16[1,256,256]{2,1,0:T(8,128)(2,1)S(1)}, u32[]{:S(2)}, u32[]{:S(2)}) collective-permute-start(bf16[1,256,256]{2,1,0:T(8,128)(2,1)S(1)} %dynamic-slice_bitcast_fusion), channel_id=1, source_target_pairs={{0,5},{1,4},{2,7},{3,6},{4,1},{5,0},{6,3},{7,2},{8,13},{9,12},{10,... | collective-permute-start | bytes 393224 | tf_op jit(solution)/shard_map/ppermute | solution.py:296
  6.0 3.1 %pool.1 = (f32[4,64,384]{2,1,0:T(8,128)}, bf16[4,64,384]{2,1,0:T(8,128)(2,1)}) custom-call(s32[32]{0:T(128)} %owners_ref.1, s32[32,128]{1,0:T(8,128)} %bitcast.53, bf16[4096,128]{1,0:T(8,128)(2,1)} %feat_ref.1, bf16[4096,128]{1,0:T(8,128)(2,1)} %grad_hbm.1), custom_call_target="tpu_custom_call" | custom-call | bytes 3000000 | tf_op jit(solution)/shard_map/pool/pallas_call | solution.py:65
  9.2 0.1 collective-permute-start
  9.2 0.9 %collective-permute-done.2 = bf16[1,64,2048]{2,1,0:T(8,128)(2,1)S(1)} collective-permute-done((bf16[1,64,2048]{2,1,0:T(8,128)(2,1)}, bf16[1,64,2048]{2,1,0:T(8,128)(2,1)S(1)}, u32[]{:S(2)}, u32[]{:S(2)}) %collective-permute-start.2) | collective-permute-done | bytes 262176 | tf_op jit(solution)/shard_map/ppermute | solution.py:296
  10.1 0.1 pad_maximum_fusion
  10.1 2.2 %collective-permute-start.10 = (bf16[2,64,2048]{2,1,0:T(8,128)(2,1)S(1)}, bf16[2,64,2048]{2,1,0:T(8,128)(2,1)S(1)}, u32[]{:S(2)}, u32[]{:S(2)}) collective-permute-start(bf16[2,64,2048]{2,1,0:T(8,128)(2,1)S(1)} %pad_maximum_fusion), channel_id=1, source_target_pairs={{0,17},{1,16},{2,19},{3,18},{4,21},{5,20},{6,23},{7,22},{8,25},{9,... | collective-permute-start | bytes 1572872 | tf_op jit(solution)/shard_map/ppermute | solution.py:296
  12.3 0.1 fusion.13
  12.4 2.6 %collective-permute-start.4 = (bf16[64,384]{1,0:T(8,128)(2,1)S(1)}, bf16[64,384]{1,0:T(8,128)(2,1)S(1)}, u32[]{:S(2)}, u32[]{:S(2)}) collective-permute-start(bf16[64,384]{1,0:T(8,128)(2,1)S(1)} %get-tuple-element.41), channel_id=1, source_target_pairs={{0,5},{1,4},{2,7},{3,6},{4,1},{5,0},{6,3},{7,2},{8,13},{9,12},{10,... | collective-permute-start | bytes 147464 | tf_op jit(solution)/shard_map/ppermute | solution.py:296
  15.1 1.3 %collective-permute-start.6 = (bf16[64,384]{1,0:T(8,128)(2,1)S(1)}, bf16[64,384]{1,0:T(8,128)(2,1)S(1)}, u32[]{:S(2)}, u32[]{:S(2)}) collective-permute-start(bf16[64,384]{1,0:T(8,128)(2,1)S(1)} %get-tuple-element.42), channel_id=1, source_target_pairs={{0,6},{1,7},{2,4},{3,5},{4,2},{5,3},{6,0},{7,1},{8,14},{9,15},{10,... | collective-permute-start | bytes 147464 | tf_op jit(solution)/shard_map/ppermute | solution.py:296
  16.4 0.1 collective-permute-start.5
  16.6 1.7 %collective-permute-start.3 = (bf16[2,256,256]{2,1,0:T(8,128)(2,1)S(1)}, bf16[2,256,256]{2,1,0:T(8,128)(2,1)S(1)}, u32[]{:S(2)}, u32[]{:S(2)}) collective-permute-start(bf16[2,256,256]{2,1,0:T(8,128)(2,1)S(1)} %pad_maximum_fusion.1.refs_8_), channel_id=1, source_target_pairs={{0,3},{1,2},{2,1},{3,0},{4,7},{5,6},{6,5},{7,4},{8,11},{9,10},{10,... | collective-permute-start | bytes 786440 | tf_op jit(solution)/shard_map/ppermute | solution.py:296
  18.3 3.2 %collective-permute-done.6 = bf16[64,384]{1,0:T(8,128)(2,1)S(1)} collective-permute-done((bf16[64,384]{1,0:T(8,128)(2,1)S(1)}, bf16[64,384]{1,0:T(8,128)(2,1)S(1)}, u32[]{:S(2)}, u32[]{:S(2)}) %collective-permute-start.6) | collective-permute-done | bytes 49184 | tf_op jit(solution)/shard_map/ppermute | solution.py:296
  21.4 0.1 collective-permute-done.5
  21.5 0.1 slice_reduce_fusion
  21.7 0.1 fusion.7
  21.8 2.0 %collective-permute-start.9 = (bf16[64,256]{1,0:T(8,128)(2,1)S(1)}, bf16[64,256]{1,0:T(8,128)(2,1)S(1)}, u32[]{:S(2)}, u32[]{:S(2)}) collective-permute-start(bf16[64,256]{1,0:T(8,128)(2,1)S(1)} %pad_maximum_fusion.3.refs_4_.refs_0_), channel_id=1, source_target_pairs={{0,24},{1,25},{2,26},{3,27},{4,28},{5,29},{6,30},{7,31},{8,16},{9,... | collective-permute-start | bytes 98312 | tf_op jit(solution)/shard_map/ppermute | solution.py:296
  23.8 0.5 collective-permute-start.8
  24.3 0.8 %collective-permute-start.7 = (bf16[64,256]{1,0:T(8,128)(2,1)S(1)}, bf16[64,256]{1,0:T(8,128)(2,1)S(1)}, u32[]{:S(2)}, u32[]{:S(2)}) collective-permute-start(bf16[64,256]{1,0:T(8,128)(2,1)S(1)} %pad_maximum_fusion.3.refs_4_.refs_0_), channel_id=1, source_target_pairs={{0,9},{1,8},{2,11},{3,10},{4,13},{5,12},{6,15},{7,14},{8,1},{9,0},... | collective-permute-start | bytes 98312 | tf_op jit(solution)/shard_map/ppermute | solution.py:296
  25.1 1.6 %collective-permute-done.9.refs_7_.refs_3_ = bf16[64,256]{1,0:T(8,128)(2,1)S(1)} collective-permute-done((bf16[64,256]{1,0:T(8,128)(2,1)S(1)}, bf16[64,256]{1,0:T(8,128)(2,1)S(1)}, u32[]{:S(2)}, u32[]{:S(2)}) %collective-permute-start.9) | collective-permute-done | bytes 32800 | tf_op jit(solution)/shard_map/ppermute | solution.py:296
  26.7 0.8 %collective-permute-done.8.refs_6_.refs_2_ = bf16[64,256]{1,0:T(8,128)(2,1)S(1)} collective-permute-done((bf16[64,256]{1,0:T(8,128)(2,1)S(1)}, bf16[64,256]{1,0:T(8,128)(2,1)S(1)}, u32[]{:S(2)}, u32[]{:S(2)}) %collective-permute-start.8) | collective-permute-done | bytes 32800 | tf_op jit(solution)/shard_map/ppermute | solution.py:296
  27.4 0.2 collective-permute-done.7.refs_5_.refs_1_
  27.6 0.7 %collective-permute-start.12 = (bf16[2,256,256]{2,1,0:T(8,128)(2,1)S(1)}, bf16[2,256,256]{2,1,0:T(8,128)(2,1)S(1)}, u32[]{:S(2)}, u32[]{:S(2)}) collective-permute-start(bf16[2,256,256]{2,1,0:T(8,128)(2,1)S(1)} %collective-permute-done.3.refs_6_), channel_id=1, source_target_pairs={{0,1},{1,0},{2,3},{3,2},{4,5},{5,4},{6,7},{7,6},{8,9},{9,8},{10,11... | collective-permute-start | bytes 786440 | tf_op jit(solution)/shard_map/ppermute | solution.py:296
  28.4 0.9 %hidden.1 = (bf16[256,2048]{1,0:T(8,128)(2,1)S(1)}, f32[256,256]{1,0:T(8,128)S(1)}) custom-call(bf16[64,2048]{1,0:T(8,128)(2,1)S(1)} %copy-done.2, bf16[64,2048]{1,0:T(8,128)(2,1)S(1)} %bitcast.52, bf16[64,2048]{1,0:T(8,128)(2,1)S(1)} %get-tuple-element.40.refs_2_, bf16[64,2048]{1,0:T(8,128)(2,1)S(1)} %get-tuple-element.39.refs_3_, ...), custom_call_target="tpu_custom_call" | custom-call | tf_op jit(solution)/shard_map/hidden/pallas_call | solution.py:125
  29.3 0.1 collective-permute-done.12.refs_7_
  29.5 2.3 %attend.1 = (bf16[4,64,128]{2,1,0:T(8,128)(2,1)S(1)}, bf16[4,256,256]{2,1,0:T(8,128)(2,1)S(1)}, bf16[4,256,256]{2,1,0:T(8,128)(2,1)S(1)}) custom-call(bf16[64,256]{1,0:T(8,128)(2,1)S(1)} %pad_maximum_fusion.3.refs_4_.refs_0_, bf16[64,256]{1,0:T(8,128)(2,1)S(1)} %collective-permute-done.7.refs_5_.refs_1_, ...), custom_call_target="tpu_custom_call" | custom-call | bytes 3000000 | tf_op jit(solution)/shard_map/attend/pallas_call | solution.py:208
  31.7 0.4 collective-permute-start.19
  32.2 0.7 %collective-permute-start.13 = (bf16[64,128]{1,0:T(8,128)(2,1)S(1)}, bf16[64,128]{1,0:T(8,128)(2,1)S(1)}, u32[]{:S(2)}, u32[]{:S(2)}) collective-permute-start(bf16[64,128]{1,0:T(8,128)(2,1)S(1)} %get-tuple-element.44), channel_id=1, source_target_pairs={{0,17},{1,16},{2,19},{3,18},{4,21},{5,20},{6,23},{7,22},{8,25},{9,... | collective-permute-start | bytes 49160 | tf_op jit(solution)/shard_map/ppermute | solution.py:296
  32.9 1.1 %collective-permute-start.15 = (bf16[64,128]{1,0:T(8,128)(2,1)S(1)}, bf16[64,128]{1,0:T(8,128)(2,1)S(1)}, u32[]{:S(2)}, u32[]{:S(2)}) collective-permute-start(bf16[64,128]{1,0:T(8,128)(2,1)S(1)} %get-tuple-element.45), channel_id=1, source_target_pairs={{0,9},{1,8},{2,11},{3,10},{4,13},{5,12},{6,15},{7,14},{8,1},{9,0},... | collective-permute-start | bytes 49160 | tf_op jit(solution)/shard_map/ppermute | solution.py:296
  34.0 1.4 %collective-permute-start.14 = (bf16[64,128]{1,0:T(8,128)(2,1)S(1)}, bf16[64,128]{1,0:T(8,128)(2,1)S(1)}, u32[]{:S(2)}, u32[]{:S(2)}) collective-permute-start(bf16[64,128]{1,0:T(8,128)(2,1)S(1)} %get-tuple-element.46), channel_id=1, source_target_pairs={{0,24},{1,25},{2,26},{3,27},{4,28},{5,29},{6,30},{7,31},{8,16},{9,... | collective-permute-start | bytes 49160 | tf_op jit(solution)/shard_map/ppermute | solution.py:296
  35.4 0.1 fusion.12
  35.6 2.6 %collective-permute-start.20 = (bf16[256,256]{1,0:T(8,128)(2,1)S(1)}, bf16[256,256]{1,0:T(8,128)(2,1)S(1)}, u32[]{:S(2)}, u32[]{:S(2)}) collective-permute-start(bf16[256,256]{1,0:T(8,128)(2,1)S(1)} %get-tuple-element.36), channel_id=1, source_target_pairs={{0,6},{1,7},{2,4},{3,5},{4,2},{5,3},{6,0},{7,1},{8,14},{9,15},{10,... | collective-permute-start | bytes 393224 | tf_op jit(solution)/shard_map/ppermute | solution.py:296
  38.2 1.6 %collective-permute-start.21 = (bf16[256,256]{1,0:T(8,128)(2,1)S(1)}, bf16[256,256]{1,0:T(8,128)(2,1)S(1)}, u32[]{:S(2)}, u32[]{:S(2)}) collective-permute-start(bf16[256,256]{1,0:T(8,128)(2,1)S(1)} %get-tuple-element.38), channel_id=1, source_target_pairs={{0,5},{1,4},{2,7},{3,6},{4,1},{5,0},{6,3},{7,2},{8,13},{9,12},{10,... | collective-permute-start | bytes 393224 | tf_op jit(solution)/shard_map/ppermute | solution.py:296
  39.8 0.2 collective-permute-start.16
  40.0 8.1 %collective-permute-done.16 = bf16[1,64,128]{2,1,0:T(8,128)(2,1)S(1)} collective-permute-done((bf16[1,64,128]{2,1,0:T(8,128)(2,1)S(1)}, bf16[1,64,128]{2,1,0:T(8,128)(2,1)S(1)}, u32[]{:S(2)}, u32[]{:S(2)}) %collective-permute-start.16) | collective-permute-done | bytes 16416 | tf_op jit(solution)/shard_map/ppermute | solution.py:296
  48.1 0.6 %collective-permute-start.17 = (bf16[2,64,128]{2,1,0:T(8,128)(2,1)S(1)}, bf16[2,64,128]{2,1,0:T(8,128)(2,1)S(1)}, u32[]{:S(2)}, u32[]{:S(2)}) collective-permute-start(bf16[2,64,128]{2,1,0:T(8,128)(2,1)S(1)} %pad_maximum_fusion.4), channel_id=1, source_target_pairs={{0,5},{1,4},{2,7},{3,6},{4,1},{5,0},{6,3},{7,2},{8,13},{9,12},{10,... | collective-permute-start | bytes 98312 | tf_op jit(solution)/shard_map/ppermute | solution.py:296
  48.7 0.1 fusion.3
  48.8 2.0 %collective-permute-start.26 = (bf16[256,256]{1,0:T(8,128)(2,1)S(1)}, bf16[256,256]{1,0:T(8,128)(2,1)S(1)}, u32[]{:S(2)}, u32[]{:S(2)}) collective-permute-start(bf16[256,256]{1,0:T(8,128)(2,1)S(1)} %fusion.3), channel_id=1, source_target_pairs={{0,25},{1,24},{2,27},{3,26},{4,29},{5,28},{6,31},{7,30},{8,17},{9,... | collective-permute-start | bytes 393224 | tf_op jit(solution)/shard_map/ppermute | solution.py:296
  50.9 0.7 %collective-permute-start.25 = (bf16[256,256]{1,0:T(8,128)(2,1)S(1)}, bf16[256,256]{1,0:T(8,128)(2,1)S(1)}, u32[]{:S(2)}, u32[]{:S(2)}) collective-permute-start(bf16[256,256]{1,0:T(8,128)(2,1)S(1)} %fusion.3), channel_id=1, source_target_pairs={{0,17},{1,16},{2,19},{3,18},{4,21},{5,20},{6,23},{7,22},{8,25},{9,... | collective-permute-start | bytes 393224 | tf_op jit(solution)/shard_map/ppermute | solution.py:296
  51.6 0.4 collective-permute-start.24
  52.0 0.2 collective-permute-start.23
  52.2 0.4 collective-permute-done.17
  52.6 0.2 collective-permute-start.18
  52.8 1.1 %collective-permute-done.18.far = bf16[4,64,128]{2,1,0:T(8,128)(2,1)S(1)} collective-permute-done((bf16[4,64,128]{2,1,0:T(8,128)(2,1)S(1)}, bf16[4,64,128]{2,1,0:T(8,128)(2,1)S(1)}, u32[]{:S(2)}, u32[]{:S(2)}) %collective-permute-start.18) | collective-permute-done | bytes 65568 | tf_op jit(solution)/shard_map/ppermute | solution.py:296
  53.9 2.8 %unpool.1 = bf16[4096,128]{1,0:T(8,128)(2,1)} custom-call(s32[32]{0:T(128)S(1)} %copy-done.6, s32[32,128]{1,0:T(8,128)S(1)} %bitcast.54, bf16[4096,128]{1,0:T(8,128)(2,1)S(1)} %copy-done.1, bf16[4,64,128]{2,1,0:T(8,128)(2,1)S(1)} %pad_maximum_fusion.2.near, bf16[4,64,128]{2,1,0:T(8,128)(2,1)S(1)} %collective-permute-done.18.far), custom_call_target="tpu_custom_call" | custom-call | tf_op jit(solution)/shard_map/unpool/pallas_call | solution.py:252
  56.7 1.6 %collective-permute-done.25.refs_2_ = bf16[256,256]{1,0:T(8,128)(2,1)S(1)} collective-permute-done((bf16[256,256]{1,0:T(8,128)(2,1)S(1)}, bf16[256,256]{1,0:T(8,128)(2,1)S(1)}, u32[]{:S(2)}, u32[]{:S(2)}) %collective-permute-start.25) | collective-permute-done | bytes 131104 | tf_op jit(solution)/shard_map/ppermute | solution.py:296
  58.4 1.1 %spread.1 = f32[256,1024]{1,0:T(8,128)} custom-call(bf16[256,256]{1,0:T(8,128)(2,1)S(1)} %collective-permute-done.23.refs_0_, bf16[256,256]{1,0:T(8,128)(2,1)S(1)} %collective-permute-done.24.refs_1_, bf16[256,256]{1,0:T(8,128)(2,1)S(1)} %collective-permute-done.25.refs_2_, bf16[256,256]{1,0:T(8,128)(2,1)S(1)} %collective-permute-done.26.refs_3_), custom_call_target="tpu_custom_call" | custom-call | tf_op jit(solution)/shard_map/spread/pallas_call | solution.py:282
  (46 shorter events, 0.3 us)
Async XLA Ops:
  0.6 2.5 %copy-start = (bf16[256,1024]{1,0:T(8,128)(2,1)S(1)}, bf16[256,1024]{1,0:T(8,128)(2,1)}, u32[]{:S(2)}) copy-start(bf16[256,1024]{1,0:T(8,128)(2,1)} %param.9) | copy-start | bytes 1572868
  0.6 9.4 %collective-permute-start.2 = (bf16[1,64,2048]{2,1,0:T(8,128)(2,1)}, bf16[1,64,2048]{2,1,0:T(8,128)(2,1)S(1)}, u32[]{:S(2)}, u32[]{:S(2)}) collective-permute-start(bf16[1,64,2048]{2,1,0:T(8,128)(2,1)} %bitcast.50), channel_id=1, source_target_pairs={{0,9},{1,8},{2,11},{3,10},{4,13},{5,12},{6,15},{7,14},{8,1},{9,0},... | collective-permute-start | bytes 786440 | tf_op jit(solution)/shard_map/ppermute | solution.py:296
  3.1 9.2 %collective-permute-start.1 = (bf16[1,256,256]{2,1,0:T(8,128)(2,1)S(1)}, bf16[1,256,256]{2,1,0:T(8,128)(2,1)S(1)}, u32[]{:S(2)}, u32[]{:S(2)}) collective-permute-start(bf16[1,256,256]{2,1,0:T(8,128)(2,1)S(1)} %dynamic-slice_bitcast_fusion), channel_id=1, source_target_pairs={{0,5},{1,4},{2,7},{3,6},{4,1},{5,0},{6,3},{7,2},{8,13},{9,12},{10,... | collective-permute-start | bytes 393224 | tf_op jit(solution)/shard_map/ppermute | solution.py:296
  6.0 4.0 %copy-start.2 = (bf16[64,2048]{1,0:T(8,128)(2,1)S(1)}, bf16[64,2048]{1,0:T(8,128)(2,1)}, u32[]{:S(2)}) copy-start(bf16[64,2048]{1,0:T(8,128)(2,1)} %refs_0_.1) | copy-start | bytes 786436
  9.1 3.2 %copy-start.7 = (f32[4,64,384]{2,1,0:T(8,128)S(1)}, f32[4,64,384]{2,1,0:T(8,128)}, u32[]{:S(2)}) copy-start(f32[4,64,384]{2,1,0:T(8,128)} %get-tuple-element.19) | copy-start | bytes 1179652
  9.2 3.2 %collective-permute-start = (bf16[4,64,384]{2,1,0:T(8,128)(2,1)}, bf16[4,64,384]{2,1,0:T(8,128)(2,1)S(1)}, u32[]{:S(2)}, u32[]{:S(2)}) collective-permute-start(bf16[4,64,384]{2,1,0:T(8,128)(2,1)} %get-tuple-element.17), channel_id=1, source_target_pairs={{0,1},{1,0},{2,3},{3,2},{4,5},{5,4},{6,7},{7,6},{8,9},{9,8},{10,11... | collective-permute-start | bytes 589832 | tf_op jit(solution)/shard_map/ppermute | solution.py:296
  10.1 18.2 %collective-permute-start.10 = (bf16[2,64,2048]{2,1,0:T(8,128)(2,1)S(1)}, bf16[2,64,2048]{2,1,0:T(8,128)(2,1)S(1)}, u32[]{:S(2)}, u32[]{:S(2)}) collective-permute-start(bf16[2,64,2048]{2,1,0:T(8,128)(2,1)S(1)} %pad_maximum_fusion), channel_id=1, source_target_pairs={{0,17},{1,16},{2,19},{3,18},{4,21},{5,20},{6,23},{7,22},{8,25},{9,... | collective-permute-start | bytes 1572872 | tf_op jit(solution)/shard_map/ppermute | solution.py:296
  12.4 5.8 %collective-permute-start.4 = (bf16[64,384]{1,0:T(8,128)(2,1)S(1)}, bf16[64,384]{1,0:T(8,128)(2,1)S(1)}, u32[]{:S(2)}, u32[]{:S(2)}) collective-permute-start(bf16[64,384]{1,0:T(8,128)(2,1)S(1)} %get-tuple-element.41), channel_id=1, source_target_pairs={{0,5},{1,4},{2,7},{3,6},{4,1},{5,0},{6,3},{7,2},{8,13},{9,12},{10,... | collective-permute-start | bytes 147464 | tf_op jit(solution)/shard_map/ppermute | solution.py:296
  15.1 6.3 %collective-permute-start.6 = (bf16[64,384]{1,0:T(8,128)(2,1)S(1)}, bf16[64,384]{1,0:T(8,128)(2,1)S(1)}, u32[]{:S(2)}, u32[]{:S(2)}) collective-permute-start(bf16[64,384]{1,0:T(8,128)(2,1)S(1)} %get-tuple-element.42), channel_id=1, source_target_pairs={{0,6},{1,7},{2,4},{3,5},{4,2},{5,3},{6,0},{7,1},{8,14},{9,15},{10,... | collective-permute-start | bytes 147464 | tf_op jit(solution)/shard_map/ppermute | solution.py:296
  16.4 5.1 %collective-permute-start.5 = (bf16[64,384]{1,0:T(8,128)(2,1)S(1)}, bf16[64,384]{1,0:T(8,128)(2,1)S(1)}, u32[]{:S(2)}, u32[]{:S(2)}) collective-permute-start(bf16[64,384]{1,0:T(8,128)(2,1)S(1)} %get-tuple-element.43), channel_id=1, source_target_pairs={{0,3},{1,2},{2,1},{3,0},{4,7},{5,6},{6,5},{7,4},{8,11},{9,10},{10,... | collective-permute-start | bytes 147464 | tf_op jit(solution)/shard_map/ppermute | solution.py:296
  16.6 11.0 %collective-permute-start.3 = (bf16[2,256,256]{2,1,0:T(8,128)(2,1)S(1)}, bf16[2,256,256]{2,1,0:T(8,128)(2,1)S(1)}, u32[]{:S(2)}, u32[]{:S(2)}) collective-permute-start(bf16[2,256,256]{2,1,0:T(8,128)(2,1)S(1)} %pad_maximum_fusion.1.refs_8_), channel_id=1, source_target_pairs={{0,3},{1,2},{2,1},{3,0},{4,7},{5,6},{6,5},{7,4},{8,11},{9,10},{10,... | collective-permute-start | bytes 786440 | tf_op jit(solution)/shard_map/ppermute | solution.py:296
  21.8 6.6 %copy-start.3 = (bf16[128,2048]{1,0:T(8,128)(2,1)S(1)}, bf16[128,2048]{1,0:T(8,128)(2,1)}, u32[]{:S(2)}) copy-start(bf16[128,2048]{1,0:T(8,128)(2,1)} %refs_10_.1) | copy-start | bytes 1572868
  21.8 4.9 %collective-permute-start.9 = (bf16[64,256]{1,0:T(8,128)(2,1)S(1)}, bf16[64,256]{1,0:T(8,128)(2,1)S(1)}, u32[]{:S(2)}, u32[]{:S(2)}) collective-permute-start(bf16[64,256]{1,0:T(8,128)(2,1)S(1)} %pad_maximum_fusion.3.refs_4_.refs_0_), channel_id=1, source_target_pairs={{0,24},{1,25},{2,26},{3,27},{4,28},{5,29},{6,30},{7,31},{8,16},{9,... | collective-permute-start | bytes 98312 | tf_op jit(solution)/shard_map/ppermute | solution.py:296
  23.8 3.7 %collective-permute-start.8 = (bf16[64,256]{1,0:T(8,128)(2,1)S(1)}, bf16[64,256]{1,0:T(8,128)(2,1)S(1)}, u32[]{:S(2)}, u32[]{:S(2)}) collective-permute-start(bf16[64,256]{1,0:T(8,128)(2,1)S(1)} %pad_maximum_fusion.3.refs_4_.refs_0_), channel_id=1, source_target_pairs={{0,17},{1,16},{2,19},{3,18},{4,21},{5,20},{6,23},{7,22},{8,25},{9,... | collective-permute-start | bytes 98312 | tf_op jit(solution)/shard_map/ppermute | solution.py:296
  24.3 3.3 %collective-permute-start.7 = (bf16[64,256]{1,0:T(8,128)(2,1)S(1)}, bf16[64,256]{1,0:T(8,128)(2,1)S(1)}, u32[]{:S(2)}, u32[]{:S(2)}) collective-permute-start(bf16[64,256]{1,0:T(8,128)(2,1)S(1)} %pad_maximum_fusion.3.refs_4_.refs_0_), channel_id=1, source_target_pairs={{0,9},{1,8},{2,11},{3,10},{4,13},{5,12},{6,15},{7,14},{8,1},{9,0},... | collective-permute-start | bytes 98312 | tf_op jit(solution)/shard_map/ppermute | solution.py:296
  26.7 1.7 %collective-permute-start.11 = (bf16[2,256,256]{2,1,0:T(8,128)(2,1)S(1)}, bf16[2,256,256]{2,1,0:T(8,128)(2,1)S(1)}, u32[]{:S(2)}, u32[]{:S(2)}) collective-permute-start(bf16[2,256,256]{2,1,0:T(8,128)(2,1)S(1)} %pad_maximum_fusion.1.refs_8_), channel_id=1, source_target_pairs={{0,1},{1,0},{2,3},{3,2},{4,5},{5,4},{6,7},{7,6},{8,9},{9,8},{10,11... | collective-permute-start | bytes 786440 | tf_op jit(solution)/shard_map/ppermute | solution.py:296
  27.6 1.8 %collective-permute-start.12 = (bf16[2,256,256]{2,1,0:T(8,128)(2,1)S(1)}, bf16[2,256,256]{2,1,0:T(8,128)(2,1)S(1)}, u32[]{:S(2)}, u32[]{:S(2)}) collective-permute-start(bf16[2,256,256]{2,1,0:T(8,128)(2,1)S(1)} %collective-permute-done.3.refs_6_), channel_id=1, source_target_pairs={{0,1},{1,0},{2,3},{3,2},{4,5},{5,4},{6,7},{7,6},{8,9},{9,8},{10,11... | collective-permute-start | bytes 786440 | tf_op jit(solution)/shard_map/ppermute | solution.py:296
  28.4 1.1 %copy-start.4 = (bf16[2048,128]{1,0:T(8,128)(2,1)S(1)}, bf16[2048,128]{1,0:T(8,128)(2,1)}, u32[]{:S(2)}) copy-start(bf16[2048,128]{1,0:T(8,128)(2,1)} %refs_8_.1) | copy-start | bytes 1572868
  31.7 3.6 %collective-permute-start.19 = (bf16[4,256,256]{2,1,0:T(8,128)(2,1)S(1)}, bf16[4,256,256]{2,1,0:T(8,128)(2,1)S(1)}, u32[]{:S(2)}, u32[]{:S(2)}) collective-permute-start(bf16[4,256,256]{2,1,0:T(8,128)(2,1)S(1)} %get-tuple-element.31), channel_id=1, source_target_pairs={{0,1},{1,0},{2,3},{3,2},{4,5},{5,4},{6,7},{7,6},{8,9},{9,8},{10,11... | collective-permute-start | bytes 1572872 | tf_op jit(solution)/shard_map/ppermute | solution.py:296
  32.2 6.0 %collective-permute-start.13 = (bf16[64,128]{1,0:T(8,128)(2,1)S(1)}, bf16[64,128]{1,0:T(8,128)(2,1)S(1)}, u32[]{:S(2)}, u32[]{:S(2)}) collective-permute-start(bf16[64,128]{1,0:T(8,128)(2,1)S(1)} %get-tuple-element.44), channel_id=1, source_target_pairs={{0,17},{1,16},{2,19},{3,18},{4,21},{5,20},{6,23},{7,22},{8,25},{9,... | collective-permute-start | bytes 49160 | tf_op jit(solution)/shard_map/ppermute | solution.py:296
  32.9 6.8 %collective-permute-start.15 = (bf16[64,128]{1,0:T(8,128)(2,1)S(1)}, bf16[64,128]{1,0:T(8,128)(2,1)S(1)}, u32[]{:S(2)}, u32[]{:S(2)}) collective-permute-start(bf16[64,128]{1,0:T(8,128)(2,1)S(1)} %get-tuple-element.45), channel_id=1, source_target_pairs={{0,9},{1,8},{2,11},{3,10},{4,13},{5,12},{6,15},{7,14},{8,1},{9,0},... | collective-permute-start | bytes 49160 | tf_op jit(solution)/shard_map/ppermute | solution.py:296
  34.0 5.8 %collective-permute-start.14 = (bf16[64,128]{1,0:T(8,128)(2,1)S(1)}, bf16[64,128]{1,0:T(8,128)(2,1)S(1)}, u32[]{:S(2)}, u32[]{:S(2)}) collective-permute-start(bf16[64,128]{1,0:T(8,128)(2,1)S(1)} %get-tuple-element.46), channel_id=1, source_target_pairs={{0,24},{1,25},{2,26},{3,27},{4,28},{5,29},{6,30},{7,31},{8,16},{9,... | collective-permute-start | bytes 49160 | tf_op jit(solution)/shard_map/ppermute | solution.py:296
  35.5 18.4 %copy-start.1 = (bf16[4096,128]{1,0:T(8,128)(2,1)S(1)}, bf16[4096,128]{1,0:T(8,128)(2,1)}, u32[]{:S(2)}) copy-start(bf16[4096,128]{1,0:T(8,128)(2,1)} %feat_ref.1) | copy-start | bytes 3145732
  35.6 13.2 %collective-permute-start.20 = (bf16[256,256]{1,0:T(8,128)(2,1)S(1)}, bf16[256,256]{1,0:T(8,128)(2,1)S(1)}, u32[]{:S(2)}, u32[]{:S(2)}) collective-permute-start(bf16[256,256]{1,0:T(8,128)(2,1)S(1)} %get-tuple-element.36), channel_id=1, source_target_pairs={{0,6},{1,7},{2,4},{3,5},{4,2},{5,3},{6,0},{7,1},{8,14},{9,15},{10,... | collective-permute-start | bytes 393224 | tf_op jit(solution)/shard_map/ppermute | solution.py:296
  38.2 10.6 %collective-permute-start.22 = (bf16[256,256]{1,0:T(8,128)(2,1)S(1)}, bf16[256,256]{1,0:T(8,128)(2,1)S(1)}, u32[]{:S(2)}, u32[]{:S(2)}) collective-permute-start(bf16[256,256]{1,0:T(8,128)(2,1)S(1)} %get-tuple-element.37), channel_id=1, source_target_pairs={{0,3},{1,2},{2,1},{3,0},{4,7},{5,6},{6,5},{7,4},{8,11},{9,10},{10,... | collective-permute-start | bytes 393224 | tf_op jit(solution)/shard_map/ppermute | solution.py:296
  38.2 10.6 %collective-permute-start.21 = (bf16[256,256]{1,0:T(8,128)(2,1)S(1)}, bf16[256,256]{1,0:T(8,128)(2,1)S(1)}, u32[]{:S(2)}, u32[]{:S(2)}) collective-permute-start(bf16[256,256]{1,0:T(8,128)(2,1)S(1)} %get-tuple-element.38), channel_id=1, source_target_pairs={{0,5},{1,4},{2,7},{3,6},{4,1},{5,0},{6,3},{7,2},{8,13},{9,12},{10,... | collective-permute-start | bytes 393224 | tf_op jit(solution)/shard_map/ppermute | solution.py:296
  39.8 8.3 %collective-permute-start.16 = (bf16[1,64,128]{2,1,0:T(8,128)(2,1)S(1)}, bf16[1,64,128]{2,1,0:T(8,128)(2,1)S(1)}, u32[]{:S(2)}, u32[]{:S(2)}) collective-permute-start(bf16[1,64,128]{2,1,0:T(8,128)(2,1)S(1)} %fusion.11), channel_id=1, source_target_pairs={{0,3},{1,2},{2,1},{3,0},{4,7},{5,6},{6,5},{7,4},{8,11},{9,10},{10,... | collective-permute-start | bytes 49160 | tf_op jit(solution)/shard_map/ppermute | solution.py:296
  48.1 4.5 %collective-permute-start.17 = (bf16[2,64,128]{2,1,0:T(8,128)(2,1)S(1)}, bf16[2,64,128]{2,1,0:T(8,128)(2,1)S(1)}, u32[]{:S(2)}, u32[]{:S(2)}) collective-permute-start(bf16[2,64,128]{2,1,0:T(8,128)(2,1)S(1)} %pad_maximum_fusion.4), channel_id=1, source_target_pairs={{0,5},{1,4},{2,7},{3,6},{4,1},{5,0},{6,3},{7,2},{8,13},{9,12},{10,... | collective-permute-start | bytes 98312 | tf_op jit(solution)/shard_map/ppermute | solution.py:296
  48.8 5.1 %copy-start.5 = (s32[4096]{0:T(1024)S(1)}, s32[4096]{0:T(1024)}, u32[]{:S(2)}) copy-start(s32[4096]{0:T(1024)} %param.14) | copy-start | bytes 49156
  48.8 5.1 %copy-start.6 = (s32[32]{0:T(128)S(1)}, s32[32]{0:T(128)}, u32[]{:S(2)}) copy-start(s32[32]{0:T(128)} %owners_ref.1) | copy-start | bytes 388
  48.8 7.9 %collective-permute-start.26 = (bf16[256,256]{1,0:T(8,128)(2,1)S(1)}, bf16[256,256]{1,0:T(8,128)(2,1)S(1)}, u32[]{:S(2)}, u32[]{:S(2)}) collective-permute-start(bf16[256,256]{1,0:T(8,128)(2,1)S(1)} %fusion.3), channel_id=1, source_target_pairs={{0,25},{1,24},{2,27},{3,26},{4,29},{5,28},{6,31},{7,30},{8,17},{9,... | collective-permute-start | bytes 393224 | tf_op jit(solution)/shard_map/ppermute | solution.py:296
  50.9 7.5 %collective-permute-start.25 = (bf16[256,256]{1,0:T(8,128)(2,1)S(1)}, bf16[256,256]{1,0:T(8,128)(2,1)S(1)}, u32[]{:S(2)}, u32[]{:S(2)}) collective-permute-start(bf16[256,256]{1,0:T(8,128)(2,1)S(1)} %fusion.3), channel_id=1, source_target_pairs={{0,17},{1,16},{2,19},{3,18},{4,21},{5,20},{6,23},{7,22},{8,25},{9,... | collective-permute-start | bytes 393224 | tf_op jit(solution)/shard_map/ppermute | solution.py:296
  51.6 6.7 %collective-permute-start.24 = (bf16[256,256]{1,0:T(8,128)(2,1)S(1)}, bf16[256,256]{1,0:T(8,128)(2,1)S(1)}, u32[]{:S(2)}, u32[]{:S(2)}) collective-permute-start(bf16[256,256]{1,0:T(8,128)(2,1)S(1)} %fusion.3), channel_id=1, source_target_pairs={{0,9},{1,8},{2,11},{3,10},{4,13},{5,12},{6,15},{7,14},{8,1},{9,0},... | collective-permute-start | bytes 393224 | tf_op jit(solution)/shard_map/ppermute | solution.py:296
  52.0 6.3 %collective-permute-start.23 = (bf16[256,256]{1,0:T(8,128)(2,1)S(1)}, bf16[256,256]{1,0:T(8,128)(2,1)S(1)}, u32[]{:S(2)}, u32[]{:S(2)}) collective-permute-start(bf16[256,256]{1,0:T(8,128)(2,1)S(1)} %fusion.3), channel_id=1, source_target_pairs={{0,1},{1,0},{2,3},{3,2},{4,5},{5,4},{6,7},{7,6},{8,9},{9,8},{10,11... | collective-permute-start | bytes 393224 | tf_op jit(solution)/shard_map/ppermute | solution.py:296
  52.6 1.3 %collective-permute-start.18 = (bf16[4,64,128]{2,1,0:T(8,128)(2,1)S(1)}, bf16[4,64,128]{2,1,0:T(8,128)(2,1)S(1)}, u32[]{:S(2)}, u32[]{:S(2)}) collective-permute-start(bf16[4,64,128]{2,1,0:T(8,128)(2,1)S(1)} %pad_maximum_fusion.2.near), channel_id=1, source_target_pairs={{0,1},{1,0},{2,3},{3,2},{4,5},{5,4},{6,7},{7,6},{8,9},{9,8},{10,11... | collective-permute-start | bytes 196616 | tf_op jit(solution)/shard_map/ppermute | solution.py:296
